TPU v7x, 32 devices: a whole 2x2x4 slice. The times are simulated.
32 devices in a mesh: section: 2 (over core), group: 2 (over x), replica: 8 (over z, y).
Axes of the slice: x: 2, y: 2, z: 4, core: 2. Of those that a mesh axis runs over, the one named last changes fastest.
Arguments:
- first_layer_input: bfloat16 [2, 8, 512, 1024], P(None, 'replica', 'group'), may hold values from -6 to 6
- boundary: int32 [2, 8], P(None, 'replica'), may hold values from 0 to 512, as said below
- input_gain: bfloat16 [2, 1024], P('section', 'group'), may hold values from 0.25 to 1.75
- in_proj: bfloat16 [2, 1024, 4384], P('section', 'group'), may hold values from -0.1875 to 0.1875
- conv_weight: bfloat16 [2, 2304, 4], P('section', 'group'), may hold values from -3 to 3
- conv_bias: bfloat16 [2, 2304], P('section', 'group'), may hold values from -3 to 3
- head_params: bfloat16 [2, 32, 3], P('section', 'group'), may hold values from -7 to 1.5, as said below
- output_gain: bfloat16 [2, 2048], P('section', 'group'), may hold values from 0.25 to 1.75
- out_proj: bfloat16 [2, 2048, 1024], P('section', 'group'), may hold values from -0.125 to 0.125
- cotangent: bfloat16 [2, 8, 512, 1024], P(None, 'replica', 'group'), may hold values from -6 to 6
Outputs:
- segment_output: bfloat16 [2, 2, 8, 512, 1024], P('section', None, 'replica', 'group')
- input_grad: bfloat16 [2, 2, 8, 512, 1024], P('section', None, 'replica', 'group')
- grad_input_gain: float32 [2, 1024], P('section', 'group')
- grad_in_proj: float32 [2, 1024, 4384], P('section', 'group')
- grad_conv_weight: float32 [2, 2304, 4], P('section', 'group')
- grad_conv_bias: float32 [2, 2304], P('section', 'group')
- grad_head_params: float32 [2, 32, 3], P('section', 'group')
- grad_output_gain: float32 [2, 2048], P('section', 'group')
- grad_out_proj: float32 [2, 2048, 1024], P('section', 'group')
Inputs may be any that keep to these rules, and one draw needn't show every extreme that they name: `boundary`: one of the row's two sequences is longer than 256 tokens; 0 and 512 mean a single sequence; some row of each micro-batch holds a single sequence. `head_params`: column 0 is a bias added before softplus, column 1 the logarithm of a decay rate, column 2 a skip gain.
All inputs are finite; a program needn't handle non-finite values.
Results may differ from a plain program's by a relative error of at most 0.015.
The roundings to bfloat16 on the way count: a program that leaves them out, or rounds other values in their place, can miss the bound.
Values may be sent and summed in bfloat16 or wider, within the bound.
No kernel may reach another device: no remote copies, remote signals or barrier semaphores. Data moves between devices by JAX's collectives and lax.ppermute only.
A program may use at most 256 MiB of HBM per device.

v0:
```python
import jax
import jax.numpy as jnp
from jax import lax
from jax.sharding import PartitionSpec as P

MODEL_WIDTH = 1024
HEADS = 32
HDIM = 64
NS = 128
KW = 4
SPAN = 256
DI = 2048
CONVC = 2304


def shifted(block, axis, distance):
    devices = range(lax.axis_size(axis))
    route = [(i - distance, i) for i in devices if i - distance in devices]
    return lax.ppermute(block, axis, route)


def rms_scale(values, gain):
    return values * lax.rsqrt(jnp.mean(values * values, axis=-1, keepdims=True) + 1e-05) * gain


def contract_rows(left, right):
    return lax.dot_general(
        left, right, (((0,), (0,)), ((), ())), preferred_element_type=jnp.float32
    )


def contract_cols(left, right):
    return lax.dot_general(
        left, right, (((1,), (1,)), ((), ())), preferred_element_type=jnp.float32
    )


def store_slot(store, value, slot_index, is_valid):
    previous = lax.dynamic_index_in_dim(store, slot_index, 0, keepdims=False)
    return lax.dynamic_update_index_in_dim(
        store, jnp.where(is_valid, value, previous), slot_index, 0
    )


def read_slot(store, slot_index):
    return lax.dynamic_index_in_dim(store, slot_index, 0, keepdims=False)


def conv_silu(raw_mix, edge_rows, conv_weight, conv_bias, positions, boundary_pos):
    width = conv_weight.shape[1]
    padded = jnp.concatenate([edge_rows, raw_mix], axis=0)
    length = raw_mix.shape[0]
    total = jnp.zeros_like(raw_mix) + conv_bias[None, :]
    for offset in range(width):
        lag = width - 1 - offset
        source = padded[offset : offset + length]
        anchor = positions - lag
        dropped = (anchor < 0) | (anchor < boundary_pos) & (boundary_pos <= positions)
        total = total + jnp.where(dropped[:, None], 0.0, source * conv_weight[None, :, offset])
    return jax.nn.silu(total)


def ssd_blocks(values_x, read_b, read_c, step_size, rate, positions, boundary_pos):
    count = values_x.shape[0] // SPAN
    highest = lax.Precision.HIGHEST

    def block_step(state, block_item):
        block_x, block_b, block_c, block_dt, block_rate, block_pos = block_item
        decay_sum = jnp.cumsum(block_rate, axis=0)
        ordered = block_pos[:, None] >= block_pos[None, :]
        crossed = (block_pos[None, :] < boundary_pos) & (boundary_pos <= block_pos[:, None])
        inside = ordered & jnp.logical_not(crossed)
        spread = decay_sum.T[:, :, None] - decay_sum.T[:, None, :]
        decay_mat = jnp.exp(jnp.where(inside[None], spread, -jnp.inf))
        intersection = jnp.dot(block_c, block_b.T, precision=highest)
        mixing = decay_mat * intersection[None] * block_dt.T[:, None, :]
        direct = jnp.einsum("hij,jhp->ihp", mixing, block_x, precision=highest)
        fresh_start = (block_pos[0] <= boundary_pos) & (boundary_pos <= block_pos)
        carried = jnp.einsum("in,hpn->ihp", block_c, state, precision=highest)
        carry_scale = jnp.where(fresh_start[:, None], 0.0, jnp.exp(decay_sum))
        tail_cut = (block_pos < boundary_pos) & (boundary_pos <= block_pos[-1])
        tail_scale = (
            jnp.where(tail_cut[:, None], 0.0, jnp.exp(decay_sum[-1][None, :] - decay_sum))
            * block_dt
        )
        fresh = jnp.einsum("jh,jhp,jn->hpn", tail_scale, block_x, block_b, precision=highest)
        whole_cut = (block_pos[0] <= boundary_pos) & (boundary_pos <= block_pos[-1])
        kept_scale = jnp.where(whole_cut, 0.0, jnp.exp(decay_sum[-1]))
        new_state = state * kept_scale[:, None, None] + fresh
        return (new_state, direct + carried * carry_scale[:, :, None])

    items = (
        values_x.reshape(count, SPAN, HEADS, HDIM),
        read_b.reshape(count, SPAN, NS),
        read_c.reshape(count, SPAN, NS),
        step_size.reshape(count, SPAN, HEADS),
        rate.reshape(count, SPAN, HEADS),
        positions.reshape(count, SPAN),
    )
    start = jnp.zeros((HEADS, HDIM, NS), jnp.float32)
    final_state, outputs = lax.scan(jax.checkpoint(block_step), start, items)
    return (final_state, outputs.reshape(values_x.shape))


def mix_front(
    raw_mix, edge_rows, step_raw, conv_weight, conv_bias, head_params, positions, boundary_pos
):
    length = raw_mix.shape[0]
    convolved = conv_silu(raw_mix, edge_rows, conv_weight, conv_bias, positions, boundary_pos)
    values_x = convolved[:, :DI].reshape(length, HEADS, HDIM)
    read_b = convolved[:, DI : DI + NS]
    read_c = convolved[:, DI + NS :]
    step_size = jax.nn.softplus(step_raw + head_params[:, 0])
    rate = -step_size * jnp.exp(head_params[:, 1])
    local_state, y_zero = ssd_blocks(
        values_x, read_b, read_c, step_size, rate, positions, boundary_pos
    )
    crossing = (positions[0] <= boundary_pos) & (boundary_pos <= positions)
    reach = jnp.where(crossing[:, None], 0.0, jnp.exp(jnp.cumsum(rate, axis=0)))
    whole_cut = (positions[0] <= boundary_pos) & (boundary_pos <= positions[-1])
    decay = jnp.where(whole_cut, 0.0, jnp.exp(jnp.sum(rate, axis=0)))
    return (values_x, read_c, y_zero, local_state, decay, reach)


def finish(y_zero, reach, values_x, read_c, gate_cols, incoming, head_params, output_gain):
    carried = jnp.einsum("in,hpn->ihp", read_c, incoming, precision=lax.Precision.HIGHEST)
    mixed_heads = y_zero + reach[:, :, None] * carried + head_params[:, 2][None, :, None] * values_x
    mixed = mixed_heads.reshape(gate_cols.shape) * jax.nn.silu(gate_cols)
    return rms_scale(mixed, output_gain)


def pass_states(local_state):
    incoming = shifted(local_state, "group", 1)
    return incoming


def pass_adjoints(grad_incoming):
    adjoint = shifted(grad_incoming, "group", -1)
    return adjoint


def front_pieces(layer_in, weights):
    input_gain, in_proj = (weights[0], weights[1])
    values = layer_in.astype(jnp.float32)
    normed = rms_scale(values, input_gain.astype(jnp.float32)).astype(jnp.bfloat16)
    projected = jnp.dot(normed, in_proj, preferred_element_type=jnp.float32)
    return (
        values,
        normed,
        projected[:, :DI],
        projected[:, DI : DI + CONVC],
        projected[:, DI + CONVC :],
    )


def layer_forward(layer_in, boundary_pos, weights, positions):
    conv_weight, conv_bias, head_params, output_gain, out_proj = weights[2:]
    values, normed, gate_cols, raw_mix, step_raw = front_pieces(layer_in, weights)
    length = raw_mix.shape[0]
    edge_rows = shifted(raw_mix[length - KW + 1 :], "group", 1)
    heads_float = head_params.astype(jnp.float32)
    values_x, read_c, y_zero, local_state, decay, reach = mix_front(
        raw_mix,
        edge_rows,
        step_raw,
        conv_weight.astype(jnp.float32),
        conv_bias.astype(jnp.float32),
        heads_float,
        positions,
        boundary_pos,
    )
    incoming = pass_states(local_state)
    gated = finish(
        y_zero,
        reach,
        values_x,
        read_c,
        gate_cols,
        incoming,
        heads_float,
        output_gain.astype(jnp.float32),
    )
    result = values + jnp.dot(
        gated.astype(jnp.bfloat16), out_proj, preferred_element_type=jnp.float32
    )
    return (result, edge_rows, incoming)


def projection_grads(normed, grad_projected, gated_low, upstream):
    return (contract_rows(normed, grad_projected), contract_rows(gated_low, upstream))


def layer_backward(layer_in, boundary_pos, edge_rows, incoming, weights, upstream, positions):
    input_gain, in_proj, conv_weight, conv_bias, head_params, output_gain, out_proj = weights
    values, normed, gate_cols, raw_mix, step_raw = front_pieces(layer_in, weights)
    length = raw_mix.shape[0]
    gain_float = input_gain.astype(jnp.float32)

    def front_local(raw_part, edge_part, step_part, conv_part, bias_part, heads_part):
        return mix_front(
            raw_part,
            edge_part,
            step_part,
            conv_part,
            bias_part,
            heads_part,
            positions,
            boundary_pos,
        )

    front, front_pull = jax.vjp(
        front_local,
        raw_mix,
        edge_rows,
        step_raw,
        conv_weight.astype(jnp.float32),
        conv_bias.astype(jnp.float32),
        head_params.astype(jnp.float32),
    )
    values_x, read_c, y_zero, local_state, decay, reach = front
    gated, finish_pull = jax.vjp(
        finish,
        y_zero,
        reach,
        values_x,
        read_c,
        gate_cols,
        incoming,
        head_params.astype(jnp.float32),
        output_gain.astype(jnp.float32),
    )
    gated_low = gated.astype(jnp.bfloat16)
    grad_gated = contract_cols(upstream, out_proj)
    (
        grad_y_zero,
        grad_reach,
        grad_values_x,
        grad_read_c,
        grad_gate,
        grad_incoming,
        grad_heads_late,
        grad_output_gain,
    ) = finish_pull(grad_gated)
    adjoint = pass_adjoints(grad_incoming)
    grad_decay = jnp.sum(adjoint * incoming, axis=(1, 2))
    grad_raw, grad_edge, grad_step, grad_conv_weight, grad_conv_bias, grad_heads_early = front_pull(
        (grad_values_x, grad_read_c, grad_y_zero, adjoint, grad_decay, grad_reach)
    )
    returned = shifted(grad_edge, "group", -1)
    grad_raw = jnp.concatenate(
        [grad_raw[: length - KW + 1], grad_raw[length - KW + 1 :] + returned], axis=0
    )
    grad_projected = jnp.concatenate([grad_gate, grad_raw, grad_step], axis=1).astype(jnp.bfloat16)
    grad_normed = contract_cols(grad_projected, in_proj)
    grad_in_proj, grad_out_proj = projection_grads(normed, grad_projected, gated_low, upstream)
    unused_norm, norm_pull = jax.vjp(rms_scale, values, gain_float)
    grad_values, grad_input_gain = norm_pull(grad_normed)
    grad_values = grad_values + upstream.astype(jnp.float32)
    grads = (
        grad_input_gain,
        grad_in_proj,
        grad_conv_weight,
        grad_conv_bias,
        grad_heads_late + grad_heads_early,
        grad_output_gain,
        grad_out_proj,
    )
    return (grad_values, grads)


def on_device(
    first_layer_input,
    boundary,
    input_gain,
    in_proj,
    conv_weight,
    conv_bias,
    head_params,
    output_gain,
    out_proj,
    cotangent,
):
    section_index = lax.axis_index("section")
    micro_count = first_layer_input.shape[0]
    tokens_dev = first_layer_input.shape[2]
    positions = lax.axis_index("group") * tokens_dev + jnp.arange(tokens_dev, dtype=jnp.int32)
    bounds = boundary[:, 0]
    gathered = (
        lax.all_gather(input_gain, "group", axis=1, tiled=True),
        lax.all_gather(in_proj, "group", axis=1, tiled=True),
        lax.all_gather(conv_weight, "group", axis=1, tiled=True),
        lax.all_gather(conv_bias, "group", axis=1, tiled=True),
        lax.all_gather(head_params, "group", axis=1, tiled=True),
        lax.all_gather(output_gain, "group", axis=1, tiled=True),
        lax.all_gather(out_proj, "group", axis=1, tiled=True),
    )
    weights = tuple((piece[0] for piece in gathered))
    inputs = jnp.zeros((micro_count, tokens_dev, MODEL_WIDTH), jnp.bfloat16)
    outputs = jnp.zeros((micro_count, tokens_dev, MODEL_WIDTH), jnp.bfloat16)
    edges = jnp.zeros((micro_count, KW - 1, CONVC), jnp.float32)
    states = jnp.zeros((micro_count, HEADS, HDIM, NS), jnp.float32)
    arrived = jnp.zeros((tokens_dev, MODEL_WIDTH), jnp.bfloat16)
    for moment in range(micro_count + 1):
        slot_raw = moment - section_index
        is_valid = (slot_raw >= 0) & (slot_raw < micro_count)
        slot_index = jnp.clip(slot_raw, 0, micro_count - 1)
        boundary_pos = read_slot(bounds, slot_index)
        layer_in = jnp.where(
            section_index == 0, first_layer_input[min(moment, micro_count - 1), 0], arrived
        )
        result, edge_rows, incoming = layer_forward(layer_in, boundary_pos, weights, positions)
        result_low = result.astype(jnp.bfloat16)
        inputs = store_slot(inputs, layer_in, slot_index, is_valid)
        outputs = store_slot(outputs, result_low, slot_index, is_valid)
        edges = store_slot(edges, edge_rows, slot_index, is_valid)
        states = store_slot(states, incoming, slot_index, is_valid)
        if moment < micro_count:
            arrived = shifted(result_low, "section", 1)
    again = (
        lax.all_gather(input_gain, "group", axis=1, tiled=True),
        lax.all_gather(in_proj, "group", axis=1, tiled=True),
        lax.all_gather(conv_weight, "group", axis=1, tiled=True),
        lax.all_gather(conv_bias, "group", axis=1, tiled=True),
        lax.all_gather(head_params, "group", axis=1, tiled=True),
        lax.all_gather(output_gain, "group", axis=1, tiled=True),
        lax.all_gather(out_proj, "group", axis=1, tiled=True),
    )
    back_weights = tuple((piece[0] for piece in again))
    totals = None
    grad_store = jnp.zeros((micro_count, tokens_dev, MODEL_WIDTH), jnp.bfloat16)
    arrived_grad = jnp.zeros((tokens_dev, MODEL_WIDTH), jnp.bfloat16)
    for moment in range(micro_count + 1):
        slot_raw = moment - 1 + section_index
        is_valid = (slot_raw >= 0) & (slot_raw < micro_count)
        slot_index = jnp.clip(slot_raw, 0, micro_count - 1)
        boundary_pos = read_slot(bounds, slot_index)
        upstream = jnp.where(
            section_index == 1, cotangent[min(moment, micro_count - 1), 0], arrived_grad
        )
        grad_values, grads = layer_backward(
            read_slot(inputs, slot_index),
            boundary_pos,
            read_slot(edges, slot_index),
            read_slot(states, slot_index),
            back_weights,
            upstream,
            positions,
        )
        masked = tuple((jnp.where(is_valid, piece, 0.0) for piece in grads))
        if totals is None:
            totals = masked
        else:
            totals = tuple((total + piece for total, piece in zip(totals, masked)))
        sent = grad_values.astype(jnp.bfloat16)
        grad_store = store_slot(grad_store, sent, slot_index, is_valid)
        if moment < micro_count:
            arrived_grad = shifted(sent, "section", -1)
    shares = (
        lax.psum_scatter(
            totals[0].astype(jnp.bfloat16), "group", scatter_dimension=0, tiled=True
        ).astype(jnp.float32),
        lax.psum_scatter(
            totals[1].astype(jnp.bfloat16), "group", scatter_dimension=0, tiled=True
        ).astype(jnp.float32),
        lax.psum_scatter(
            totals[2].astype(jnp.bfloat16), "group", scatter_dimension=0, tiled=True
        ).astype(jnp.float32),
        lax.psum_scatter(
            totals[3].astype(jnp.bfloat16), "group", scatter_dimension=0, tiled=True
        ).astype(jnp.float32),
        lax.psum_scatter(
            totals[4].astype(jnp.bfloat16), "group", scatter_dimension=0, tiled=True
        ).astype(jnp.float32),
        lax.psum_scatter(
            totals[5].astype(jnp.bfloat16), "group", scatter_dimension=0, tiled=True
        ).astype(jnp.float32),
        lax.psum_scatter(
            totals[6].astype(jnp.bfloat16), "group", scatter_dimension=0, tiled=True
        ).astype(jnp.float32),
    )
    summed = (
        lax.psum(shares[0].astype(jnp.bfloat16), "replica").astype(jnp.float32),
        lax.psum(shares[1].astype(jnp.bfloat16), "replica").astype(jnp.float32),
        lax.psum(shares[2].astype(jnp.bfloat16), "replica").astype(jnp.float32),
        lax.psum(shares[3].astype(jnp.bfloat16), "replica").astype(jnp.float32),
        lax.psum(shares[4].astype(jnp.bfloat16), "replica").astype(jnp.float32),
        lax.psum(shares[5].astype(jnp.bfloat16), "replica").astype(jnp.float32),
        lax.psum(shares[6].astype(jnp.bfloat16), "replica").astype(jnp.float32),
    )
    return (
        outputs[None, :, None],
        grad_store[None, :, None],
        summed[0][None],
        summed[1][None],
        summed[2][None],
        summed[3][None],
        summed[4][None],
        summed[5][None],
        summed[6][None],
    )


def solution(mesh):
    placed = (
        P(None, "replica", "group", None),
        P(None, "replica"),
        P("section", "group"),
        P("section", "group", None),
        P("section", "group", None),
        P("section", "group"),
        P("section", "group", None),
        P("section", "group"),
        P("section", "group", None),
        P(None, "replica", "group", None),
    )
    return jax.shard_map(
        on_device,
        mesh=mesh,
        in_specs=placed,
        out_specs=(
            P("section", None, "replica", "group", None),
            P("section", None, "replica", "group", None),
            P("section", "group"),
            P("section", "group", None),
            P("section", "group", None),
            P("section", "group"),
            P("section", "group", None),
            P("section", "group"),
            P("section", "group", None),
        ),
        check_vma=False,
    )
```

profile of v0, /device:TPU:0, one launch (start us, length us, event | category | flops | bytes accessed | tf_op | source)
XLA Modules:
  0.0 1491.3 jit_solution(10965129176252997882)
XLA Ops:
  49.4 5.3 all_gather.33
  83.1 42.8 %all-gather.3.cloned.1.call-done = bf16[1,1024,4384]{1,2,0:T(8,128)(2,1)} async-done(((bf16[1,512,4384]{1,2,0:T(8,128)(2,1)}), bf16[1,1024,4384]{1,2,0:T(8,128)(2,1)}) %all-gather.3.cloned.1.call-update) | async-done | bytes 8978448 | tf_op jit(solution)/shard_map/all_gather | solution.py:290
  125.9 6.4 fusion.16
  152.7 7.0 divide_multiply_fusion.2
  175.6 29.5 %collective-permute-done.1 = f32[32,64,128]{2,1,0:T(8,128)S(1)} collective-permute-done((f32[32,64,128]{2,1,0:T(8,128)S(1)}, f32[32,64,128]{2,1,0:T(8,128)S(1)}, u32[]{:S(2)}, u32[]{:S(2)}) %collective-permute-start.1) | collective-permute-done | bytes 1048608 | tf_op jit(solution)/shard_map/ppermute | solution.py:19
  208.9 10.9 fusion.218
  235.3 6.4 fusion.14
  246.4 5.0 collective-permute-start.3
  275.1 7.1 divide_multiply_fusion.1
  298.2 16.6 %collective-permute-done.4 = f32[32,64,128]{2,1,0:T(8,128)S(1)} collective-permute-done((f32[32,64,128]{2,1,0:T(8,128)S(1)}, f32[32,64,128]{2,1,0:T(8,128)S(1)}, u32[]{:S(2)}, u32[]{:S(2)}) %collective-permute-start.4) | collective-permute-done | bytes 1048608 | tf_op jit(solution)/shard_map/ppermute | solution.py:19
  318.5 11.0 fusion.216
  335.8 5.4 bitcast_dynamic-update-slice_fusion.8
  352.8 5.2 collective-permute-start.6
  359.4 6.2 fusion.10
  388.0 7.0 divide_multiply_fusion
  423.2 5.9 collective-permute-done.7
  432.5 11.6 fusion.212
  476.8 6.4 fusion.389
  483.2 10.5 collective-permute-done.8
  513.8 13.3 fusion.67
  540.0 10.2 bitcast_add_fusion.4
  553.1 6.1 fusion.347
  559.2 5.0 fusion.710
  567.6 5.8 convolution_bitcast_fusion.2
  575.9 5.2 fusion.353
  581.2 6.0 fusion.676
  615.8 7.4 fusion.360
  641.1 8.8 fusion.449
  665.3 14.1 fusion.207
  682.4 4.7 multiply_reduce_fusion.34
  692.1 6.6 fusion.2
  731.1 6.5 fusion.390
  737.6 12.1 collective-permute-done.11
  766.6 5.1 multiply_reduce_fusion.19
  771.9 13.3 fusion.69
  798.2 10.2 bitcast_add_fusion.2
  811.3 6.1 fusion.338
  817.4 5.0 fusion.709
  825.7 5.8 convolution_bitcast_fusion.1
  833.4 5.3 fusion.344
  838.9 6.1 fusion.677
  845.1 4.8 select_multiply_fusion.7
  887.2 14.1 fusion.202
  916.3 7.1 fusion.358
  926.7 8.7 fusion.451
  938.0 4.6 multiply_reduce_fusion.24
  960.5 8.2 add_convert_fusion.1
  969.3 11.6 collective-permute-done.14
  997.8 5.1 multiply_reduce_fusion.18
  1003.1 13.4 fusion.71
  1039.2 10.0 bitcast_add_fusion
  1052.2 5.5 fusion.708
  1062.3 5.2 convolution_bitcast_fusion
  1070.6 4.8 fusion.329
  1080.0 5.4 fusion.678
  1094.8 10.5 add_convert_fusion
  1109.8 109.1 %reduce-scatter.9.cloned.1.call-done = bf16[512,4384]{0,1:T(8,128)(2,1)} async-done(((bf16[1024,4384]{0,1:T(8,128)(2,1)}), bf16[512,4384]{0,1:T(8,128)(2,1)}) %reduce-scatter.9.cloned.1.call-update) | async-done | bytes 4489232 | tf_op jit(solution)/shard_map/reduce_scatter | solution.py:362
  1237.7 10.9 fusion.214
  1255.0 4.9 fusion.308
  1261.8 8.0 fusion.356
  1269.8 6.9 all-reduce.53
  1280.5 39.7 %all-reduce.51 = (bf16[1,16,3]{1,2,0:T(4,128)(2,1)S(1)}, bf16[1,512]{1,0:T(2,128)(2,1)S(1)}, bf16[1,1152,4]{1,2,0:T(4,128)(2,1)S(1)}, bf16[1,1152]{1,0:T(2,128)(2,1)S(1)}, bf16[1,1024]{1,0:T(2,128)(2,1)S(1)}) all-reduce(bf16[1,16,3]{1,2,0:T(4,128)(2,1)S(1)} %bitcast.1015, ...), channel_id=1, replica_groups=mesh['section'=2,'group'=2,'replica'=8] {'replica'}, use_global_device_ids=true, to_apply=%region_117.119 | all-reduce | flops 7344 | bytes 29376 | tf_op jit(solution)/shard_map/psum | solution.py:386
  1323.2 151.1 %all-reduce.56.cloned.1.call-done = (bf16[1,512,4384]{1,2,0:T(8,128)(2,1)}, bf16[1,1024,1024]{2,1,0:T(8,128)(2,1)}) async-done(((bf16[1,512,4384]{1,2,0:T(8,128)(2,1)}, bf16[1,1024,1024]{2,1,0:T(8,128)(2,1)}), (bf16[1,512,4384]{1,2,0:T(8,128)(2,1)}, bf16[1,1024,1024]{2,1,0:T(8,128)(2,1)})) %all-reduce.56.cloned.1.call-update) | async-done | bytes 6586384 | tf_op jit(solution)/shard_map/psum | solution.py:383
  1474.3 7.3 broadcast_in_dim.1273
  (1229 shorter events, 614.1 us)
Async XLA Ops:
  7.2 42.2 %copy-start.299 = (bf16[1,1024]{1,0:T(2,128)(2,1)S(1)}, bf16[1,1024]{1,0:T(2,128)(2,1)}, u32[]{:S(2)}) copy-start(bf16[1,1024]{1,0:T(2,128)(2,1)} %param.18) | copy-start | bytes 6148
  7.2 47.5 %copy-start.338 = (bf16[1,512]{1,0:T(2,128)(2,1)S(1)}, bf16[1,512]{1,0:T(2,128)(2,1)}, u32[]{:S(2)}) copy-start(bf16[1,512]{1,0:T(2,128)(2,1)} %param.13) | copy-start | bytes 3076
  7.2 51.8 %copy-start.96 = (bf16[2,1,256,1024]{3,2,1,0:T(8,128)(2,1)S(1)}, bf16[2,1,256,1024]{3,2,1,0:T(8,128)(2,1)}, u32[]{:S(2)}) copy-start(bf16[2,1,256,1024]{3,2,1,0:T(8,128)(2,1)} %param.11) | copy-start | bytes 3145732
  7.2 118.7 %all-gather.3.cloned.1.call-start = ((), (), s32[]{:S(2)}) async-start(), calls=%async_computation.4 | async-start | bytes 13467648 | tf_op jit(solution)/shard_map/all_gather | solution.py:290
  8.0 51.3 %copy-start.260 = (bf16[1,1152,4]{1,2,0:T(4,128)(2,1)S(1)}, bf16[1,1152,4]{1,2,0:T(4,128)(2,1)}, u32[]{:S(2)}) copy-start(bf16[1,1152,4]{1,2,0:T(4,128)(2,1)} %param.15) | copy-start | bytes 27652
  8.0 55.9 %copy-start.297 = (bf16[1,1152]{1,0:T(2,128)(2,1)S(1)}, bf16[1,1152]{1,0:T(2,128)(2,1)}, u32[]{:S(2)}) copy-start(bf16[1,1152]{1,0:T(2,128)(2,1)} %param.16) | copy-start | bytes 6916
  8.0 61.6 %copy-start.344 = (bf16[1,16,3]{1,2,0:T(4,128)(2,1)S(1)}, bf16[1,16,3]{1,2,0:T(4,128)(2,1)}, u32[]{:S(2)}) copy-start(bf16[1,16,3]{1,2,0:T(4,128)(2,1)} %param.17) | copy-start | bytes 292
  8.0 217.0 %all-gather.5.cloned.1.call-start = ((), (), s32[]{:S(2)}) async-start(), calls=%async_computation.5 | async-start | bytes 6291456 | tf_op jit(solution)/shard_map/all_gather | solution.py:295
  8.7 1101.0 %reduce-scatter.11.cloned.1.call-start = ((), (), s32[]{:S(2)}) async-start(), calls=%async_computation.7 | async-start | bytes 6291456 | tf_op jit(solution)/shard_map/reduce_scatter | solution.py:377
  63.9 211.1 %copy-start.121 = (f32[2304]{0:T(1024)}, f32[2304]{0:T(1024)S(1)}, u32[]{:S(2)}) copy-start(f32[2304]{0:T(1024)S(1)} %get-tuple-element.749) | copy-start | bytes 27652
  63.9 211.1 %copy-start.127 = (f32[2304]{0:T(1024)}, f32[2304]{0:T(1024)S(1)}, u32[]{:S(2)}) copy-start(f32[2304]{0:T(1024)S(1)} %get-tuple-element.750) | copy-start | bytes 27652
  63.9 211.1 %copy-start.133 = (f32[2304]{0:T(1024)}, f32[2304]{0:T(1024)S(1)}, u32[]{:S(2)}) copy-start(f32[2304]{0:T(1024)S(1)} %get-tuple-element.751) | copy-start | bytes 27652
  63.9 211.1 %copy-start.139 = (f32[2304]{0:T(1024)}, f32[2304]{0:T(1024)S(1)}, u32[]{:S(2)}) copy-start(f32[2304]{0:T(1024)S(1)} %get-tuple-element.752) | copy-start | bytes 27652
  68.4 84.2 %copy-start.147 = (f32[2304]{0:T(1024)}, f32[2304]{0:T(1024)S(1)}, u32[]{:S(2)}) copy-start(f32[2304]{0:T(1024)S(1)} %convert_reduce_fusion) | copy-start | bytes 27652
  74.3 51.6 %copy-start.339 = (f32[32]{0:T(128)}, f32[32]{0:T(128)S(1)}, u32[]{:S(2)}) copy-start(f32[32]{0:T(128)S(1)} %get-tuple-element.902) | copy-start | bytes 388
  74.3 63.4 %copy-start.246 = (f32[32]{0:T(128)}, f32[32]{0:T(128)S(1)}, u32[]{:S(2)}) copy-start(f32[32]{0:T(128)S(1)} %get-tuple-element.903) | copy-start | bytes 388
  74.3 64.5 %copy-start.206 = (f32[32]{0:T(128)}, f32[32]{0:T(128)S(1)}, u32[]{:S(2)}) copy-start(f32[32]{0:T(128)S(1)} %get-tuple-element.904) | copy-start | bytes 388
  135.4 17.2 %collective-permute-start = (f32[3,2304]{1,0:T(4,128)}, f32[3,2304]{1,0:T(4,128)S(1)}, u32[]{:S(2)}, u32[]{:S(2)}) collective-permute-start(f32[3,2304]{1,0:T(4,128)} %copy.685), channel_id=1, source_target_pairs={{0,8},{1,9},{2,10},{3,11},{4,12},{5,13},{6,14},{7,15},{16,24},{17,... | collective-permute-start | bytes 82952 | tf_op jit(solution)/shard_map/ppermute | solution.py:19
  169.0 36.1 %collective-permute-start.1 = (f32[32,64,128]{2,1,0:T(8,128)S(1)}, f32[32,64,128]{2,1,0:T(8,128)S(1)}, u32[]{:S(2)}, u32[]{:S(2)}) collective-permute-start(f32[32,64,128]{2,1,0:T(8,128)S(1)} %fusion.258), channel_id=1, source_target_pairs={{0,8},{1,9},{2,10},{3,11},{4,12},{5,13},{6,14},{7,15},{16,24},{17,... | collective-permute-start | bytes 3145736 | tf_op jit(solution)/shard_map/ppermute | solution.py:19
  173.3 35.5 %copy-start.73 = (f32[256,2048]{0,1:T(8,128)S(1)}, f32[256,2048]{0,1:T(8,128)}, u32[]{:S(2)}) copy-start(f32[256,2048]{0,1:T(8,128)} %copy.687) | copy-start | bytes 6291460
  173.3 35.5 %copy-start.202 = (pred[256,256]{1,0:T(8,128)(4,1)S(1)}, pred[256,256]{1,0:T(8,128)(4,1)}, u32[]{:S(2)}) copy-start(pred[256,256]{1,0:T(8,128)(4,1)} %get-tuple-element.914) | copy-start | bytes 196612
  173.3 35.5 %copy-start.234 = (f32[32,256]{1,0:T(8,128)S(1)}, f32[32,256]{1,0:T(8,128)}, u32[]{:S(2)}) copy-start(f32[32,256]{1,0:T(8,128)} %copy.695) | copy-start | bytes 98308
  173.4 35.5 %copy-start.235 = (f32[32,256]{1,0:T(8,128)S(1)}, f32[32,256]{1,0:T(8,128)}, u32[]{:S(2)}) copy-start(f32[32,256]{1,0:T(8,128)} %copy.693) | copy-start | bytes 98308
  173.4 35.5 %copy-start.237 = (f32[256,32]{0,1:T(8,128)S(1)}, f32[256,32]{0,1:T(8,128)}, u32[]{:S(2)}) copy-start(f32[256,32]{0,1:T(8,128)} %copy.696) | copy-start | bytes 98308
  173.4 35.5 %copy-start.340 = (f32[32]{0:T(128)S(1)}, f32[32]{0:T(128)}, u32[]{:S(2)}) copy-start(f32[32]{0:T(128)} %copy-done.339) | copy-start | bytes 388
  229.6 4.6 collective-permute-start.2
  246.4 28.7 %collective-permute-start.3 = (f32[3,2304]{1,0:T(4,128)}, f32[3,2304]{1,0:T(4,128)}, u32[]{:S(2)}, u32[]{:S(2)}) collective-permute-start(f32[3,2304]{1,0:T(4,128)} %copy.700), channel_id=1, source_target_pairs={{0,8},{1,9},{2,10},{3,11},{4,12},{5,13},{6,14},{7,15},{16,24},{17,... | collective-permute-start | bytes 82952 | tf_op jit(solution)/shard_map/ppermute | solution.py:19
  291.5 23.2 %collective-permute-start.4 = (f32[32,64,128]{2,1,0:T(8,128)S(1)}, f32[32,64,128]{2,1,0:T(8,128)S(1)}, u32[]{:S(2)}, u32[]{:S(2)}) collective-permute-start(f32[32,64,128]{2,1,0:T(8,128)S(1)} %fusion.261), channel_id=1, source_target_pairs={{0,8},{1,9},{2,10},{3,11},{4,12},{5,13},{6,14},{7,15},{16,24},{17,... | collective-permute-start | bytes 3145736 | tf_op jit(solution)/shard_map/ppermute | solution.py:19
  294.4 24.1 %copy-start.74 = (f32[256,2048]{0,1:T(8,128)S(1)}, f32[256,2048]{0,1:T(8,128)}, u32[]{:S(2)}) copy-start(f32[256,2048]{0,1:T(8,128)} %copy.702) | copy-start | bytes 6291460
  294.4 24.1 %copy-start.199 = (pred[256,256]{1,0:T(8,128)(4,1)S(1)}, pred[256,256]{1,0:T(8,128)(4,1)}, u32[]{:S(2)}) copy-start(pred[256,256]{1,0:T(8,128)(4,1)} %get-tuple-element.913) | copy-start | bytes 196612
  294.4 24.1 %copy-start.236 = (f32[32,256]{1,0:T(8,128)S(1)}, f32[32,256]{1,0:T(8,128)}, u32[]{:S(2)}) copy-start(f32[32,256]{1,0:T(8,128)} %copy.708) | copy-start | bytes 98308
  294.5 24.1 %copy-start.238 = (f32[32,256]{1,0:T(8,128)S(1)}, f32[32,256]{1,0:T(8,128)}, u32[]{:S(2)}) copy-start(f32[32,256]{1,0:T(8,128)} %copy.706) | copy-start | bytes 98308
  294.5 24.1 %copy-start.239 = (f32[256,32]{0,1:T(8,128)S(1)}, f32[256,32]{0,1:T(8,128)}, u32[]{:S(2)}) copy-start(f32[256,32]{0,1:T(8,128)} %copy.709) | copy-start | bytes 98308
  294.5 24.1 %copy-start.341 = (f32[32]{0:T(128)S(1)}, f32[32]{0:T(128)}, u32[]{:S(2)}) copy-start(f32[32]{0:T(128)} %copy-done.339) | copy-start | bytes 388
  298.2 44.4 %copy-start.145 = (f32[2,3,2304]{2,1,0:T(4,128)}, f32[2,3,2304]{2,1,0:T(4,128)S(1)}, u32[]{:S(2)}) copy-start(f32[2,3,2304]{2,1,0:T(4,128)S(1)} %bitcast_dynamic-update-slice_fusion.11) | copy-start | bytes 165892
  341.2 3.2 collective-permute-start.5
  352.8 35.1 %collective-permute-start.6 = (f32[3,2304]{1,0:T(4,128)}, f32[3,2304]{1,0:T(4,128)}, u32[]{:S(2)}, u32[]{:S(2)}) collective-permute-start(f32[3,2304]{1,0:T(4,128)} %copy.713), channel_id=1, source_target_pairs={{0,8},{1,9},{2,10},{3,11},{4,12},{5,13},{6,14},{7,15},{16,24},{17,... | collective-permute-start | bytes 82952 | tf_op jit(solution)/shard_map/ppermute | solution.py:19
  405.5 23.7 %collective-permute-start.7 = (f32[32,64,128]{2,1,0:T(8,128)}, f32[32,64,128]{2,1,0:T(8,128)S(1)}, u32[]{:S(2)}, u32[]{:S(2)}) collective-permute-start(f32[32,64,128]{2,1,0:T(8,128)} %fusion.264), channel_id=1, source_target_pairs={{0,8},{1,9},{2,10},{3,11},{4,12},{5,13},{6,14},{7,15},{16,24},{17,... | collective-permute-start | bytes 3145736 | tf_op jit(solution)/shard_map/ppermute | solution.py:19
  467.9 25.8 %collective-permute-start.8 = (f32[32,64,128]{2,1,0:T(8,128)}, f32[32,64,128]{2,1,0:T(8,128)S(1)}, u32[]{:S(2)}, u32[]{:S(2)}) collective-permute-start(f32[32,64,128]{2,1,0:T(8,128)} %fusion.237), channel_id=1, source_target_pairs={{8,0},{9,1},{10,2},{11,3},{12,4},{13,5},{14,6},{15,7},{24,16},{25,... | collective-permute-start | bytes 3145736 | tf_op jit(solution)/shard_map/ppermute | solution.py:19
  476.8 21.4 %copy-start.118 = (f32[256,32]{1,0:T(8,128)S(1)}, f32[256,32]{1,0:T(8,128)}, u32[]{:S(2)}) copy-start(f32[256,32]{1,0:T(8,128)} %copy-done.117) | copy-start | bytes 98308
  513.8 13.3 copy-start.204
  606.9 7.3 collective-permute-start.9
  652.3 51.5 %collective-permute-start.10 = (bf16[256,1024]{1,0:T(8,128)(2,1)}, bf16[256,1024]{1,0:T(8,128)(2,1)}, u32[]{:S(2)}, u32[]{:S(2)}) collective-permute-start(bf16[256,1024]{1,0:T(8,128)(2,1)} %get-tuple-element.807), channel_id=1, source_target_pairs={{16,0},{17,1},{18,2},{19,3},{20,4},{21,5},{22,6},{23,7},{24,8},{25... | collective-permute-start | bytes 1572872 | tf_op jit(solution)/shard_map/ppermute | solution.py:19
  722.0 27.7 %collective-permute-start.11 = (f32[32,64,128]{2,1,0:T(8,128)}, f32[32,64,128]{2,1,0:T(8,128)}, u32[]{:S(2)}, u32[]{:S(2)}) collective-permute-start(f32[32,64,128]{2,1,0:T(8,128)} %fusion.230), channel_id=1, source_target_pairs={{8,0},{9,1},{10,2},{11,3},{12,4},{13,5},{14,6},{15,7},{24,16},{25,... | collective-permute-start | bytes 3145736 | tf_op jit(solution)/shard_map/ppermute | solution.py:19
  731.0 27.9 %copy-start.104 = (f32[256,128]{1,0:T(8,128)S(1)}, f32[256,128]{1,0:T(8,128)}, u32[]{:S(2)}) copy-start(f32[256,128]{1,0:T(8,128)} %get-tuple-element.622) | copy-start | bytes 393220
  792.8 38.7 %copy-start.108 = (f32[256,32]{1,0:T(8,128)}, f32[256,32]{1,0:T(8,128)S(1)}, u32[]{:S(2)}) copy-start(f32[256,32]{1,0:T(8,128)S(1)} %copy.841) | copy-start | bytes 98308
  849.9 14.1 copy-start.24
  871.4 42.9 %collective-permute-start.12 = (f32[3,2304]{1,0:T(4,128)}, f32[3,2304]{1,0:T(4,128)}, u32[]{:S(2)}, u32[]{:S(2)}) collective-permute-start(f32[3,2304]{1,0:T(4,128)} %pad_add_fusion.4), channel_id=1, source_target_pairs={{8,0},{9,1},{10,2},{11,3},{12,4},{13,5},{14,6},{15,7},{24,16},{25,... | collective-permute-start | bytes 82952 | tf_op jit(solution)/shard_map/ppermute | solution.py:19
  908.5 29.5 %copy-start.211 = (f32[256]{0:T(256)}, f32[256]{0:T(256)S(1)}, u32[]{:S(2)}) copy-start(f32[256]{0:T(256)S(1)} %fusion.602) | copy-start | bytes 3076
  924.9 10.5 collective-permute-start.13
  952.6 28.3 %collective-permute-start.14 = (f32[32,64,128]{2,1,0:T(8,128)}, f32[32,64,128]{2,1,0:T(8,128)}, u32[]{:S(2)}, u32[]{:S(2)}) collective-permute-start(f32[32,64,128]{2,1,0:T(8,128)} %fusion.223), channel_id=1, source_target_pairs={{8,0},{9,1},{10,2},{11,3},{12,4},{13,5},{14,6},{15,7},{24,16},{25,... | collective-permute-start | bytes 3145736 | tf_op jit(solution)/shard_map/ppermute | solution.py:19
  968.7 16.3 %copy-start.119 = (f32[256,32]{1,0:T(8,128)S(1)}, f32[256,32]{1,0:T(8,128)}, u32[]{:S(2)}) copy-start(f32[256,32]{1,0:T(8,128)} %get-tuple-element.628) | copy-start | bytes 98308
  968.7 21.4 %copy-start.102 = (f32[256,128]{1,0:T(8,128)S(1)}, f32[256,128]{1,0:T(8,128)}, u32[]{:S(2)}) copy-start(f32[256,128]{1,0:T(8,128)} %get-tuple-element.634) | copy-start | bytes 393220
  968.7 250.1 %reduce-scatter.9.cloned.1.call-start = ((), (), s32[]{:S(2)}) async-start(), calls=%async_computation.6 | async-start | bytes 13467648 | tf_op jit(solution)/shard_map/reduce_scatter | solution.py:362
  1003.1 13.4 copy-start.203
  1003.1 16.4 %copy-start.189 = (f32[256,32]{0,1:T(8,128)S(1)}, f32[256,32]{0,1:T(8,128)}, u32[]{:S(2)}) copy-start(f32[256,32]{0,1:T(8,128)} %multiply_reduce_fusion.27) | copy-start | bytes 98308
  1003.1 18.6 %copy-start.271 = (pred[256]{0:T(512)(128)(4,1)S(1)}, pred[256]{0:T(512)(128)(4,1)}, u32[]{:S(2)}) copy-start(pred[256]{0:T(512)(128)(4,1)} %get-tuple-element.908) | copy-start | bytes 772
  1062.3 17.6 %copy-start.71 = (f32[256,2048]{1,0:T(8,128)S(1)}, f32[256,2048]{1,0:T(8,128)}, u32[]{:S(2)}) copy-start(f32[256,2048]{1,0:T(8,128)} %get-tuple-element.853) | copy-start | bytes 6291460
  1086.4 6.5 collective-permute-start.15
  1105.6 155.4 %reduce-scatter.15.cloned.1.call-start = ((), (), s32[]{:S(2)}) async-start(), calls=%async_computation.9 | async-start | bytes 12288
  1108.4 171.0 %reduce-scatter.13.cloned.1.call-start = ((), (), s32[]{:S(2)}) async-start(), calls=%async_computation.8 | async-start | bytes 884736
  1109.7 364.6 %all-reduce.56.cloned.1.call-start = ((), (), s32[]{:S(2)}) async-start(), calls=%async_computation.10 | async-start | bytes 13172736 | tf_op jit(solution)/shard_map/psum | solution.py:383
  1261.8 15.1 %copy-start.301 = (f32[256]{0:T(256)S(1)}, f32[256]{0:T(256)}, u32[]{:S(2)}) copy-start(f32[256]{0:T(256)} %get-tuple-element.748) | copy-start | bytes 3076
  1261.8 15.1 %copy-start.67 = (bf16[256,1024]{1,0:T(8,128)(2,1)S(1)}, bf16[256,1024]{1,0:T(8,128)(2,1)}, u32[]{:S(2)}) copy-start(bf16[256,1024]{1,0:T(8,128)(2,1)} %copy-done.66) | copy-start | bytes 1572868
  (312 other events, 1441.9 us)
Sparse Core Ops, SparseCore 0:
  9.6 116.2 all-gather.2
  127.5 67.1 all-gather.4
  968.9 60.4 reduce-scatter.10
  1105.7 113.0 reduce-scatter.8
  1220.9 9.7 reduce-scatter.14
  1232.9 15.2 reduce-scatter.12
  1252.3 221.9 all-reduce.55
where the time goes:
time: 1510 us; the launch traced here: 1490 us
  matrix products  419 us (28%)
  waiting for transfers between devices  391 us (26%)
  local copies, waits for them, and re-layouts  278 us (18%)
  other arithmetic  256 us (17%)
  blocking collectives  69.7 us (5%)
  between operations  45.6 us (3%)
  starting transfers between devices  32.5 us (2%)
    psum x1, waiting for transfers between devices, on_device(): lax.psum(shares[1].astype(jnp.bfloat16), 'replica').astype(jnp.float32)  151 us
    dot_general x12, matrix products, block_step(): direct = jnp.einsum('hij,jhp->ihp', mixing, block_x, precision=highest)  143 us
    reduce_scatter x1, waiting for transfers between devices, on_device(): lax.psum_scatter(totals[1].astype(jnp.bfloat16), 'group', scatter_dimensi...  109 us
    ppermute x16, waiting for transfers between devices, shifted(): return lax.ppermute(block, axis, route)  86.2 us
    unnamed x728, local copies, waits for them, and re-layouts  58.5 us
    dot_general x6, matrix products, contract_rows(): lax.dot_general(left, right, (((0,), (0,)), ((), ())), preferred_element_...  49.2 us
    dot_general x12, matrix products, finish(): jnp.einsum('in,hpn->ihp', read_c, incoming, precision=lax.Precision.HIGHEST)  45.5 us
    dot_general x12, matrix products, block_step(): carried = jnp.einsum('in,hpn->ihp', block_c, state, precision=highest)  44.8 us
  transfers between devices with their start and end apart: 23, of which 9 were waited for; matrix products, arithmetic and copies ran while one was open for 33% of the time, Pallas kernels for 0%

commit v1 on v0

v1 whole, which is shorter than its diff:
```python
import functools

import jax
import jax.numpy as jnp
from jax import lax
from jax.experimental import pallas as pl
from jax.experimental.pallas import tpu as pltpu
from jax.sharding import PartitionSpec as P

DM = 1024
HEADS = 32
HDIM = 64
NS = 128
KW = 4
DI = 2048
CONVC = 2304
HL = HEADS // 2
DH = DI // 2
CH = DH + 2 * NS
CP = DH + CH + 128
LANE = 128
TILE = 256
RC = 32
HEAD_ROWS = 8
EPS = 1e-05
VMEM_BYTES = 63 * 1024 * 1024

f32 = jnp.float32
bf16 = jnp.bfloat16


def nn(left, right):
    return jnp.dot(left, right, preferred_element_type=f32)


def nt(left, right):
    return lax.dot_general(left, right, (((1,), (1,)), ((), ())), preferred_element_type=f32)


def tn(left, right):
    return lax.dot_general(left, right, (((0,), (0,)), ((), ())), preferred_element_type=f32)


def tile_at(index, size):
    return pl.ds(pl.multiple_of(index * size, size), size)


def loop(count, body):
    def step(index, carry):
        body(index)
        return carry

    lax.fori_loop(0, count, step, 0)


def iota(shape, dim):
    return lax.broadcasted_iota(jnp.int32, shape, dim)


def sigmoid(values):
    return 0.5 * jnp.tanh(0.5 * values) + 0.5


def softplus(values):
    small = jnp.exp(-jnp.abs(values))
    series = small * (1.0 - small * (0.5 - small * (1.0 / 3.0 - small * 0.25)))
    return jnp.maximum(values, 0.0) + jnp.where(small < 0.03, series, jnp.log(1.0 + small))


def split3(values):
    high = values.astype(bf16)
    rest = values - high.astype(f32)
    middle = rest.astype(bf16)
    low = (rest - middle.astype(f32)).astype(bf16)
    return high, middle, low


def pack3(values):
    high, middle, low = split3(values)
    packed = (
        high.astype(f32)
        + pltpu.roll(middle.astype(f32), HL, 1)
        + pltpu.roll(low.astype(f32), 2 * HL, 1)
    )
    return packed.astype(bf16)


def fill_spread(spread_s, width):
    shape = spread_s.shape
    row = iota(shape, 0)
    col = iota(shape, 1)
    hit = (row < 3 * HL) & ((row & (HL - 1)) == col // width)
    spread_s[...] = jnp.where(hit, 1.0, 0.0).astype(bf16)


def fill_gather(gather_s):
    shape = gather_s.shape
    hit = iota(shape, 0) // HDIM == iota(shape, 1)
    gather_s[...] = jnp.where(hit, 1.0, 0.0).astype(bf16)


def head_sums(values, gather_s):
    high = values.astype(bf16)
    low = (values - high.astype(f32)).astype(bf16)
    rows = values.shape[0]
    both = nn(jnp.concatenate([high, low], axis=0), gather_s[...])
    return both[:rows] + both[rows:]


def fill_masks(mask_s, bound, count):
    rows = mask_s.shape[1]
    pos = iota((rows, LANE), 0)
    for lag in range(1, KW):
        anchor = pos - lag
        dropped = (anchor < 0) | ((anchor < bound) & (bound <= pos)) | (pos >= count)
        mask_s[lag - 1] = jnp.where(dropped, 0.0, 1.0)


def conv_phase(proj_s, par, mask_s, conv_s, pre_s, count):
    def body(index):
        src = pl.ds(pl.multiple_of(DH + index * LANE, LANE), LANE)
        dst = tile_at(index, LANE)
        taps = par[0:8, dst]
        for at in range(0, count, 64):
            pre = taps[4:5] + taps[3:4] * proj_s[HEAD_ROWS + at : HEAD_ROWS + at + 64, src]
            for lag in range(1, KW):
                begin = HEAD_ROWS + at - lag
                part = proj_s[begin : begin + 64, src] * mask_s[lag - 1, at : at + 64]
                pre = pre + taps[3 - lag : 4 - lag] * part
            if pre_s is not None:
                pre_s[at : at + 64, dst] = pre
            conv_s[at : at + 64, dst] = pre * sigmoid(pre)

    loop(CH // LANE, body)


def step_phase(proj_s, hp, dt_s, rate_s, cs_s, cst_s, count):
    span = count // 2
    lanes = iota((count, LANE), 1)
    raw = proj_s[HEAD_ROWS : HEAD_ROWS + count, DH + CH : CP] + hp[0:1, :]
    step = jnp.where(lanes < HL, softplus(raw), 0.0)
    rate = -step * hp[1:2, :]
    dt_s[...] = step
    rate_s[...] = rate
    lower = jnp.where(iota((span, span), 0) >= iota((span, span), 1), 1.0, 0.0).astype(bf16)
    for block in range(2):
        rows = slice(block * span, (block + 1) * span)
        triple = jnp.concatenate(split3(rate[rows]), axis=1)
        sums = nn(lower, triple)
        total = sums[:, :LANE] + sums[:, LANE : 2 * LANE] + sums[:, 2 * LANE :]
        cs_s[rows] = total
        cst_s[block] = jnp.transpose(total)


def scaled_inputs(conv_s, dt_s, spread_s, xdt_s, xlo_s, count):
    def body(index):
        rows = tile_at(index, RC * 4)
        scale = nn(pack3(dt_s[rows]), spread_s[...])
        v = conv_s[rows, :DH] * scale
        xdt_s[rows] = v.astype(bf16)
        xlo_s[rows] = (v - v.astype(bf16).astype(f32)).astype(bf16)

    loop(count // (RC * 4), body)


def tail_weight(cs_s, bound, span):
    total = cs_s[0:span]
    pos = iota((span, LANE), 0)
    cut = (pos < bound) & (bound <= span - 1)
    lanes = iota((span, LANE), 1)
    keep = jnp.logical_not(cut) & (lanes < HL)
    return jnp.where(keep, jnp.exp(total[span - 1 : span] - total), 0.0)


def carry_weight(cs_s, bound, span):
    total = cs_s[span : 2 * span]
    pos = iota((span, LANE), 0) + span
    fresh = (span <= bound) & (bound <= pos)
    lanes = iota((span, LANE), 1)
    keep = jnp.logical_not(fresh) & (lanes < HL)
    return jnp.where(keep, jnp.exp(total), 0.0)


def inside_mask(block, bound, span, flipped):
    shape = (span, span)
    later = iota(shape, 1 if flipped else 0) + block * span
    early = iota(shape, 0 if flipped else 1) + block * span
    keep = (later >= early) & jnp.logical_not((early < bound) & (bound <= later))
    return jnp.where(keep, 1.0, 0.0)


def split2(values):
    high = values.astype(bf16)
    return high, (values - high.astype(f32)).astype(bf16)


def nt3(left, right):
    left_high, left_low = split2(left)
    right_high, right_low = split2(right)
    return nt(
        jnp.concatenate([left_high, left_low, left_high], axis=1),
        jnp.concatenate([right_high, right_high, right_low], axis=1),
    )


def nn3(left, right):
    left_high, left_low = split2(left)
    right_high, right_low = split2(right)
    return nn(
        jnp.concatenate([left_high, left_low, left_high], axis=1),
        jnp.concatenate([right_high, right_high, right_low], axis=0),
    )


def mix_tokens(first, second, high, low):
    rows = first.shape[0]
    first_high, first_low = split2(first)
    second_high, second_low = split2(second)
    stacked = jnp.concatenate([first_high, second_high, first_low, second_low], axis=0)
    both = nn(stacked, jnp.concatenate([high, low], axis=1))
    left, right = both[:, :LANE], both[:, LANE:]
    total = left[: 2 * rows] + right[: 2 * rows] + left[2 * rows :]
    keep = iota((rows, LANE), 1) < HDIM
    return jnp.where(keep, total[:rows], total[rows:])


def copies(pairs, sems, base):
    return [
        pltpu.make_async_copy(src, dst, sems.at[base + at]) for at, (src, dst) in enumerate(pairs)
    ]


def load_outer(layer, sec, wo_a, wo_b, wo_s, sem):
    held = pltpu.make_async_copy(wo_a, wo_s, sem)
    given = pltpu.make_async_copy(wo_b, wo_s, sem)

    @pl.when(sec == layer)
    def _():
        held.start()

    @pl.when(sec != layer)
    def _():
        given.start()

    return held


def load_weights(layer, sec, grp, w_a, w_b, w_x, w_y, w_s, sems):
    width = w_a.shape[1]
    part = w_x.shape[0]
    mine = pl.ds(pl.multiple_of(grp * width, width), width)
    other = pl.ds(pl.multiple_of((1 - grp) * width, width), width)
    first = pl.multiple_of(grp * DH, DH)
    steps = pl.multiple_of(DI + CONVC + grp * HL, HL)
    places = [
        (pl.ds(first, DH), pl.ds(0, DH)),
        (pl.ds(DI + first, DH), pl.ds(DH, DH)),
        (pl.ds(2 * DI, 2 * NS), pl.ds(2 * DH, 2 * NS)),
        (pl.ds(steps, HL), pl.ds(DH + CH, HL)),
    ]
    w_s[DH + CH + HL : CP, mine] = jnp.zeros((LANE - HL, width), bf16)

    def pieces(block):
        return copies([(block.at[src], w_s.at[dst, mine]) for src, dst in places], sems, 0)

    held, given = pieces(w_a), pieces(w_b)

    @pl.when(sec == layer)
    def _():
        for copy in held:
            copy.start()

    @pl.when(sec != layer)
    def _():
        for copy in given:
            copy.start()

    at_x = pl.ds(pl.multiple_of(sec * part, part), part)
    at_y = pl.ds(pl.multiple_of((1 - sec) * part, part), part)
    far = copies([(w_x, w_s.at[at_x, other]), (w_y, w_s.at[at_y, other])], sems, 5)
    for copy in far:
        copy.start()
    return held + far


def column_of(stat_ref, hold_s):
    hold_s[...] = jnp.zeros_like(hold_s)
    hold_s[0:8] = stat_ref[...]
    return jnp.transpose(hold_s[...])


def forward_kernel(layer, *refs):
    (scal, par, hp, w_a, w_b, w_x, w_y, wo_a, wo_b) = refs[:9]
    if layer == 0:
        in_own, in_far = refs[9:11]
        rest = refs[11:]
    else:
        u_prev, p_own, p_far, in_own, in_far = refs[9:14]
        rest = refs[14:]
    (u_out, proj_out, ys_out, st_out, mix_out, sum_out, stat_out) = rest[:7]
    (w_s, wo_s, u_s, n_s, proj_s, conv_s, mask_s, dt_s, rate_s, cs_s, cst_s, xdt_s,
     y_s, mix_s, st_s, pp_s, g_s, spread_s, stat_s, hold_s, in_s, xlo_s, sems) = rest[7:]
    sec, grp, bound = scal[0], scal[1], scal[2]
    count = u_s.shape[0]
    span = count // 2
    piece = count // 2
    place_own = pl.ds(pl.multiple_of(grp * piece, piece), piece)
    place_far = pl.ds(pl.multiple_of((1 - grp) * piece, piece), piece)
    token_target = u_s if layer == 0 else in_s
    token_in = copies(
        [(in_own, token_target.at[place_own]), (in_far, token_target.at[place_far])], sems, 8
    )
    if layer == 0:
        for copy in token_in:
            copy.start()
    else:
        more = copies([(u_prev, u_s), (p_own, pp_s.at[0]), (p_far, pp_s.at[1])], sems, 10)
        for copy in more:
            copy.start()
    w_in = load_weights(layer, sec, grp, w_a, w_b, w_x, w_y, w_s, sems)
    if layer == 1:
        for copy in token_in:
            copy.start()
        wo_in = load_outer(layer, sec, wo_a, wo_b, wo_s, sems.at[4])
    fill_masks(mask_s, bound, count)
    fill_spread(spread_s, HDIM)
    proj_s[0:HEAD_ROWS] = jnp.zeros((HEAD_ROWS, CP), f32)
    gain_in = par[6:7, :DM]
    if layer == 0:
        for copy in token_in:
            copy.wait()
    else:
        for copy in more:
            copy.wait()

    def norm_rows(index):
        rows = tile_at(index, RC)
        values = u_s[rows].astype(f32)
        if layer == 1:
            total = pp_s[0, rows] + pp_s[1, rows]
            pp_s[0, rows] = total
            low = (values + total).astype(bf16)
            u_s[rows] = low
            values = low.astype(f32)
        scale = lax.rsqrt(jnp.mean(values * values, axis=-1, keepdims=True) + EPS)
        n_s[rows] = (values * scale * gain_in).astype(bf16)

    loop(count // RC, norm_rows)
    out_sum = None
    if layer == 1:
        out_sum = pltpu.make_async_copy(pp_s.at[0], sum_out, sems.at[18])
        out_sum.start()
    out_u = pltpu.make_async_copy(u_s, u_out, sems.at[13])
    out_u.start()
    for copy in w_in:
        copy.wait()

    body_rows = slice(HEAD_ROWS, HEAD_ROWS + count)

    def project(index):
        lane = tile_at(index, TILE)
        proj_s[body_rows, lane] = nt(n_s[...], w_s[lane, :])

    loop(CP // TILE, project)
    proj_s[body_rows, CP - LANE : CP] = nt(n_s[...], w_s[CP - LANE : CP, :])
    out_proj = pltpu.make_async_copy(proj_s, proj_out, sems.at[14])
    out_proj.start()

    conv_phase(proj_s, par, mask_s, conv_s, None, count)
    step_phase(proj_s, hp, dt_s, rate_s, cs_s, cst_s, count)
    scaled_inputs(conv_s, dt_s, spread_s, xdt_s, xlo_s, count)

    skip = par[7:8, :DH]
    gain_out = par[5:6, :DH]
    lanes = iota((RC, LANE), 1)

    def mix_rows(index):
        rows = tile_at(index, RC)
        shifted_rows = pl.ds(pl.multiple_of(HEAD_ROWS + index * RC, HEAD_ROWS), RC)
        gate = proj_s[shifted_rows, :DH]
        value = y_s[rows] + skip * conv_s[rows, :DH]
        y_s[rows] = value
        mixed = value * (gate * sigmoid(gate))
        conv_s[rows, :DH] = mixed
        if layer == 1:
            mix_s[rows] = (mixed * gain_out).astype(bf16)
        square = jnp.sum(mixed * mixed, axis=-1, keepdims=True)
        stat_s[rows] = jnp.where(lanes == 0, square, 0.0)

    flushed = []
    for block in range(2):
        rows = slice(block * span, (block + 1) * span)
        low_b = conv_s[rows, DH : DH + NS].astype(bf16)
        low_c = conv_s[rows, DH + NS : CH].astype(bf16)
        g_s[...] = nt3(conv_s[rows, DH + NS : CH], conv_s[rows, DH : DH + NS]) * inside_mask(block, bound, span, False)

        def pair(index):
            lane = tile_at(index, LANE)
            near = xdt_s[rows, lane]
            near_low = xlo_s[rows, lane]
            turned_cs = pltpu.roll(cs_s[rows], lax.rem(LANE - 2 * index, LANE), 1)
            for at in range(0, span, LANE):
                size = at + LANE
                here = slice(block * span + at, block * span + at + LANE)
                mixings = []
                for side in range(2):
                    head = 2 * index + side
                    col = jnp.broadcast_to(turned_cs[at : at + LANE, side : side + 1], (LANE, LANE))
                    line = cst_s[block, pl.ds(head, 1), :][:, :size]
                    wide = jnp.concatenate([col] * (size // LANE), axis=1)
                    decay = jnp.exp(jnp.minimum(wide - line, 0.0))
                    mixings.append(decay * g_s[at : at + LANE, :size])
                y_s[here, lane] = mix_tokens(*mixings, near[:size], near_low[:size])

        loop(HL // 2, pair)
        if block == 0:
            weight = pack3(tail_weight(cs_s, bound, span))
            turned = jnp.transpose(conv_s[rows, DH : DH + NS])

            def state_tile(index):
                lane = tile_at(index, TILE)
                scaled = (xdt_s[rows, lane].astype(f32) + xlo_s[rows, lane].astype(f32)) * nn(weight, spread_s[:, lane])
                st_s[:, lane] = nn3(turned, scaled)

            loop(DH // TILE, state_tile)
        else:
            weight = pack3(carry_weight(cs_s, bound, span))

            def carry_tile(index):
                lane = tile_at(index, TILE)
                carried = nn3(conv_s[rows, DH + NS : CH], st_s[:, lane])
                y_s[rows, lane] += carried * nn(weight, spread_s[:, lane])

            loop(DH // TILE, carry_tile)
        first_tile = block * (span // RC)
        loop(span // RC, lambda index: mix_rows(first_tile + index))
        flushed += copies(
            [
                (y_s.at[rows], ys_out.at[rows]),
                (conv_s.at[rows, pl.ds(0, DH)], mix_out.at[rows]),
            ],
            sems,
            16 if block == 0 else 20,
        )
        for copy in flushed[-2:]:
            copy.start()
    out_st = pltpu.make_async_copy(st_s, st_out, sems.at[15])
    out_st.start()

    if layer == 1:
        wo_in.wait()
        for copy in token_in:
            copy.wait()

        def out_tile(index):
            lane = tile_at(index, TILE)
            partial = nn(mix_s[...], wo_s[:, lane])
            dots = jnp.sum(partial * in_s[:, lane].astype(f32), axis=-1, keepdims=True)
            stat_s[...] += jnp.where(iota((count, LANE), 1) == 1, dots, 0.0)

        loop(DM // TILE, out_tile)
    stat_out[...] = jnp.transpose(stat_s[...])[0:8]
    for copy in (out_u, out_proj, out_st, *flushed):
        copy.wait()
    if layer == 1:
        out_sum.wait()


def backward_kernel(layer, *refs):
    (scal, par, hp, w_a, w_b, w_x, w_y, wo_a, wo_b) = refs[:9]
    (u_in, proj_in, ys_in, st_in, stat_own, stat_far, in_own, in_far) = refs[9:17]
    if layer == 1:
        rest = refs[17:]
    else:
        p_sum, up_in, dn_own, dn_far, par_up = refs[17:22]
        rest = refs[22:]
    (n_out, dp_out, gated_out, g_out, dn_out, small_out) = rest[:6]
    (w_s, wo_s, u_s, n_s, proj_s, conv_s, pre_s, mask_s, dt_s, rate_s, cs_s, cst_s, grad_cs_s, xdt_s,
     y_s, st_s, ad_s, pp_s, dn_s, g_s, up_s, gg_s, dys_s, dx_s, dpre_s, dp_s, gm_s, dg_s,
     spread_s, gather_s, stat_s, hold_s, xlo_s, dlo_s, sems) = rest[6:]
    sec, grp, bound = scal[0], scal[1], scal[2]
    count = u_s.shape[0]
    span = count // 2
    piece = count // 2
    place_own = pl.ds(pl.multiple_of(grp * piece, piece), piece)
    place_far = pl.ds(pl.multiple_of((1 - grp) * piece, piece), piece)
    token_in = copies([(in_own, g_s.at[place_own]), (in_far, g_s.at[place_far])], sems, 8)
    saved_in = copies([(u_in, u_s), (proj_in, proj_s), (ys_in, y_s), (st_in, st_s)], sems, 10)
    for copy in token_in:
        copy.start()
    if layer == 0:
        more = copies(
            [
                (dn_own, dn_s.at[0]),
                (dn_far, dn_s.at[1]),
                (up_in, up_s),
                (p_sum, pp_s),
            ],
            sems,
            14,
        )
        for copy in more:
            copy.start()
    wo_in = load_outer(layer, sec, wo_a, wo_b, wo_s, sems.at[4])
    for copy in saved_in[1:]:
        copy.start()
    fill_masks(mask_s, bound, count)
    fill_spread(spread_s, HDIM)
    fill_gather(gather_s)
    stats = column_of(stat_own, hold_s) + column_of(stat_far, hold_s)
    stat_s[...] = stats
    for copy in token_in:
        copy.wait()
    lane_rc = iota((RC, LANE), 1)
    if layer == 0:
        for copy in more:
            copy.wait()
        gain_up = par_up[6:7, :DM]

        def upstream_rows(index):
            rows = tile_at(index, RC)
            values = up_s[rows].astype(f32)
            scale = lax.rsqrt(jnp.mean(values * values, axis=-1, keepdims=True) + EPS)
            arrived = (dn_s[0, rows].astype(f32) + dn_s[1, rows].astype(f32)) * gain_up
            inner = jnp.mean(arrived * values, axis=-1, keepdims=True)
            total = g_s[rows].astype(f32) + scale * arrived - values * (scale * scale * scale * inner)
            low = total.astype(bf16)
            g_s[rows] = low
            dots = jnp.sum(low.astype(f32) * pp_s[rows], axis=-1, keepdims=True)
            stat_s[rows] = jnp.where(lane_rc == 1, dots, stat_s[rows])

        loop(count // RC, upstream_rows)
    out_g = pltpu.make_async_copy(g_s, g_out, sems.at[19])
    out_g.start()
    wo_in.wait()

    def gated_tile(index):
        lane = tile_at(index, TILE)
        gg_s[:, lane] = nt(g_s[...], wo_s[lane, :])

    loop(DH // TILE, gated_tile)
    for copy in saved_in[1:]:
        copy.wait()
    w_in = load_weights(layer, sec, grp, w_a, w_b, w_x, w_y, w_s, sems)
    saved_in[0].start()

    conv_phase(proj_s, par, mask_s, conv_s, pre_s, count)
    step_phase(proj_s, hp, dt_s, rate_s, cs_s, cst_s, count)
    scaled_inputs(conv_s, dt_s, spread_s, xdt_s, xlo_s, count)

    skip = par[7:8, :DH]
    gain_out = par[5:6, :DH]
    gain_in = par[6:7, :DM]

    def fold(values):
        return jnp.sum(values.reshape(-1, 8, values.shape[-1]), axis=0)

    def mix_rows(index, carry):
        gain_sum, skip_sum = carry
        rows = tile_at(index, RC)
        shifted_rows = pl.ds(pl.multiple_of(HEAD_ROWS + index * RC, HEAD_ROWS), RC)
        scale = lax.rsqrt(stat_s[rows, 0:1] * (1.0 / DI) + EPS)
        inner = stat_s[rows, 1:2] * (scale * scale * (1.0 / DI))
        if layer == 1:
            inner = inner * scale
        gate = proj_s[shifted_rows, :DH]
        gate_sig = sigmoid(gate)
        gate_act = gate * gate_sig
        value = y_s[rows]
        grad = gg_s[rows]
        mixed = value * gate_act
        scaled = mixed * scale
        dmixed = grad * gain_out * scale - mixed * inner
        mixed_low = (scaled * gain_out).astype(bf16)
        gated_s[rows] = mixed_low
        dys = dmixed * gate_act
        dgate = dmixed * value * (gate_sig + gate_act * (1.0 - gate_sig))
        dp_s[rows, :DH] = dgate.astype(bf16)
        inputs = conv_s[rows, :DH]
        gg_s[rows] = dys
        low = dys.astype(bf16)
        dys_s[rows] = low
        dlo_s[rows] = (dys - low.astype(f32)).astype(bf16)
        y_s[rows] = dys * (value - skip * inputs)
        return (gain_sum + fold(grad * scaled), skip_sum + fold(dys * inputs))

    gated_s = n_s
    zero = jnp.zeros((8, DH), f32)
    gain_sum, skip_sum = lax.fori_loop(0, count // RC, mix_rows, (zero, zero))
    small_out[...] = jnp.zeros_like(small_out)
    small_out[5:6, :DH] = jnp.sum(gain_sum, axis=0, keepdims=True)
    small_out[7:8, :DH] = jnp.sum(skip_sum, axis=0, keepdims=True)
    out_gated = pltpu.make_async_copy(n_s, gated_out, sems.at[20])
    out_gated.start()

    lane_left = iota((span, LANE), 1) < HDIM
    for block in (1, 0):
        rows = slice(block * span, (block + 1) * span)
        low_b = conv_s[rows, DH : DH + NS].astype(bf16)
        low_c = conv_s[rows, DH + NS : CH].astype(bf16)
        keep = inside_mask(block, bound, span, True)
        gm_s[...] = nt3(conv_s[rows, DH : DH + NS], conv_s[rows, DH + NS : CH]) * keep
        dg_s[...] = jnp.zeros_like(dg_s)

        def pair(index):
            lane = tile_at(index, LANE)
            near = xdt_s[rows, lane]
            far = dys_s[rows, lane]
            far_low = dlo_s[rows, lane]
            turned_cs = pltpu.roll(cs_s[rows], lax.rem(LANE - 2 * index, LANE), 1)
            for at in range(0, span, LANE):
                size = span - at
                here = slice(block * span + at, block * span + at + LANE)
                part = near[at : at + LANE]
                mixings, decays, parts = [], [], []
                for side in range(2):
                    head = 2 * index + side
                    col = jnp.broadcast_to(turned_cs[at : at + LANE, side : side + 1], (LANE, LANE))
                    line = cst_s[block, pl.ds(head, 1), :][:, at:]
                    wide = jnp.concatenate([col] * (size // LANE), axis=1)
                    decay = jnp.exp(jnp.minimum(line - wide, 0.0))
                    decays.append(decay)
                    mixings.append(decay * gm_s[at : at + LANE, at:])
                    mine = lane_left[:LANE] if side == 0 else jnp.logical_not(lane_left[:LANE])
                    parts.append(jnp.where(mine, part.astype(f32), 0.0).astype(bf16))
                dx_s[here, lane] = mix_tokens(*mixings, far[at:], far_low[at:])
                pairs = nt(jnp.concatenate(parts, axis=0), far[at:])
                dg_s[at : at + LANE, at:] += pairs[:LANE] * decays[0] + pairs[LANE:] * decays[1]

        loop(HL // 2, pair)
        grad_g = dg_s[...] * keep
        dpre_s[rows, DH : DH + NS] = nn(grad_g.astype(bf16), low_c)
        dpre_s[rows, DH + NS : CH] = nn(jnp.transpose(grad_g).astype(bf16), low_b)
        if block == 1:
            weight = pack3(carry_weight(cs_s, bound, span))
            turned_c = jnp.transpose(conv_s[rows, DH + NS : CH])

            def carry_tile(index):
                lane = tile_at(index, TILE)
                scaled = (dys_s[rows, lane].astype(f32) + dlo_s[rows, lane].astype(f32)) * nn(weight, spread_s[:, lane])
                ad_s[:, lane] = nn3(turned_c, scaled)
                dpre_s[rows, DH + NS : CH] += nt3(scaled, st_s[:, lane])

            loop(DH // TILE, carry_tile)
        else:
            weight = pack3(tail_weight(cs_s, bound, span))

            def state_tile(index):
                lane = tile_at(index, TILE)
                scale = nn(weight, spread_s[:, lane])
                low_a = ad_s[:, lane]
                inputs = xdt_s[rows, lane].astype(f32) + xlo_s[rows, lane].astype(f32)
                extra = nn3(conv_s[rows, DH : DH + NS], low_a) * scale
                dx_s[rows, lane] += extra
                both = inputs * scale
                pre_tail = jnp.sum(fold(inputs * extra), axis=0, keepdims=True)
                dpre_s[count : count + 1, lane] = pre_tail
                dpre_s[rows, DH : DH + NS] += nt3(both, low_a)

            loop(DH // TILE, state_tile)

    def head_rows(index):
        chunk = RC * 4
        rows = tile_at(index, chunk)
        steps = dt_s[rows]
        scale = nn(pack3(steps), spread_s[...])
        grad = dx_s[rows]
        sums = head_sums(jnp.concatenate([conv_s[rows, :DH] * grad, y_s[rows]], axis=0), gather_s)
        per_step = sums[:chunk]
        stat_s[rows] = per_step
        grad_cs_s[rows] = sums[chunk:] - steps * per_step
        dpre_s[rows, :DH] = gg_s[rows] * skip + grad * scale

    loop(count // (RC * 4), head_rows)
    tail = jnp.broadcast_to(dpre_s[count : count + 1, :DH], (8, DH))
    tail_heads = head_sums(tail, gather_s)[0:1]
    last = iota((span, LANE), 0) == span - 1
    upper = jnp.where(iota((span, span), 0) <= iota((span, span), 1), 1.0, 0.0).astype(bf16)
    bias_sum = jnp.zeros((1, LANE), f32)
    decay_sum = jnp.zeros((1, LANE), f32)
    for block in range(2):
        rows = slice(block * span, (block + 1) * span)
        raw = proj_s[HEAD_ROWS + block * span : HEAD_ROWS + (block + 1) * span, DH + CH : CP]
        grad_cs = grad_cs_s[rows]
        if block == 0:
            grad_cs = grad_cs + jnp.where(last, tail_heads, 0.0)
        sums = nn(upper, jnp.concatenate(split3(grad_cs), axis=1))
        grad_rate = sums[:, :LANE] + sums[:, LANE : 2 * LANE] + sums[:, 2 * LANE :]
        grad_step = stat_s[rows] - grad_rate * hp[1:2, :]
        lanes = iota((span, LANE), 1)
        grad_raw = jnp.where(lanes < HL, grad_step * sigmoid(raw + hp[0:1, :]), 0.0)
        dp_s[rows, DH + CH : CP] = grad_raw.astype(bf16)
        bias_sum = bias_sum + jnp.sum(grad_raw, axis=0, keepdims=True)
        decay_sum = decay_sum + jnp.sum(grad_rate * rate_s[rows], axis=0, keepdims=True)
    small_out[8:9, :LANE] = bias_sum
    small_out[9:10, :LANE] = decay_sum

    dpre_s[count : count + 8] = jnp.zeros((8, CH), f32)

    def conv_back(index):
        src = pl.ds(pl.multiple_of(DH + index * LANE, LANE), LANE)
        dst = tile_at(index, LANE)
        taps = par[0:8, dst]
        sums = [jnp.zeros((8, LANE), f32) for _ in range(KW + 1)]
        for at in range(0, count, 64):
            pre = pre_s[at : at + 64, dst]
            sig = sigmoid(pre)
            grad = dpre_s[at : at + 64, dst] * (sig + pre * sig * (1.0 - sig))
            dpre_s[at : at + 64, dst] = grad
            sums[4] = sums[4] + fold(grad)
            for lag in range(KW):
                begin = HEAD_ROWS + at - lag
                part = proj_s[begin : begin + 64, src]
                if lag:
                    part = part * mask_s[lag - 1, at : at + 64]
                sums[3 - lag] = sums[3 - lag] + fold(grad * part)
        for at in range(0, count, 64):
            total = taps[3:4] * dpre_s[at : at + 64, dst]
            for lag in range(1, KW):
                begin = at + lag
                part = dpre_s[begin : begin + 64, dst] * mask_s[lag - 1, begin : begin + 64]
                total = total + taps[3 - lag : 4 - lag] * part
            dp_s[at : at + 64, src] = total.astype(bf16)
        for at in range(KW + 1):
            small_out[at : at + 1, dst] = jnp.sum(sums[at], axis=0, keepdims=True)

    loop(CH // LANE, conv_back)
    out_dp = pltpu.make_async_copy(dp_s, dp_out, sems.at[21])
    out_dp.start()
    for copy in w_in:
        copy.wait()
    saved_in[0].wait()

    def normed_tile(index):
        lane = tile_at(index, TILE)
        gg_s[:, lane] = nn(dp_s[...], w_s[:, lane])

    loop(DM // TILE, normed_tile)
    out_gated.wait()

    def norm_rows(index, gain_sum):
        rows = tile_at(index, RC)
        values = u_s[rows].astype(f32)
        scale = lax.rsqrt(jnp.mean(values * values, axis=-1, keepdims=True) + EPS)
        unit = values * scale
        n_s[rows] = (unit * gain_in).astype(bf16)
        grad = gg_s[rows]
        dys_s[rows] = grad.astype(bf16)
        return gain_sum + fold(grad * unit)

    gain_total = lax.fori_loop(0, count // RC, norm_rows, jnp.zeros((8, DM), f32))
    small_out[6:7, :DM] = jnp.sum(gain_total, axis=0, keepdims=True)
    out_n = pltpu.make_async_copy(n_s, n_out, sems.at[22])
    out_dn = pltpu.make_async_copy(dys_s, dn_out, sems.at[23])
    out_n.start()
    out_dn.start()
    for copy in (out_g, out_dp, out_n, out_dn):
        copy.wait()


def project_kernel(layer, scal, par, wo_a, wo_b, stat_own, stat_far, mix_in, p_out, wo_s, low_s, stat_s, hold_s, sems):
    sec = scal[0]
    count = mix_in.shape[0]
    from_a = pltpu.make_async_copy(wo_a, wo_s, sems.at[0])
    from_b = pltpu.make_async_copy(wo_b, wo_s, sems.at[0])

    @pl.when(sec == layer)
    def _():
        from_a.start()

    @pl.when(sec != layer)
    def _():
        from_b.start()

    stats = column_of(stat_own, hold_s) + column_of(stat_far, hold_s)
    stat_s[...] = lax.rsqrt(stats * (1.0 / DI) + EPS)
    gain_out = par[5:6, :DH]

    def rows_of(index):
        rows = tile_at(index, RC)
        low_s[rows] = (mix_in[rows] * stat_s[rows, 0:1] * gain_out).astype(bf16)

    loop(count // RC, rows_of)
    from_a.wait()

    def out_tile(index):
        lane = tile_at(index, TILE)
        p_out[:, lane] = nn(low_s[...], wo_s[:, lane]).astype(p_out.dtype)

    loop(DM // TILE, out_tile)


ANY = pl.BlockSpec(memory_space=pl.ANY)
VM = pl.BlockSpec(memory_space=pltpu.VMEM)
SM = pl.BlockSpec(memory_space=pltpu.SMEM)


def call(kernel, args, specs, outs, out_specs, scratch, name, flops):
    return pl.pallas_call(
        kernel,
        in_specs=specs,
        out_specs=out_specs,
        out_shape=[jax.ShapeDtypeStruct(shape, dtype) for shape, dtype in outs],
        scratch_shapes=scratch,
        compiler_params=pltpu.CompilerParams(vmem_limit_bytes=VMEM_BYTES),
        cost_estimate=pl.CostEstimate(
            flops=flops, bytes_accessed=20_000_000, transcendentals=4_000_000
        ),
        name=name,
    )(*args)


def vm(shape, dtype):
    return pltpu.VMEM(shape, dtype)


def run_forward(layer, scal, par, hp, weights, tokens, saved):
    count = 2 * tokens[0].shape[0]
    span = count // 2
    args = [scal, par, hp, *weights]
    specs = [SM, VM, VM] + [ANY] * 6
    if layer == 1:
        args += saved
        specs += [ANY, ANY, ANY]
    args += tokens
    specs += [ANY, ANY]
    outs = [
        ((count, DM), bf16),
        ((count + HEAD_ROWS, CP), f32),
        ((count, DH), f32),
        ((NS, DH), f32),
        ((count, DH), f32),
        ((count, DM) if layer == 1 else (8, LANE), f32),
        ((8, count), f32),
    ]
    out_specs = [ANY] * 6 + [VM]
    scratch = [
        vm((CP, DM), bf16),
        vm((DH, DM), bf16),
        vm((count, DM), bf16),
        vm((count, DM), bf16),
        vm((count + HEAD_ROWS, CP), f32),
        vm((count, CH), f32),
        vm((KW - 1, count + 8, LANE), f32),
        vm((count, LANE), f32),
        vm((count, LANE), f32),
        vm((count, LANE), f32),
        vm((2, LANE, span), f32),
        vm((count, DH), bf16),
        vm((count, DH), f32),
        vm((count, DH), bf16),
        vm((NS, DH), f32),
        vm((2, count, DM), f32),
        vm((span, span), f32),
        vm((LANE, DH), bf16),
        vm((count, LANE), f32),
        vm((LANE, count), f32),
        vm((count, DM), bf16),
        vm((count, DH), bf16),
        pltpu.SemaphoreType.DMA((22,)),
    ]
    return call(
        functools.partial(forward_kernel, layer),
        args,
        specs,
        outs,
        out_specs,
        scratch,
        "forward_%d" % layer,
        35_000_000_000,
    )


def assemble_kernel(scal, *refs):
    got, own = refs[:3], refs[3:6]
    a1, a1_got, came, came_got, b1, b1_got = refs[6:12]
    in_out, out_out, whole_s, outer_s, in_s, out_s, sems = refs[12:]
    sec, grp = scal[0], scal[1]
    half = whole_s.shape[1] // 2
    quart = whole_s.shape[2] // 2
    outer = outer_s.shape[0] // 2
    share = b1.shape[0]

    def first_pairs(blocks, core):
        near, far, wide = blocks
        pairs = []
        for at, block in ((scal[2], near), (1 - scal[2], far)):
            rows = pl.ds(pl.multiple_of(at * half, 16), half)
            pairs.append((block, whole_s.at[core, rows]))
        return pairs + [(wide.at[pl.ds(0, outer)], outer_s.at[pl.ds(core * outer, outer)])]

    def outer_pairs(early, wide, core):
        return [
            (early, outer_s.at[pl.ds(core * outer, share)]),
            (wide.at[pl.ds(outer, share)], outer_s.at[pl.ds(core * outer + share, share)]),
        ]

    def second_pairs(block, moved, core):
        near = pl.ds(pl.multiple_of(grp * quart, quart), quart)
        far = pl.ds(pl.multiple_of((1 - grp) * quart, quart), quart)
        return [
            (block.at[:, near], whole_s.at[core, :, near]),
            (moved, whole_s.at[core, :, far]),
        ]

    def fetch(pairs):
        started = copies(pairs, sems, 0)
        for copy in started:
            copy.start()
        for copy in started:
            copy.wait()

    @pl.when(sec == 0)
    def _():
        fetch(first_pairs(own, 0) + first_pairs(got, 1))

    @pl.when(sec != 0)
    def _():
        fetch(
            second_pairs(a1, came, 1)
            + second_pairs(a1_got, came_got, 0)
            + outer_pairs(b1, own[2], 1)
            + outer_pairs(b1_got, got[2], 0)
        )

    width = in_s.shape[1]
    quarter = width // 2
    step = 64
    started = []

    def send(piece, sem):
        copy = pltpu.make_async_copy(in_s.at[piece], in_out.at[piece], sems.at[sem])
        copy.start()
        started.append(copy)

    def emit(target, source, count, side):
        def body(index):
            at = pl.multiple_of(index * step, step)
            for core in range(2):
                value = whole_s[core, pl.ds(source + at, step), side * quarter : (side + 1) * quarter]
                lane = slice(core * quarter, (core + 1) * quarter)
                in_s[pl.ds(target + at, step), lane] = value.astype(f32)

        loop(count // step, body)

    for at, (target, source, side) in enumerate(
        ((0, 0, 0), (DH, 0, 1), (DI, DH, 0), (DI + DH, DH, 1))
    ):
        emit(target, source, DH, side)
        send(pl.ds(target, DH), 8 + at)
    for core in range(2):
        lane = slice(core * quarter, (core + 1) * quarter)
        left, right = slice(0, quarter), slice(quarter, width)
        shared = slice(2 * DH, 2 * DH + 2 * NS)
        in_s[2 * DI : 2 * DI + 2 * NS, lane] = whole_s[core, shared, left].astype(f32) + whole_s[
            core, shared, right
        ].astype(f32)
        steps = slice(DH + CH, DH + CH + HL)
        in_s[DI + CONVC : DI + CONVC + HL, lane] = whole_s[core, steps, left].astype(f32)
        in_s[DI + CONVC + HL :, lane] = whole_s[core, steps, right].astype(f32)
    send(pl.ds(2 * DI, 2 * NS + HEADS), 12)

    def body(index):
        rows = tile_at(index, step)
        out_s[rows] = outer_s[rows].astype(f32)

    loop(out_s.shape[0] // step, body)
    copy = pltpu.make_async_copy(out_s, out_out, sems.at[13])
    copy.start()
    started.append(copy)
    for copy in started:
        copy.wait()


def run_assemble(scal, got, own, second, columns):
    rows, width = second[0].shape
    outer = (4 * second[-1].shape[0], second[-1].shape[1])
    return call(
        assemble_kernel,
        [scal, *got, *own, *second],
        [SM] + [ANY] * 12,
        [((columns, width), f32), (outer, f32)],
        [ANY, ANY],
        [
            vm((2, rows, width), bf16),
            vm(outer, bf16),
            vm((columns, width), f32),
            vm(outer, f32),
            pltpu.SemaphoreType.DMA((14,)),
        ],
        "assemble",
        6_000_000_000,
    )


def run_project(layer, scal, par, wo_a, wo_b, stat_own, stat_far, mixed):
    count = mixed.shape[0]
    return call(
        functools.partial(project_kernel, layer),
        [scal, par, wo_a, wo_b, stat_own, stat_far, mixed],
        [SM, VM, ANY, ANY, VM, VM, VM],
        [((count, DM), f32)],
        [VM],
        [
            vm((DH, DM), bf16),
            vm((count, DH), bf16),
            vm((count, LANE), f32),
            vm((LANE, count), f32),
            pltpu.SemaphoreType.DMA((1,)),
        ],
        "project_%d" % layer,
        6_000_000_000,
    )[0]


def run_backward(layer, scal, par, hp, weights, saved, tokens, late):
    count = 2 * tokens[0].shape[0]
    span = count // 2
    args = [scal, par, hp, *weights, *saved, *tokens]
    specs = [SM, VM, VM] + [ANY] * 6 + [ANY] * 4 + [VM, VM] + [ANY] * 2
    if layer == 0:
        args += late
        specs += [ANY] * 4 + [VM]
    outs = [
        ((count, DM), bf16),
        ((count, CP), bf16),
        ((count, DH), bf16),
        ((count, DM), bf16),
        ((count, DM), bf16),
        ((16, CH), f32),
    ]
    out_specs = [ANY] * 5 + [VM]
    scratch = [
        vm((CP, DM), bf16),
        vm((DH, DM), bf16),
        vm((count, DM), bf16),
        vm((count, DM), bf16),
        vm((count + HEAD_ROWS, CP), f32),
        vm((count, CH), f32),
        vm((count, CH), f32),
        vm((KW - 1, count + 8, LANE), f32),
        vm((count, LANE), f32),
        vm((count, LANE), f32),
        vm((count, LANE), f32),
        vm((2, LANE, span), f32),
        vm((count, LANE), f32),
        vm((count, DH), bf16),
        vm((count, DH), f32),
        vm((NS, DH), f32),
        vm((NS, DH), f32),
        vm((count, DM), f32),
        vm((2, count, DM), bf16),
        vm((count, DM), bf16),
        vm((count, DM), bf16),
        vm((count, DM), f32),
        vm((count, DM), bf16),
        vm((count, DH), f32),
        vm((count + 8, CH), f32),
        vm((count, CP), bf16),
        vm((span, span), f32),
        vm((span, span), f32),
        vm((LANE, DH), bf16),
        vm((DH, LANE), bf16),
        vm((count, LANE), f32),
        vm((LANE, count), f32),
        vm((count, DH), bf16),
        vm((count, DH), bf16),
        pltpu.SemaphoreType.DMA((24,)),
    ]
    return call(
        functools.partial(backward_kernel, layer),
        args,
        specs,
        outs,
        out_specs,
        scratch,
        "backward_%d" % layer,
        55_000_000_000,
    )


def swap(block, axis):
    return lax.ppermute(block, axis, [(0, 1), (1, 0)])


def flip(block, mask):
    size = lax.axis_size("replica")
    return lax.ppermute(block, "replica", [(at, at ^ mask) for at in range(size)])


def add_low(left, right):
    return (left.astype(f32) + right.astype(f32)).astype(bf16)


def halves(block, which):
    size = block.shape[0] // 2
    keep = lax.dynamic_slice_in_dim(block, which * size, size, 0)
    send = lax.dynamic_slice_in_dim(block, (1 - which) * size, size, 0)
    return keep, send


def stages_of(bits):
    return [(at,) for at in range(bits)]


def scatter_sum(pieces, stages, rep):
    for (bit,) in stages:
        cut = [halves(piece, (rep >> bit) & 1) for piece in pieces]
        sent = flip(sum_low([send for keep, send in cut]), 1 << bit)
        pieces = [sum_low([keep for keep, send in cut]), sent]
    return sum_low(pieces)


def sum_low(pieces):
    total = pieces[0].astype(f32)
    for piece in pieces[1:]:
        total = total + piece.astype(f32)
    return total.astype(bf16)


def collect(block, stage, rep):
    pieces = [block] + [flip(block, away << stage[0]) for away in range(1, 1 << len(stage))]
    for level in range(len(stage)):
        which = (rep >> stage[level]) & 1
        pieces = [
            in_order(pieces[at], pieces[at + 1], which, 0) for at in range(0, len(pieces), 2)
        ]
    return pieces[0]


def in_order(mine, other, which, dim):
    return jnp.where(
        which == 0,
        jnp.concatenate([mine, other], axis=dim),
        jnp.concatenate([other, mine], axis=dim),
    )


def gather_back(block, order, rep):
    for bit in reversed(order):
        block = in_order(block, flip(block, bit), (rep >> bit) & 1, 0)
    return block


def on_device(
    first_layer_input,
    boundary,
    input_gain,
    in_proj,
    conv_weight,
    conv_bias,
    head_params,
    output_gain,
    out_proj,
    cotangent,
):
    sec = lax.axis_index("section")
    grp = lax.axis_index("group")
    rep = lax.axis_index("replica")
    replicas = lax.axis_size("replica")
    bits = replicas.bit_length() - 1
    order_a = stages_of(bits)
    order_b = order_a[1::-1] + order_a[2:]

    bound = lax.dynamic_index_in_dim(boundary[:, 0], sec, 0, keepdims=False)
    scal = jnp.stack([sec, grp, bound]).astype(jnp.int32)
    u_own = lax.dynamic_index_in_dim(first_layer_input[:, 0], sec, 0, keepdims=False)
    u_far = swap(u_own, "group")
    cot_own = lax.dynamic_index_in_dim(cotangent[:, 0], sec, 0, keepdims=False)

    block = jnp.swapaxes(in_proj, 1, 2)[0]
    far_grp = 1 - grp
    other = jnp.concatenate(
        [
            lax.dynamic_slice_in_dim(block, far_grp * DH, DH, 0),
            lax.dynamic_slice_in_dim(block, DI + far_grp * DH, DH, 0),
            block[2 * DI : 2 * DI + 2 * NS],
            lax.dynamic_slice_in_dim(block, DI + CONVC + far_grp * HL, HL, 0),
            jnp.zeros((LANE - HL, block.shape[1]), bf16),
        ],
        axis=0,
    )
    keep, give = halves(other, sec)
    got = swap(give, "section")
    first_x = swap(jnp.where(sec == 0, keep, got), "group")
    keep, got, cot_own, first_x = lax.optimization_barrier((keep, got, cot_own, first_x))
    second_x = swap(jnp.where(sec == 1, keep, got), "group")
    cot_far = swap(cot_own, "group")
    w_a, w_b = block, swap(block, "section")
    wo_a = out_proj[0]
    wo_b = swap(wo_a, "section")
    weights = [
        (w_a, w_b, w_x, swap(w_x, "section"), wo_a, wo_b) for w_x in (first_x, second_x)
    ]

    width = conv_bias.shape[1]
    half_in = input_gain.shape[1]

    def row_of(*pieces):
        line = jnp.concatenate(pieces)
        return jnp.pad(line, (0, width - line.shape[0]))[None]

    smalls = jnp.concatenate(
        [
            conv_weight[0].T,
            conv_bias,
            row_of(output_gain[0]),
            row_of(input_gain[0], head_params[0].T.reshape(-1)),
            jnp.zeros((1, width), bf16),
        ],
        axis=0,
    )
    both = in_order(smalls[None], swap(smalls, "section")[None], sec, 0)
    far_both = swap(both, "group")
    both = both.astype(f32)
    full = in_order(both, far_both.astype(f32), grp, 2)
    pars, hps = [], []
    for layer in range(2):
        taps = jnp.concatenate(
            [
                lax.dynamic_slice_in_dim(full[layer, 0:5], grp * DH, DH, 1),
                full[layer, 0:5, DI:],
            ],
            axis=1,
        )
        line = both[layer, 6]
        heads = line[half_in : half_in + 3 * HL].reshape(3, HL)
        gain_in = jnp.concatenate(
            [full[layer, 6, :half_in], full[layer, 6, width : width + half_in]]
        )
        rest = jnp.stack([both[layer, 5, :DH], gain_in, jnp.repeat(heads[2], HDIM)])
        pars.append(jnp.concatenate([taps, jnp.pad(rest, ((0, 0), (0, CH - DH)))], axis=0))
        lines = jnp.stack([heads[0], jnp.exp(heads[1]), heads[2]])
        hps.append(jnp.pad(lines, ((0, 5), (0, LANE - HL))))

    tokens = [u_own, u_far]
    cots = [cot_own, cot_far]
    quarter = half_in // 2

    def own_quarter(normed):
        return jnp.concatenate(
            [
                lax.dynamic_slice_in_dim(normed, at * half_in + sec * quarter, quarter, 1)
                for at in range(2)
            ],
            axis=1,
        )

    def own_channels(gated):
        return lax.dynamic_slice_in_dim(gated, sec * (DH // 2), DH // 2, 1)

    def join_in(normed, dproj):
        far_n, far_p = swap(normed, "section"), swap(dproj, "section")
        return (tn(dproj, own_quarter(normed)) + tn(far_p, own_quarter(far_n))).astype(bf16)

    def join_out(gated, upstream):
        far_g, far_u = swap(gated, "section"), swap(upstream, "section")
        return (tn(own_channels(gated), upstream) + tn(own_channels(far_g), far_u)).astype(bf16)

    def guarded(branch, operand):
        shapes = jax.eval_shape(branch, operand)

        def nothing(operand):
            return jax.tree.map(lambda leaf: jnp.zeros(leaf.shape, leaf.dtype), shapes)

        return lax.cond(bound >= 0, branch, nothing, operand)

    u0, proj0, ys0, st0, mix0, unused_sum, stat0 = guarded(
        lambda tokens: run_forward(0, scal, pars[0], hps[0], weights[0], tokens, None), tokens
    )
    stat0, cot_far = lax.optimization_barrier((stat0, cots[1]))
    cots = [cot_own, cot_far]
    stat0_far = swap(stat0, "group")
    p0 = run_project(0, scal, pars[0], wo_a, wo_b, stat0, stat0_far, mix0)
    p0_far = swap(p0.astype(jnp.float16), "group").astype(f32)
    u1, proj1, ys1, st1, mix1, p_total, stat1 = run_forward(
        1, scal, pars[1], hps[1], weights[1], cots, [u0, p0, p0_far]
    )
    stat1_far = swap(stat1, "group")
    piece = u_own.shape[0]

    def own_rows(block):
        return lax.dynamic_slice_in_dim(block, grp * piece, piece, 0)

    def far_rows(block):
        return lax.dynamic_slice_in_dim(block, (1 - grp) * piece, piece, 0)

    scale1 = lax.rsqrt((stat1 + stat1_far)[0] * (1.0 / DI) + EPS)[:, None]
    gated1 = (mix1 * scale1 * pars[1][5:6, :DH]).astype(bf16)
    b1 = join_out(gated1, in_order(cot_own, cot_far, grp, 0))
    stat1_far, b1 = lax.optimization_barrier((stat1_far, b1))
    share = b1.shape[0] // 2
    b1_late = b1[share:]
    b1 = lax.psum(b1[:share], "replica")

    def second_layer(stat1_far):
        n1, dp1, unused_gated, unused_g, dn1, small1 = run_backward(
            1, scal, pars[1], hps[1], weights[1],
            [u1, proj1, ys1, st1, stat1, stat1_far], cots, None,
        )
        dn1_far = swap(dn1, "group")
        dn1_far, a1 = lax.optimization_barrier((dn1_far, join_in(n1, dp1)))
        return dn1, dn1_far, a1, small1

    dn1, dn1_far, a1, small1 = guarded(second_layer, stat1_far)
    a1, b1 = lax.optimization_barrier((a1, b1))
    a1 = lax.psum(a1, "replica")

    def to_sections(first, second):
        held = jnp.where(sec == 0, first, second)
        given = swap(jnp.where(sec == 0, second, first), "section")
        return in_order(held[None], given[None], sec, 0)

    def swap_rows(part_a):
        stay = lax.dynamic_slice_in_dim(part_a, grp * quarter, quarter, 1)
        leave = lax.dynamic_slice_in_dim(part_a, far_grp * quarter, quarter, 1)
        return in_order(stay, swap(leave, "group"), grp, 1)

    def to_owner(block, layer):
        return lax.ppermute(block, "section", [(1 - layer, layer)])

    def gather_back(block, stages):
        for stage in reversed(stages):
            block = collect(block, stage, rep)
        return block

    def first_layer(dn1_far):
        n0, dp0, gated0, g0, dn0, small0 = run_backward(
            0, scal, pars[0], hps[0], weights[0],
            [u0, proj0, ys0, st0, stat0, stat0_far], cots,
            [p_total, u1, dn1, dn1_far, pars[1]],
        )
        a0 = join_in(n0, dp0)
        b0 = jnp.concatenate([join_out(gated0, g0), b1_late], axis=0)
        cut = [halves(block, (rep >> stages[0][0]) & 1) for block, stages in ((a0, order_a), (b0, order_b))]
        cut, dn0, g0, small0, late_gated, late_small = lax.optimization_barrier(
            (cut, dn0, g0, small0, gated1, small1)
        )
        sent = [
            flip(send, 1 << stages[0][0])
            for (keep, send), stages in zip(cut, (order_a, order_b))
        ]
        dn0_far = swap(far_rows(dn0), "group")

        p1 = nn(late_gated, jnp.where(sec == 1, wo_a, wo_b))
        p1_far = swap(far_rows(p1).astype(bf16), "group")
        small = jnp.stack([small0, late_small])
        small = small + swap(small, "section")
        far = swap(small, "group")
        shared = small + far
        own_x = jnp.concatenate([small[:, 0:5, :DH], far[:, 0:5, :LANE]], axis=2)
        own_y = jnp.concatenate([small[:, 0:5, LANE:DH], shared[:, 0:5, DH:]], axis=2)
        conv_part = jnp.where(grp == 0, own_x, own_y)
        gain_in = lax.dynamic_slice_in_dim(shared[:, 6, :DM], grp * half_in, half_in, 1)
        skip = small[:, 7, :DH].reshape(2, HL, HDIM).sum(axis=2)
        line = jnp.concatenate([gain_in, small[:, 8, :HL], small[:, 9, :HL], skip], axis=1)
        packed = jnp.concatenate(
            [
                conv_part,
                jnp.pad(small[:, 5:6, :DH], ((0, 0), (0, 0), (0, width - DH))),
                jnp.pad(line, ((0, 0), (0, width - line.shape[1])))[:, None],
                jnp.zeros((2, 1, width), f32),
            ],
            axis=1,
        )
        sent, dn0_far, p1_far, packed = lax.optimization_barrier((sent, dn0_far, p1_far, packed))
        state = [[keep, came] for (keep, send), came in zip(cut, sent)]
        values = u_own.astype(f32)
        scale = lax.rsqrt(jnp.mean(values * values, axis=-1, keepdims=True) + EPS)
        arrived = (own_rows(dn0).astype(f32) + dn0_far.astype(f32)) * pars[0][6:7, :DM]
        inner = jnp.mean(arrived * values, axis=-1, keepdims=True)
        grad1 = own_rows(g0)
        grad0 = (
            grad1.astype(f32) + scale * arrived - values * (scale * scale * scale * inner)
        ).astype(bf16)

        input_grad = to_sections(grad0, grad1)
        out0 = own_rows(u1)
        out1 = (out0.astype(f32) + own_rows(p1) + p1_far.astype(f32)).astype(bf16)
        segment_output = to_sections(out0, out1)
        for at in range(1, bits):
            cut = [
                [halves(piece, (rep >> stages[at][0]) & 1) for piece in pieces]
                for pieces, stages in zip(state, (order_a, order_b))
            ]
            sent = [
                flip(sum_low([send for keep, send in pair]), 1 << stages[at][0])
                for pair, stages in zip(cut, (order_a, order_b))
            ]
            far_packed = flip(packed, 1 << at)
            state = [
                [sum_low([keep for keep, send in pair]), came] for pair, came in zip(cut, sent)
            ]
            state, far_packed = lax.optimization_barrier((state, far_packed))
            packed = packed + far_packed
        a0, b0 = sum_low(state[0]), sum_low(state[1])
        far_packed = flip(packed, 1)
        a0 = swap_rows(a0)
        a0, far_packed = lax.optimization_barrier((a0, far_packed))
        packed = packed + far_packed
        a0, b0 = gather_back(a0, order_a[1:]), gather_back(b0, order_b[1:])
        packed = jnp.where(sec == 0, packed[0], packed[1])
        heads = packed[6, half_in : half_in + 3 * HL].reshape(3, HL)
        smalls = (packed[6:7, :half_in], packed[0:4], packed[4:5], heads, packed[5:6, :DH])
        return segment_output, input_grad, smalls, a0, b0

    segment_output, input_grad, smalls, a0, b0 = guarded(first_layer, dn1_far)
    a0_far = flip(a0, 1 << order_a[0][0])
    b0 = collect(b0, order_b[0], rep)
    came = swap(lax.dynamic_slice_in_dim(a1, far_grp * quarter, quarter, 1), "group")
    side = (rep >> order_a[0][0]) & 1
    grad_in_proj, grad_out_proj = run_assemble(
        jnp.stack([sec, grp, side]).astype(jnp.int32),
        [to_owner(a0, 0), to_owner(a0_far, 0), swap(b0, "section")],
        [a0, a0_far, b0],
        [a1, to_owner(a1, 1), came, to_owner(came, 1), b1, to_owner(b1, 1)],
        in_proj.shape[2],
    )
    grad_in_proj = jnp.swapaxes(grad_in_proj, 0, 1)
    return (
        segment_output[None, :, None],
        input_grad[None, :, None],
        smalls[0],
        grad_in_proj[None],
        smalls[1].T[None],
        smalls[2],
        smalls[3].T[None],
        smalls[4],
        grad_out_proj[None],
    )


def solution(mesh):
    placed = (
        P(None, "replica", "group", None),
        P(None, "replica"),
        P("section", "group"),
        P("section", "group", None),
        P("section", "group", None),
        P("section", "group"),
        P("section", "group", None),
        P("section", "group"),
        P("section", "group", None),
        P(None, "replica", "group", None),
    )
    return jax.shard_map(
        on_device,
        mesh=mesh,
        in_specs=placed,
        out_specs=(
            P("section", None, "replica", "group", None),
            P("section", None, "replica", "group", None),
            P("section", "group"),
            P("section", "group", None),
            P("section", "group", None),
            P("section", "group"),
            P("section", "group", None),
            P("section", "group"),
            P("section", "group", None),
        ),
        check_vma=False,
    )
```

time: 1510 us -> 521 us (0.35)
  matrix products: 419 us -> 19.3 us
  local copies, waits for them, and re-layouts: 278 us -> 36.9 us
  other arithmetic: 256 us -> 39.9 us
  waiting for transfers between devices: 391 us -> 194 us
  Pallas kernels: 0 us -> 159 us
  blocking collectives: 69.7 us -> 0 us
  between operations: 45.6 us -> 15.4 us
  starting transfers between devices: 32.5 us -> 48.1 us
    dot_general x81 -> x9, matrix products: 419 us -> 19.3 us  [the longest x8 16.4 us: tn(): lax.dot_general(left, right, (((0,), (0,)), ((), ())), preferred_element_...]
    pallas_call x0 -> x6, Pallas kernels: none -> 159 us  [call(): pl.pallas_call(kernel, in_specs=specs, out_specs=out_specs, out_shape=[ja...]
    psum x1 -> x2, waiting for transfers between devices: 151 us -> 6.15 us  [the longest x1 6.15 us: on_device(): b1 = lax.psum(b1[:share], 'replica')]
    reduce_scatter x2 -> x0, waiting for transfers between devices: 109 us -> none  [the longest x1 109 us: on_device(): lax.psum_scatter(totals[1].astype(jnp.bfloat16), 'group', scatter_dimensi...]
    ppermute x16 -> x52, waiting for transfers between devices: 86.2 us -> 188 us  [the longest x32 99.6 us: swap(): return lax.ppermute(block, axis, [(0, 1), (1, 0)])]
    reduce_sum x33 -> x2, other arithmetic: 80.9 us -> 1.06 us  [the longest x1 0.65 us: first_layer(): skip = small[:, 7, :DH].reshape(2, HL, HDIM).sum(axis=2)]
    mul x31 -> x0, other arithmetic: 65 us -> none  [the longest x5 28.7 us: conv_silu(): return jax.nn.silu(total)]
    slice x42 -> x19, local copies, waits for them, and re-layouts: 68.5 us -> 10.4 us  [the longest x1 1.55 us: first_layer(): skip = small[:, 7, :DH].reshape(2, HL, HDIM).sum(axis=2)]
  transfers between devices with their start and end apart: 23 -> 54, of which waited for: 9 -> 23; matrix products, arithmetic and copies ran while one was open for 33% -> 16% of each run, Pallas kernels for 0% -> 23%
where the time goes in v1:
time: 521 us; the launch traced here: 514 us
  waiting for transfers between devices  194 us (37%)
  Pallas kernels  159 us (31%)
  starting transfers between devices  48.1 us (9%)
  other arithmetic  39.9 us (8%)
  local copies, waits for them, and re-layouts  36.9 us (7%)
  matrix products  19.3 us (4%)
  between operations  15.4 us (3%)
    pallas_call x6, Pallas kernels, call(): pl.pallas_call(kernel, in_specs=specs, out_specs=out_specs, out_shape=[ja...  159 us
    ppermute x32, waiting for transfers between devices, swap(): return lax.ppermute(block, axis, [(0, 1), (1, 0)])  99.6 us
    ppermute x15, waiting for transfers between devices, flip(): lax.ppermute(block, 'replica', [(at, at ^ mask) for at in range(size)])  88.6 us
    ppermute x32, starting transfers between devices, swap(): return lax.ppermute(block, axis, [(0, 1), (1, 0)])  21.3 us
    dot_general x8, matrix products, tn(): lax.dot_general(left, right, (((0,), (0,)), ((), ())), preferred_element_...  16.4 us
    ppermute x15, starting transfers between devices, flip(): lax.ppermute(block, 'replica', [(at, at ^ mask) for at in range(size)])  14.8 us
    ppermute x5, starting transfers between devices, to_owner(): return lax.ppermute(block, 'section', [(1 - layer, layer)])  11.9 us
    select_n x10, other arithmetic, in_order(): jnp.where(which == 0, jnp.concatenate([mine, other], axis=dim), jnp.conca...  11.5 us
  transfers between devices with their start and end apart: 54, of which 23 were waited for; matrix products, arithmetic and copies ran while one was open for 16% of the time, Pallas kernels for 23%

profile of v1, /device:TPU:0, one launch (start us, length us, event | category | flops | bytes accessed | tf_op | source)
XLA Modules:
  0.0 514.2 jit_solution(14265264378560475282)
XLA Ops:
  15.1 2.6 collective-permute-start.34
  17.9 1.8 broadcast_select_fusion.3
  25.0 32.8 %collective-permute-done.28 = bf16[2,8,1152]{2,1,0:T(8,128)(2,1)S(1)} collective-permute-done((bf16[2,8,1152]{2,1,0:T(8,128)(2,1)S(1)}, bf16[2,8,1152]{2,1,0:T(8,128)(2,1)S(1)}, u32[]{:S(2)}, u32[]{:S(2)}) %collective-permute-start.28) | collective-permute-done | bytes 36896 | tf_op jit(solution)/shard_map/ppermute | solution.py:1083
  57.8 2.5 broadcast_select_fusion.2
  60.3 1.8 collective-permute-start.37
  63.1 2.1 collective-permute-done.32
  66.3 28.6 %conditional.3 = (bf16[512,1024]{1,0:T(8,128)(2,1)}, f32[520,2432]{1,0:T(8,128)}, f32[512,1024]{1,0:T(8,128)}, f32[128,1024]{1,0:T(8,128)}, f32[512,1024]{1,0:T(8,128)}, /*index=5*/f32[8,512]{1,0:T(8,128)S(1)}) conditional(s32[]{:T(128)} %bitcast.12, () %tuple.48, (s32[3]{0:T(128)S(1)}, f32[8,1280]{1,0:T(8,128)S(1)}, f32[8,128]{1,0:T(8,128)S(1)}, ...), branch_computations={%region_0.1_spmd, %region_1.2_spmd} | conditional | flops 35000000512 | bytes 24980812 | solution.py:1266
  67.4 27.4 %forward_0.1 = (bf16[512,1024]{1,0:T(8,128)(2,1)}, f32[520,2432]{1,0:T(8,128)}, f32[512,1024]{1,0:T(8,128)}, f32[128,1024]{1,0:T(8,128)}, f32[512,1024]{1,0:T(8,...) custom-call(s32[3]{0:T(128)S(1)} %get-tuple-element.123.refs_0_, f32[8,1280]{1,0:T(8,128)S(1)} %get-tuple-element.124.refs_1_, ...), custom_call_target="tpu_custom_call" | custom-call | flops 35000000512 | bytes 20000000 | tf_op jit(solution)/shard_map/cond/branch_1_fun/forward_0/pallas_call | solution.py:799
  94.9 4.7 collective-permute-done.35.refs_13_
  99.7 1.7 collective-permute-start.36
  101.4 2.1 collective-permute-done.36.stat_far
  103.4 6.3 %project_0.1.refs_10_ = f32[512,1024]{1,0:T(8,128)} custom-call(s32[3]{0:T(128)S(1)} %pad_add_fusion.scal.refs_0_, f32[8,1280]{1,0:T(8,128)S(1)} %pad_maximum_fusion.1.par, bf16[1024,1024]{1,0:T(8,128)(2,1)} %bitcast.144, bf16[1024,1024]{1,0:T(8,128)(2,1)} %collective-permute-done.33.wo_b.refs_8_, f32[8,512]{1,0:T(8,128)S(1)} %get-tuple-element.281.stat_own, ...), custom_call_target="tpu_custom_call" | custom-call | flops 6000000000 | bytes 20000000 | tf_op jit(solution)/shard_map/project_0/pallas_call | solution.py:799
  109.8 1.8 convert_element_type.170
  111.5 1.7 collective-permute-start.39
  113.5 21.6 %collective-permute-done.39 = f16[512,1024]{1,0:T(8,128)(2,1)S(1)} collective-permute-done((f16[512,1024]{1,0:T(8,128)(2,1)S(1)}, f16[512,1024]{1,0:T(8,128)(2,1)S(1)}, u32[]{:S(2)}, u32[]{:S(2)}) %collective-permute-start.39) | collective-permute-done | bytes 1048608 | tf_op jit(solution)/shard_map/ppermute | solution.py:1083
  135.1 1.5 convert_element_type.171.refs_11_
  136.6 29.8 %forward_1.1 = (bf16[512,1024]{1,0:T(8,128)(2,1)}, f32[520,2432]{1,0:T(8,128)}, f32[512,1024]{1,0:T(8,128)}, f32[128,1024]{1,0:T(8,128)}, f32[512,1024]{1,0:T(8,...) custom-call(s32[3]{0:T(128)S(1)} %pad_add_fusion.scal.refs_0_, f32[8,1280]{1,0:T(8,128)S(1)} %pad_maximum_fusion.2.refs_1_, ...), custom_call_target="tpu_custom_call" | custom-call | flops 35000000512 | bytes 20000000 | tf_op jit(solution)/shard_map/forward_1/pallas_call | solution.py:799
  166.9 2.2 maximum_select_fusion.9
  171.9 1.5 collective-permute-done.41
  173.4 2.1 fusion.39
  178.2 67.6 %conditional.4 = (bf16[512,1024]{1,0:T(8,128)(2,1)}, bf16[512,1024]{1,0:T(8,128)(2,1)}, bf16[2432,512]{1,0:T(8,128)(2,1)}, f32[16,1280]{1,0:T(8,128)}) conditional(s32[]{:T(128)} %bitcast.12, () %tuple.51, (s32[3]{0:T(128)S(1)}, f32[8,1280]{1,0:T(8,128)S(1)}, f32[8,128]{1,0:T(8,128)S(1)}, bf16[4384,512]{1,0:T(8,128)(2,1)}, ...), branch_computations={%region_2.3_spmd, %region_3.4_spmd} | conditional | flops 57554722816 | bytes 58928640 | solution.py:1266
  178.4 41.2 %backward_1.1 = (bf16[512,1024]{1,0:T(8,128)(2,1)}, bf16[512,2432]{1,0:T(8,128)(2,1)}, bf16[512,1024]{1,0:T(8,128)(2,1)}, bf16[512,1024]{1,0:T(8,128)(2,1)}, bf1...) custom-call(s32[3]{0:T(128)S(1)} %get-tuple-element.140.refs_0_, f32[8,1280]{1,0:T(8,128)S(1)} %get-tuple-element.141.refs_1_, ...), custom_call_target="tpu_custom_call" | custom-call | flops 54999998464 | bytes 20000000 | tf_op jit(solution)/shard_map/cond/branch_1_fun/backward_1/pallas_call | solution.py:799
  220.3 1.5 collective-permute-start
  222.8 3.2 fusion.1
  227.2 2.9 fusion
  230.1 15.7 %collective-permute-done = bf16[512,1024]{1,0:T(8,128)(2,1)} collective-permute-done((bf16[512,1024]{1,0:T(8,128)(2,1)}, bf16[512,1024]{1,0:T(8,128)(2,1)}, u32[]{:S(2)}, u32[]{:S(2)}) %collective-permute-start) | collective-permute-done | bytes 1048608 | tf_op jit(solution)/shard_map/cond/branch_1_fun/ppermute | solution.py:1083
  245.8 6.1 %all-reduce.11.cloned.1.call-done.refs_10_ = bf16[256,1024]{1,0:T(8,128)(2,1)} async-done(((bf16[256,1024]{1,0:T(8,128)(2,1)}), bf16[256,1024]{1,0:T(8,128)(2,1)}) %all-reduce.11.cloned.1.call-update) | async-done | bytes 524304 | tf_op jit(solution)/shard_map/psum | solution.py:1294
  252.0 208.8 %conditional.5 = (f32[1,512]{1,0:T(1,128)}, f32[4,1152]{1,0:T(4,128)}, f32[1,1152]{1,0:T(1,128)}, f32[3,16]{1,0:T(4,128)}, f32[1,1024]{1,0:T(1,128)}, /*index=5*...) conditional(s32[]{:T(128)} %bitcast.12, () %tuple.46, ...), branch_computations={%region_4.5_spmd, %region_5.9_spmd} | conditional | flops 59740913664 | bytes 217801312 | solution.py:1266
  252.4 45.1 %backward_0.1 = (bf16[512,1024]{1,0:T(8,128)(2,1)}, bf16[512,2432]{1,0:T(8,128)(2,1)}, bf16[512,1024]{1,0:T(8,128)(2,1)}, bf16[512,1024]{1,0:T(8,128)(2,1)}, bf1...) custom-call(s32[3]{0:T(128)S(1)} %get-tuple-element.165.refs_0_, f32[8,1280]{1,0:T(8,128)S(1)} %get-tuple-element.166.refs_1_, ...), custom_call_target="tpu_custom_call" | custom-call | flops 54999998464 | bytes 20000000 | tf_op jit(solution)/shard_map/cond/branch_1_fun/backward_0/pallas_call | solution.py:799
  302.7 2.3 fusion.28
  305.0 1.5 fusion.20
  307.6 2.1 add_convert_fusion
  309.7 2.9 fusion.18
  312.7 1.5 fusion.10
  316.7 1.5 collective-permute-start.9
  318.2 2.9 fusion.11
  324.8 1.6 collective-permute-start.7
  327.1 1.5 slice_reduce_fusion
  330.3 1.5 collective-permute-start.12
  333.9 11.8 %collective-permute-done.12 = f32[2,16,1280]{2,1,0:T(8,128)} collective-permute-done((f32[2,16,1280]{2,1,0:T(8,128)}, f32[2,16,1280]{2,1,0:T(8,128)}, u32[]{:S(2)}, u32[]{:S(2)}) %collective-permute-start.12) | collective-permute-done | bytes 163872 | tf_op jit(solution)/shard_map/cond/branch_1_fun/ppermute | solution.py:1083
  349.0 9.0 %collective-permute-done.8 = bf16[384,1024]{1,0:T(8,128)(2,1)} collective-permute-done((bf16[384,1024]{1,0:T(8,128)(2,1)}, bf16[384,1024]{1,0:T(8,128)(2,1)}, u32[]{:S(2)}, u32[]{:S(2)}) %collective-permute-start.8) | collective-permute-done | bytes 786464 | tf_op jit(solution)/shard_map/cond/branch_1_fun/ppermute | solution.py:1088
  358.0 2.9 collective-permute-done.7
  360.9 2.2 add_convert_fusion.4
  363.1 1.7 collective-permute-start.14
  364.8 2.4 add_convert_fusion.1
  367.7 1.5 select_bitcast_fusion.1
  374.1 13.0 %collective-permute-done.15 = f32[2,8,1152]{2,1,0:T(8,128)S(1)} collective-permute-done((f32[2,8,1152]{2,1,0:T(8,128)S(1)}, f32[2,8,1152]{2,1,0:T(8,128)S(1)}, u32[]{:S(2)}, u32[]{:S(2)}) %collective-permute-start.15) | collective-permute-done | bytes 73760 | tf_op jit(solution)/shard_map/cond/branch_1_fun/ppermute | solution.py:1088
  388.3 1.8 collective-permute-start.16
  392.6 2.4 maximum_select_fusion.2
  394.9 1.8 collective-permute-start.18
  397.9 17.7 %collective-permute-done.18 = f32[2,8,1152]{2,1,0:T(8,128)S(1)} collective-permute-done((f32[2,8,1152]{2,1,0:T(8,128)S(1)}, f32[2,8,1152]{2,1,0:T(8,128)S(1)}, u32[]{:S(2)}, u32[]{:S(2)}) %collective-permute-start.18) | collective-permute-done | bytes 73760 | tf_op jit(solution)/shard_map/cond/branch_1_fun/ppermute | solution.py:1088
  417.1 1.4 collective-permute-start.19
  418.6 4.2 collective-permute-done.19
  425.6 17.2 %collective-permute-done.21 = bf16[304,512]{1,0:T(8,128)(2,1)S(1)} collective-permute-done((bf16[304,512]{1,0:T(8,128)(2,1)S(1)}, bf16[304,512]{1,0:T(8,128)(2,1)S(1)}, u32[]{:S(2)}, u32[]{:S(2)}) %collective-permute-start.21) | collective-permute-done | bytes 311328 | tf_op jit(solution)/shard_map/cond/branch_1_fun/ppermute | solution.py:1088
  444.9 9.5 %collective-permute-done.24 = bf16[192,1024]{1,0:T(8,128)(2,1)S(1)} collective-permute-done((bf16[192,1024]{1,0:T(8,128)(2,1)S(1)}, bf16[192,1024]{1,0:T(8,128)(2,1)S(1)}, u32[]{:S(2)}, u32[]{:S(2)}) %collective-permute-start.24) | collective-permute-done | bytes 393248 | tf_op jit(solution)/shard_map/cond/branch_1_fun/ppermute | solution.py:1088
  455.5 3.6 collective-permute-done.22
  459.1 1.5 maximum_select_fusion
  464.1 2.8 collective-permute-start.48
  466.9 2.1 collective-permute-start.51
  469.0 10.8 %collective-permute-done.46 = bf16[384,1024]{1,0:T(8,128)(2,1)} collective-permute-done((bf16[384,1024]{1,0:T(8,128)(2,1)}, bf16[384,1024]{1,0:T(8,128)(2,1)}, u32[]{:S(2)}, u32[]{:S(2)}) %collective-permute-start.46) | collective-permute-done | bytes 786464 | tf_op jit(solution)/shard_map/ppermute | solution.py:1088
  479.8 2.7 maximum_select_fusion.8.refs_5_
  485.0 4.9 collective-permute-done.44.refs_4_
  491.9 4.5 collective-permute-start.50
  498.3 8.8 %assemble.1 = (f32[4384,512]{1,0:T(8,128)}, f32[1024,1024]{1,0:T(8,128)}) custom-call(s32[3]{0:T(128)} %pad_add_fusion.2.scal, bf16[1216,512]{1,0:T(8,128)(2,1)} %collective-permute-done.43.refs_0_, bf16[1216,512]{1,0:T(8,128)(2,1)} %collective-permute-done.45.refs_1_, bf16[768,1024]{1,0:T(8,128)(2,1)} %collective-permute-done.47.refs_2_, ...), custom_call_target="tpu_custom_call" | custom-call | flops 6000000000 | bytes 20000000 | tf_op jit(solution)/shard_map/assemble/pallas_call | solution.py:799
  (236 shorter events, 71.9 us)
Async XLA Ops:
  7.2 244.8 %all-reduce.11.cloned.1.call-start = ((), (), s32[]{:S(2)}) async-start(), calls=%async_computation | async-start | bytes 1048576 | tf_op jit(solution)/shard_map/psum | solution.py:1294
  12.8 5.2 %collective-permute-start.30 = (bf16[1216,512]{1,0:T(8,128)(2,1)}, bf16[1216,512]{1,0:T(8,128)(2,1)}, u32[]{:S(2)}, u32[]{:S(2)}) collective-permute-start(bf16[1216,512]{1,0:T(8,128)(2,1)} %constant_dynamic-slice_fusion.15), channel_id=1, source_target_pairs={{0,16},{16,0},{1,17},{17,1},{2,18},{18,2},{3,19},{19,3},{4,20},{20... | collective-permute-start | bytes 3735560 | tf_op jit(solution)/shard_map/ppermute | solution.py:1083
  13.5 10.1 %collective-permute-start.27 = (bf16[8,1152]{1,0:T(8,128)(2,1)S(1)}, bf16[8,1152]{1,0:T(8,128)(2,1)S(1)}, u32[]{:S(2)}, u32[]{:S(2)}) collective-permute-start(bf16[8,1152]{1,0:T(8,128)(2,1)S(1)} %concatenate.149), channel_id=1, source_target_pairs={{0,16},{16,0},{1,17},{17,1},{2,18},{18,2},{3,19},{19,3},{4,20},{20... | collective-permute-start | bytes 55304 | tf_op jit(solution)/shard_map/ppermute | solution.py:1083
  13.6 51.6 %collective-permute-start.29 = (bf16[4384,512]{1,0:T(8,128)(2,1)}, bf16[4384,512]{1,0:T(8,128)(2,1)}, u32[]{:S(2)}, u32[]{:S(2)}) collective-permute-start(bf16[4384,512]{1,0:T(8,128)(2,1)} %bitcast.117), channel_id=1, source_target_pairs={{0,16},{16,0},{1,17},{17,1},{2,18},{18,2},{3,19},{19,3},{4,20},{20... | collective-permute-start | bytes 13467656 | tf_op jit(solution)/shard_map/ppermute | solution.py:1083
  15.1 47.0 %collective-permute-start.34 = (bf16[256,1024]{1,0:T(8,128)(2,1)S(1)}, bf16[256,1024]{1,0:T(8,128)(2,1)}, u32[]{:S(2)}, u32[]{:S(2)}) collective-permute-start(bf16[256,1024]{1,0:T(8,128)(2,1)S(1)} %dynamic-slice_bitcast_fusion), channel_id=1, source_target_pairs={{0,8},{8,0},{1,9},{9,1},{2,10},{10,2},{3,11},{11,3},{4,12},{12,4},... | collective-permute-start | bytes 1572872 | tf_op jit(solution)/shard_map/ppermute | solution.py:1083
  17.8 45.3 %collective-permute-start.33 = (bf16[1024,1024]{1,0:T(8,128)(2,1)}, bf16[1024,1024]{1,0:T(8,128)(2,1)}, u32[]{:S(2)}, u32[]{:S(2)}) collective-permute-start(bf16[1024,1024]{1,0:T(8,128)(2,1)} %bitcast.142), channel_id=1, source_target_pairs={{0,16},{16,0},{1,17},{17,1},{2,18},{18,2},{3,19},{19,3},{4,20},{20... | collective-permute-start | bytes 6291464 | tf_op jit(solution)/shard_map/ppermute | solution.py:1083
  17.9 3.7 copy-start.23
  19.8 38.0 %copy-start = (bf16[1216,512]{1,0:T(8,128)(2,1)S(1)}, bf16[1216,512]{1,0:T(8,128)(2,1)}, u32[]{:S(2)}) copy-start(bf16[1216,512]{1,0:T(8,128)(2,1)} %get-tuple-element.283) | copy-start | bytes 3735556
  19.8 38.0 %collective-permute-start.31 = (bf16[1216,512]{1,0:T(8,128)(2,1)}, bf16[1216,512]{1,0:T(8,128)(2,1)}, u32[]{:S(2)}, u32[]{:S(2)}) collective-permute-start(bf16[1216,512]{1,0:T(8,128)(2,1)} %get-tuple-element.327), channel_id=1, source_target_pairs={{0,8},{8,0},{1,9},{9,1},{2,10},{10,2},{3,11},{11,3},{4,12},{12,4},... | collective-permute-start | bytes 3735560 | tf_op jit(solution)/shard_map/ppermute | solution.py:1083
  23.7 34.1 %collective-permute-start.28 = (bf16[2,8,1152]{2,1,0:T(8,128)(2,1)S(1)}, bf16[2,8,1152]{2,1,0:T(8,128)(2,1)S(1)}, u32[]{:S(2)}, u32[]{:S(2)}) collective-permute-start(bf16[2,8,1152]{2,1,0:T(8,128)(2,1)S(1)} %get-tuple-element.330), channel_id=1, source_target_pairs={{0,8},{8,0},{1,9},{9,1},{2,10},{10,2},{3,11},{11,3},{4,12},{12,4},... | collective-permute-start | bytes 110600 | tf_op jit(solution)/shard_map/ppermute | solution.py:1083
  60.3 41.1 %collective-permute-start.37 = (bf16[1216,512]{1,0:T(8,128)(2,1)}, bf16[1216,512]{1,0:T(8,128)(2,1)}, u32[]{:S(2)}, u32[]{:S(2)}) collective-permute-start(bf16[1216,512]{1,0:T(8,128)(2,1)} %broadcast_select_fusion.2), channel_id=1, source_target_pairs={{0,8},{8,0},{1,9},{9,1},{2,10},{10,2},{3,11},{11,3},{4,12},{12,4},... | collective-permute-start | bytes 3735560 | tf_op jit(solution)/shard_map/ppermute | solution.py:1083
  62.0 3.2 collective-permute-start.32
  62.1 37.6 %collective-permute-start.35 = (bf16[256,1024]{1,0:T(8,128)(2,1)}, bf16[256,1024]{1,0:T(8,128)(2,1)}, u32[]{:S(2)}, u32[]{:S(2)}) collective-permute-start(bf16[256,1024]{1,0:T(8,128)(2,1)} %dynamic-slice_bitcast_fusion.1.refs_12_), channel_id=1, source_target_pairs={{0,8},{8,0},{1,9},{9,1},{2,10},{10,2},{3,11},{11,3},{4,12},{12,4},... | collective-permute-start | bytes 1572872 | tf_op jit(solution)/shard_map/ppermute | solution.py:1083
  99.7 3.7 collective-permute-start.36
  101.3 35.3 %collective-permute-start.38 = (bf16[1216,512]{1,0:T(8,128)(2,1)}, bf16[1216,512]{1,0:T(8,128)(2,1)}, u32[]{:S(2)}, u32[]{:S(2)}) collective-permute-start(bf16[1216,512]{1,0:T(8,128)(2,1)} %collective-permute-done.37.refs_5_), channel_id=1, source_target_pairs={{0,16},{16,0},{1,17},{17,1},{2,18},{18,2},{3,19},{19,3},{4,20},{20... | collective-permute-start | bytes 3735560 | tf_op jit(solution)/shard_map/ppermute | solution.py:1083
  111.5 23.6 %collective-permute-start.39 = (f16[512,1024]{1,0:T(8,128)(2,1)S(1)}, f16[512,1024]{1,0:T(8,128)(2,1)S(1)}, u32[]{:S(2)}, u32[]{:S(2)}) collective-permute-start(f16[512,1024]{1,0:T(8,128)(2,1)S(1)} %convert_element_type.170), channel_id=1, source_target_pairs={{0,8},{8,0},{1,9},{9,1},{2,10},{10,2},{3,11},{11,3},{4,12},{12,4},... | collective-permute-start | bytes 3145736 | tf_op jit(solution)/shard_map/ppermute | solution.py:1083
  166.4 3.8 copy-start.9
  166.5 3.8 collective-permute-start.40
  169.0 2.9 collective-permute-start.42
  170.5 5.0 copy-start.5
  170.5 2.9 collective-permute-start.41
  178.1 284.0 %all-reduce.13.cloned.1.call-start = ((), (), s32[]{:S(2)}) async-start(), calls=%async_computation.1 | async-start | bytes 4980736 | tf_op jit(solution)/shard_map/psum | solution.py:1307
  219.7 7.5 %collective-permute-start.1 = (bf16[512,2432]{1,0:T(8,128)(2,1)}, bf16[512,2432]{1,0:T(8,128)(2,1)S(1)}, u32[]{:S(2)}, u32[]{:S(2)}) collective-permute-start(bf16[512,2432]{1,0:T(8,128)(2,1)} %get-tuple-element.158), channel_id=1, source_target_pairs={{0,16},{16,0},{1,17},{17,1},{2,18},{18,2},{3,19},{19,3},{4,20},{20... | collective-permute-start | bytes 7471112 | tf_op jit(solution)/shard_map/cond/branch_1_fun/ppermute | solution.py:1083
  219.9 6.2 %collective-permute-start.2 = (bf16[512,1024]{1,0:T(8,128)(2,1)}, bf16[512,1024]{1,0:T(8,128)(2,1)}, u32[]{:S(2)}, u32[]{:S(2)}) collective-permute-start(bf16[512,1024]{1,0:T(8,128)(2,1)} %get-tuple-element.159), channel_id=1, source_target_pairs={{0,16},{16,0},{1,17},{17,1},{2,18},{18,2},{3,19},{19,3},{4,20},{20... | collective-permute-start | bytes 3145736 | tf_op jit(solution)/shard_map/cond/branch_1_fun/ppermute | solution.py:1083
  220.3 25.5 %collective-permute-start = (bf16[512,1024]{1,0:T(8,128)(2,1)}, bf16[512,1024]{1,0:T(8,128)(2,1)}, u32[]{:S(2)}, u32[]{:S(2)}) collective-permute-start(bf16[512,1024]{1,0:T(8,128)(2,1)} %get-tuple-element.395), channel_id=1, source_target_pairs={{0,8},{8,0},{1,9},{9,1},{2,10},{10,2},{3,11},{11,3},{4,12},{12,4},... | collective-permute-start | bytes 3145736 | tf_op jit(solution)/shard_map/cond/branch_1_fun/ppermute | solution.py:1083
  297.5 15.1 %collective-permute-start.3 = (bf16[512,2432]{1,0:T(8,128)(2,1)}, bf16[512,2432]{1,0:T(8,128)(2,1)S(1)}, u32[]{:S(2)}, u32[]{:S(2)}) collective-permute-start(bf16[512,2432]{1,0:T(8,128)(2,1)} %get-tuple-element.187), channel_id=1, source_target_pairs={{0,16},{16,0},{1,17},{17,1},{2,18},{18,2},{3,19},{19,3},{4,20},{20... | collective-permute-start | bytes 7471112 | tf_op jit(solution)/shard_map/cond/branch_1_fun/ppermute | solution.py:1083
  297.6 8.9 %collective-permute-start.4 = (bf16[512,1024]{1,0:T(8,128)(2,1)}, bf16[512,1024]{1,0:T(8,128)(2,1)}, u32[]{:S(2)}, u32[]{:S(2)}) collective-permute-start(bf16[512,1024]{1,0:T(8,128)(2,1)} %get-tuple-element.188), channel_id=1, source_target_pairs={{0,16},{16,0},{1,17},{17,1},{2,18},{18,2},{3,19},{19,3},{4,20},{20... | collective-permute-start | bytes 3145736 | tf_op jit(solution)/shard_map/cond/branch_1_fun/ppermute | solution.py:1083
  298.1 9.5 %collective-permute-start.5 = (bf16[512,1024]{1,0:T(8,128)(2,1)}, bf16[512,1024]{1,0:T(8,128)(2,1)}, u32[]{:S(2)}, u32[]{:S(2)}) collective-permute-start(bf16[512,1024]{1,0:T(8,128)(2,1)} %get-tuple-element.190), channel_id=1, source_target_pairs={{0,16},{16,0},{1,17},{17,1},{2,18},{18,2},{3,19},{19,3},{4,20},{20... | collective-permute-start | bytes 3145736 | tf_op jit(solution)/shard_map/cond/branch_1_fun/ppermute | solution.py:1083
  298.2 9.4 %collective-permute-start.6 = (bf16[512,1024]{1,0:T(8,128)(2,1)}, bf16[512,1024]{1,0:T(8,128)(2,1)}, u32[]{:S(2)}, u32[]{:S(2)}) collective-permute-start(bf16[512,1024]{1,0:T(8,128)(2,1)} %get-tuple-element.223), channel_id=1, source_target_pairs={{0,16},{16,0},{1,17},{17,1},{2,18},{18,2},{3,19},{19,3},{4,20},{20... | collective-permute-start | bytes 3145736 | tf_op jit(solution)/shard_map/cond/branch_1_fun/ppermute | solution.py:1083
  314.2 4.0 copy-start.6
  314.2 4.0 copy-start.24
  315.5 10.9 %collective-permute-start.11 = (f32[2,16,1280]{2,1,0:T(8,128)S(1)}, f32[2,16,1280]{2,1,0:T(8,128)S(1)}, u32[]{:S(2)}, u32[]{:S(2)}) collective-permute-start(f32[2,16,1280]{2,1,0:T(8,128)S(1)} %pad_maximum_fusion), channel_id=1, source_target_pairs={{0,16},{16,0},{1,17},{17,1},{2,18},{18,2},{3,19},{19,3},{4,20},{20... | collective-permute-start | bytes 491528 | tf_op jit(solution)/shard_map/cond/branch_1_fun/ppermute | solution.py:1083
  316.7 32.3 %collective-permute-start.9 = (bf16[256,1024]{1,0:T(8,128)(2,1)}, bf16[256,1024]{1,0:T(8,128)(2,1)S(1)}, u32[]{:S(2)}, u32[]{:S(2)}) collective-permute-start(bf16[256,1024]{1,0:T(8,128)(2,1)} %constant_dynamic-slice_fusion.7), channel_id=1, source_target_pairs={{0,8},{8,0},{1,9},{9,1},{2,10},{10,2},{3,11},{11,3},{4,12},{12,4},... | collective-permute-start | bytes 1572872 | tf_op jit(solution)/shard_map/cond/branch_1_fun/ppermute | solution.py:1083
  322.4 38.5 %copy-start.3 = (bf16[384,1024]{1,0:T(8,128)(2,1)S(1)}, bf16[384,1024]{1,0:T(8,128)(2,1)}, u32[]{:S(2)}) copy-start(bf16[384,1024]{1,0:T(8,128)(2,1)} %get-tuple-element.207) | copy-start | bytes 2359300 | tf_op jit(solution)/shard_map/cond
  323.3 25.7 %collective-permute-start.10 = (bf16[256,1024]{1,0:T(8,128)(2,1)}, bf16[256,1024]{1,0:T(8,128)(2,1)}, u32[]{:S(2)}, u32[]{:S(2)}) collective-permute-start(bf16[256,1024]{1,0:T(8,128)(2,1)} %dynamic-slice_convert_fusion), channel_id=1, source_target_pairs={{0,8},{8,0},{1,9},{9,1},{2,10},{10,2},{3,11},{11,3},{4,12},{12,4},... | collective-permute-start | bytes 1572872 | tf_op jit(solution)/shard_map/cond/branch_1_fun/ppermute | solution.py:1083
  323.9 34.1 %collective-permute-start.8 = (bf16[384,1024]{1,0:T(8,128)(2,1)}, bf16[384,1024]{1,0:T(8,128)(2,1)}, u32[]{:S(2)}, u32[]{:S(2)}) collective-permute-start(bf16[384,1024]{1,0:T(8,128)(2,1)} %get-tuple-element.198), channel_id=1, source_target_pairs={{0,2},{1,3},{2,0},{3,1},{4,6},{5,7},{6,4},{7,5},{8,10},{9,11},{10,... | collective-permute-start | bytes 2359304 | tf_op jit(solution)/shard_map/cond/branch_1_fun/ppermute | solution.py:1088
  324.8 36.1 %collective-permute-start.7 = (bf16[1216,512]{1,0:T(8,128)(2,1)}, bf16[1216,512]{1,0:T(8,128)(2,1)}, u32[]{:S(2)}, u32[]{:S(2)}) collective-permute-start(bf16[1216,512]{1,0:T(8,128)(2,1)} %get-tuple-element.197), channel_id=1, source_target_pairs={{0,1},{1,0},{2,3},{3,2},{4,5},{5,4},{6,7},{7,6},{8,9},{9,8},{10,11... | collective-permute-start | bytes 3735560 | tf_op jit(solution)/shard_map/cond/branch_1_fun/ppermute | solution.py:1088
  330.3 15.5 %collective-permute-start.12 = (f32[2,16,1280]{2,1,0:T(8,128)}, f32[2,16,1280]{2,1,0:T(8,128)}, u32[]{:S(2)}, u32[]{:S(2)}) collective-permute-start(f32[2,16,1280]{2,1,0:T(8,128)} %fusion.38), channel_id=1, source_target_pairs={{0,8},{8,0},{1,9},{9,1},{2,10},{10,2},{3,11},{11,3},{4,12},{12,4},... | collective-permute-start | bytes 491528 | tf_op jit(solution)/shard_map/cond/branch_1_fun/ppermute | solution.py:1083
  363.1 4.6 copy-start.13
  363.1 4.6 copy-start.14
  363.1 24.0 %collective-permute-start.14 = (bf16[192,1024]{1,0:T(8,128)(2,1)}, bf16[192,1024]{1,0:T(8,128)(2,1)}, u32[]{:S(2)}, u32[]{:S(2)}) collective-permute-start(bf16[192,1024]{1,0:T(8,128)(2,1)} %get-tuple-element.339), channel_id=1, source_target_pairs={{0,1},{1,0},{2,3},{3,2},{4,5},{5,4},{6,7},{7,6},{8,9},{9,8},{10,11... | collective-permute-start | bytes 1179656 | tf_op jit(solution)/shard_map/cond/branch_1_fun/ppermute | solution.py:1088
  367.3 19.9 %collective-permute-start.13 = (bf16[608,512]{1,0:T(8,128)(2,1)}, bf16[608,512]{1,0:T(8,128)(2,1)}, u32[]{:S(2)}, u32[]{:S(2)}) collective-permute-start(bf16[608,512]{1,0:T(8,128)(2,1)} %get-tuple-element.335), channel_id=1, source_target_pairs={{0,2},{1,3},{2,0},{3,1},{4,6},{5,7},{6,4},{7,5},{8,10},{9,11},{10,... | collective-permute-start | bytes 1867784 | tf_op jit(solution)/shard_map/cond/branch_1_fun/ppermute | solution.py:1088
  371.2 21.4 %collective-permute-start.26 = (bf16[256,1024]{1,0:T(8,128)(2,1)}, bf16[256,1024]{1,0:T(8,128)(2,1)}, u32[]{:S(2)}, u32[]{:S(2)}) collective-permute-start(bf16[256,1024]{1,0:T(8,128)(2,1)} %broadcast_select_fusion), channel_id=1, source_target_pairs={{0,16},{16,0},{1,17},{17,1},{2,18},{18,2},{3,19},{19,3},{4,20},{20... | collective-permute-start | bytes 1572872 | tf_op jit(solution)/shard_map/cond/branch_1_fun/ppermute | solution.py:1083
  372.2 24.6 %collective-permute-start.25 = (bf16[256,1024]{1,0:T(8,128)(2,1)}, bf16[256,1024]{1,0:T(8,128)(2,1)S(1)}, u32[]{:S(2)}, u32[]{:S(2)}) collective-permute-start(bf16[256,1024]{1,0:T(8,128)(2,1)} %broadcast_select_fusion.1), channel_id=1, source_target_pairs={{0,16},{16,0},{1,17},{17,1},{2,18},{18,2},{3,19},{19,3},{4,20},{20... | collective-permute-start | bytes 1572872 | tf_op jit(solution)/shard_map/cond/branch_1_fun/ppermute | solution.py:1083
  372.7 14.4 %collective-permute-start.15 = (f32[2,8,1152]{2,1,0:T(8,128)S(1)}, f32[2,8,1152]{2,1,0:T(8,128)S(1)}, u32[]{:S(2)}, u32[]{:S(2)}) collective-permute-start(f32[2,8,1152]{2,1,0:T(8,128)S(1)} %fusion.31), channel_id=1, source_target_pairs={{0,2},{1,3},{2,0},{3,1},{4,6},{5,7},{6,4},{7,5},{8,10},{9,11},{10,... | collective-permute-start | bytes 221192 | tf_op jit(solution)/shard_map/cond/branch_1_fun/ppermute | solution.py:1088
  388.3 27.3 %collective-permute-start.16 = (bf16[304,512]{1,0:T(8,128)(2,1)S(1)}, bf16[304,512]{1,0:T(8,128)(2,1)S(1)}, u32[]{:S(2)}, u32[]{:S(2)}) collective-permute-start(bf16[304,512]{1,0:T(8,128)(2,1)S(1)} %get-tuple-element.343), channel_id=1, source_target_pairs={{0,4},{1,5},{2,6},{3,7},{4,0},{5,1},{6,2},{7,3},{8,12},{9,13},{10,... | collective-permute-start | bytes 933896 | tf_op jit(solution)/shard_map/cond/branch_1_fun/ppermute | solution.py:1088
  391.3 24.3 %collective-permute-start.17 = (bf16[96,1024]{1,0:T(8,128)(2,1)S(1)}, bf16[96,1024]{1,0:T(8,128)(2,1)S(1)}, u32[]{:S(2)}, u32[]{:S(2)}) collective-permute-start(bf16[96,1024]{1,0:T(8,128)(2,1)S(1)} %get-tuple-element.349), channel_id=1, source_target_pairs={{0,4},{1,5},{2,6},{3,7},{4,0},{5,1},{6,2},{7,3},{8,12},{9,13},{10,... | collective-permute-start | bytes 589832 | tf_op jit(solution)/shard_map/cond/branch_1_fun/ppermute | solution.py:1088
  394.9 20.7 %collective-permute-start.18 = (f32[2,8,1152]{2,1,0:T(8,128)S(1)}, f32[2,8,1152]{2,1,0:T(8,128)S(1)}, u32[]{:S(2)}, u32[]{:S(2)}) collective-permute-start(f32[2,8,1152]{2,1,0:T(8,128)S(1)} %add.199), channel_id=1, source_target_pairs={{0,4},{1,5},{2,6},{3,7},{4,0},{5,1},{6,2},{7,3},{8,12},{9,13},{10,... | collective-permute-start | bytes 221192 | tf_op jit(solution)/shard_map/cond/branch_1_fun/ppermute | solution.py:1088
  415.6 7.3 %collective-permute-start.20 = (f32[2,8,1152]{2,1,0:T(8,128)S(1)}, f32[2,8,1152]{2,1,0:T(8,128)S(1)}, u32[]{:S(2)}, u32[]{:S(2)}) collective-permute-start(f32[2,8,1152]{2,1,0:T(8,128)S(1)} %add.208), channel_id=1, source_target_pairs={{0,1},{1,0},{2,3},{3,2},{4,5},{5,4},{6,7},{7,6},{8,9},{9,8},{10,11... | collective-permute-start | bytes 221192 | tf_op jit(solution)/shard_map/cond/branch_1_fun/ppermute | solution.py:1088
  417.1 5.7 %collective-permute-start.19 = (bf16[304,256]{1,0:T(8,128)(2,1)S(1)}, bf16[304,256]{1,0:T(8,128)(2,1)S(1)}, u32[]{:S(2)}, u32[]{:S(2)}) collective-permute-start(bf16[304,256]{1,0:T(8,128)(2,1)S(1)} %get-tuple-element.352), channel_id=1, source_target_pairs={{0,8},{8,0},{1,9},{9,1},{2,10},{10,2},{3,11},{11,3},{4,12},{12,4},... | collective-permute-start | bytes 466952 | tf_op jit(solution)/shard_map/cond/branch_1_fun/ppermute | solution.py:1083
  418.5 24.6 %collective-permute-start.23 = (bf16[96,1024]{1,0:T(8,128)(2,1)S(1)}, bf16[96,1024]{1,0:T(8,128)(2,1)S(1)}, u32[]{:S(2)}, u32[]{:S(2)}) collective-permute-start(bf16[96,1024]{1,0:T(8,128)(2,1)S(1)} %add_convert_fusion.9), channel_id=1, source_target_pairs={{0,4},{1,5},{2,6},{3,7},{4,0},{5,1},{6,2},{7,3},{8,12},{9,13},{10,... | collective-permute-start | bytes 589832 | tf_op jit(solution)/shard_map/cond/branch_1_fun/ppermute | solution.py:1088
  423.0 19.8 %collective-permute-start.21 = (bf16[304,512]{1,0:T(8,128)(2,1)S(1)}, bf16[304,512]{1,0:T(8,128)(2,1)S(1)}, u32[]{:S(2)}, u32[]{:S(2)}) collective-permute-start(bf16[304,512]{1,0:T(8,128)(2,1)S(1)} %maximum_select_fusion.6), channel_id=1, source_target_pairs={{0,4},{1,5},{2,6},{3,7},{4,0},{5,1},{6,2},{7,3},{8,12},{9,13},{10,... | collective-permute-start | bytes 933896 | tf_op jit(solution)/shard_map/cond/branch_1_fun/ppermute | solution.py:1088
  443.0 16.0 %collective-permute-start.22 = (bf16[608,512]{1,0:T(8,128)(2,1)S(1)}, bf16[608,512]{1,0:T(8,128)(2,1)S(1)}, u32[]{:S(2)}, u32[]{:S(2)}) collective-permute-start(bf16[608,512]{1,0:T(8,128)(2,1)S(1)} %maximum_select_fusion.4), channel_id=1, source_target_pairs={{0,2},{1,3},{2,0},{3,1},{4,6},{5,7},{6,4},{7,5},{8,10},{9,11},{10,... | collective-permute-start | bytes 1867784 | tf_op jit(solution)/shard_map/cond/branch_1_fun/ppermute | solution.py:1088
  443.2 11.1 %collective-permute-start.24 = (bf16[192,1024]{1,0:T(8,128)(2,1)S(1)}, bf16[192,1024]{1,0:T(8,128)(2,1)S(1)}, u32[]{:S(2)}, u32[]{:S(2)}) collective-permute-start(bf16[192,1024]{1,0:T(8,128)(2,1)S(1)} %maximum_select_fusion.5), channel_id=1, source_target_pairs={{0,1},{1,0},{2,3},{3,2},{4,5},{5,4},{6,7},{7,6},{8,9},{9,8},{10,11... | collective-permute-start | bytes 1179656 | tf_op jit(solution)/shard_map/cond/branch_1_fun/ppermute | solution.py:1088
  460.8 6.1 %copy-start.27 = (bf16[256,1024]{1,0:T(8,128)(2,1)S(1)}, bf16[256,1024]{1,0:T(8,128)(2,1)}, u32[]{:S(2)}) copy-start(bf16[256,1024]{1,0:T(8,128)(2,1)} %all-reduce.11.cloned.1.call-done.refs_10_) | copy-start | bytes 1572868
  460.8 19.0 %collective-permute-start.46 = (bf16[384,1024]{1,0:T(8,128)(2,1)}, bf16[384,1024]{1,0:T(8,128)(2,1)}, u32[]{:S(2)}, u32[]{:S(2)}) collective-permute-start(bf16[384,1024]{1,0:T(8,128)(2,1)} %get-tuple-element.302), channel_id=1, source_target_pairs={{0,2},{1,3},{2,0},{3,1},{4,6},{5,7},{6,4},{7,5},{8,10},{9,11},{10,... | collective-permute-start | bytes 2359304 | tf_op jit(solution)/shard_map/ppermute | solution.py:1088
  461.1 28.8 %collective-permute-start.44 = (bf16[1216,512]{1,0:T(8,128)(2,1)}, bf16[1216,512]{1,0:T(8,128)(2,1)}, u32[]{:S(2)}, u32[]{:S(2)}) collective-permute-start(bf16[1216,512]{1,0:T(8,128)(2,1)} %get-tuple-element.301.refs_3_), channel_id=1, source_target_pairs={{0,1},{1,0},{2,3},{3,2},{4,5},{5,4},{6,7},{7,6},{8,9},{9,8},{10,11... | collective-permute-start | bytes 3735560 | tf_op jit(solution)/shard_map/ppermute | solution.py:1088
  463.5 28.4 %collective-permute-start.49 = (bf16[2432,256]{1,0:T(8,128)(2,1)S(1)}, bf16[2432,256]{1,0:T(8,128)(2,1)}, u32[]{:S(2)}, u32[]{:S(2)}) collective-permute-start(bf16[2432,256]{1,0:T(8,128)(2,1)S(1)} %constant_dynamic-slice_fusion.14), channel_id=1, source_target_pairs={{0,8},{8,0},{1,9},{9,1},{2,10},{10,2},{3,11},{11,3},{4,12},{12,4},... | collective-permute-start | bytes 3735560 | tf_op jit(solution)/shard_map/ppermute | solution.py:1083
  464.1 34.1 %collective-permute-start.48 = (bf16[2432,512]{1,0:T(8,128)(2,1)}, bf16[2432,512]{1,0:T(8,128)(2,1)}, u32[]{:S(2)}, u32[]{:S(2)}) collective-permute-start(bf16[2432,512]{1,0:T(8,128)(2,1)} %all-reduce.13.cloned.1.call-done.refs_6_), channel_id=1, source_target_pairs={{0,16},{1,17},{2,18},{3,19},{4,20},{5,21},{6,22},{7,23},{8,24},{9,... | collective-permute-start | bytes 7471112 | tf_op jit(solution)/shard_map/ppermute | solution.py:1320
  466.9 16.9 %collective-permute-start.51 = (bf16[256,1024]{1,0:T(8,128)(2,1)S(1)}, bf16[256,1024]{1,0:T(8,128)(2,1)}, u32[]{:S(2)}, u32[]{:S(2)}) collective-permute-start(bf16[256,1024]{1,0:T(8,128)(2,1)S(1)} %copy-done.27), channel_id=1, source_target_pairs={{0,16},{1,17},{2,18},{3,19},{4,20},{5,21},{6,22},{7,23},{8,24},{9,... | collective-permute-start | bytes 1572872 | tf_op jit(solution)/shard_map/ppermute | solution.py:1320
  483.8 14.5 %collective-permute-start.47 = (bf16[768,1024]{1,0:T(8,128)(2,1)S(1)}, bf16[768,1024]{1,0:T(8,128)(2,1)}, u32[]{:S(2)}, u32[]{:S(2)}) collective-permute-start(bf16[768,1024]{1,0:T(8,128)(2,1)S(1)} %maximum_select_fusion.8.refs_5_), channel_id=1, source_target_pairs={{0,16},{16,0},{1,17},{17,1},{2,18},{18,2},{3,19},{19,3},{4,20},{20... | collective-permute-start | bytes 4718600 | tf_op jit(solution)/shard_map/ppermute | solution.py:1083
  483.8 14.5 %collective-permute-start.43 = (bf16[1216,512]{1,0:T(8,128)(2,1)}, bf16[1216,512]{1,0:T(8,128)(2,1)}, u32[]{:S(2)}, u32[]{:S(2)}) collective-permute-start(bf16[1216,512]{1,0:T(8,128)(2,1)} %get-tuple-element.301.refs_3_), channel_id=1, source_target_pairs={{16,0},{17,1},{18,2},{19,3},{20,4},{21,5},{22,6},{23,7},{24,8},{25... | collective-permute-start | bytes 3735560 | tf_op jit(solution)/shard_map/ppermute | solution.py:1320
  489.9 8.3 %collective-permute-start.45 = (bf16[1216,512]{1,0:T(8,128)(2,1)}, bf16[1216,512]{1,0:T(8,128)(2,1)}, u32[]{:S(2)}, u32[]{:S(2)}) collective-permute-start(bf16[1216,512]{1,0:T(8,128)(2,1)} %collective-permute-done.44.refs_4_), channel_id=1, source_target_pairs={{16,0},{17,1},{18,2},{19,3},{20,4},{21,5},{22,6},{23,7},{24,8},{25... | collective-permute-start | bytes 3735560 | tf_op jit(solution)/shard_map/ppermute | solution.py:1320
  491.9 6.4 %collective-permute-start.50 = (bf16[2432,256]{1,0:T(8,128)(2,1)}, bf16[2432,256]{1,0:T(8,128)(2,1)}, u32[]{:S(2)}, u32[]{:S(2)}) collective-permute-start(bf16[2432,256]{1,0:T(8,128)(2,1)} %collective-permute-done.49.refs_8_), channel_id=1, source_target_pairs={{0,16},{1,17},{2,18},{3,19},{4,20},{5,21},{6,22},{7,23},{8,24},{9,... | collective-permute-start | bytes 3735560 | tf_op jit(solution)/shard_map/ppermute | solution.py:1320
  (19 other events, 39.5 us)
Sparse Core Ops, SparseCore 0:
  178.2 73.6 all-reduce.10
  256.6 118.4 all-reduce.12

commit v2 on v1

--- a/solution.py
+++ b/solution.py
@@ -247,7 +247,6 @@
 
 def load_weights(layer, sec, grp, w_a, w_b, w_x, w_y, w_s, sems):
     width = w_a.shape[1]
-    part = w_x.shape[0]
     mine = pl.ds(pl.multiple_of(grp * width, width), width)
     other = pl.ds(pl.multiple_of((1 - grp) * width, width), width)
     first = pl.multiple_of(grp * DH, DH)
@@ -258,7 +257,7 @@
         (pl.ds(2 * DI, 2 * NS), pl.ds(2 * DH, 2 * NS)),
         (pl.ds(steps, HL), pl.ds(DH + CH, HL)),
     ]
-    w_s[DH + CH + HL : CP, mine] = jnp.zeros((LANE - HL, width), bf16)
+    w_s[DH + CH + HL : CP] = jnp.zeros((LANE - HL, 2 * width), bf16)
 
     def pieces(block):
         return copies([(block.at[src], w_s.at[dst, mine]) for src, dst in places], sems, 0)
@@ -275,9 +274,14 @@
         for copy in given:
             copy.start()
 
-    at_x = pl.ds(pl.multiple_of(sec * part, part), part)
-    at_y = pl.ds(pl.multiple_of((1 - sec) * part, part), part)
-    far = copies([(w_x, w_s.at[at_x, other]), (w_y, w_s.at[at_y, other])], sems, 5)
+    pairs = []
+    for part, which in ((w_x, sec), (w_y, 1 - sec)):
+        wide = pl.ds(pl.multiple_of(which * DH, DH), DH)
+        thin = pl.ds(pl.multiple_of(2 * DH + which * NS, NS), NS)
+        pairs.append((part.at[pl.ds(0, DH)], w_s.at[wide, other]))
+        pairs.append((part.at[pl.ds(DH, NS)], w_s.at[thin, other]))
+    pairs.append((w_x.at[pl.ds(DH + NS, HL)], w_s.at[pl.ds(DH + CH, HL), other]))
+    far = copies(pairs, sems, 24)
     for copy in far:
         copy.start()
     return held + far
@@ -857,7 +861,7 @@
         vm((LANE, count), f32),
         vm((count, DM), bf16),
         vm((count, DH), bf16),
-        pltpu.SemaphoreType.DMA((22,)),
+        pltpu.SemaphoreType.DMA((29,)),
     ]
     return call(
         functools.partial(forward_kernel, layer),
@@ -1065,7 +1069,7 @@
         vm((LANE, count), f32),
         vm((count, DH), bf16),
         vm((count, DH), bf16),
-        pltpu.SemaphoreType.DMA((24,)),
+        pltpu.SemaphoreType.DMA((29,)),
     ]
     return call(
         functools.partial(backward_kernel, layer),
@@ -1170,17 +1174,18 @@
 
     block = jnp.swapaxes(in_proj, 1, 2)[0]
     far_grp = 1 - grp
-    other = jnp.concatenate(
-        [
-            lax.dynamic_slice_in_dim(block, far_grp * DH, DH, 0),
-            lax.dynamic_slice_in_dim(block, DI + far_grp * DH, DH, 0),
-            block[2 * DI : 2 * DI + 2 * NS],
-            lax.dynamic_slice_in_dim(block, DI + CONVC + far_grp * HL, HL, 0),
-            jnp.zeros((LANE - HL, block.shape[1]), bf16),
-        ],
-        axis=0,
-    )
-    keep, give = halves(other, sec)
+
+    def far_part(which):
+        return jnp.concatenate(
+            [
+                lax.dynamic_slice_in_dim(block, which * DI + far_grp * DH, DH, 0),
+                lax.dynamic_slice_in_dim(block, 2 * DI + which * NS, NS, 0),
+                lax.dynamic_slice_in_dim(block, DI + CONVC + far_grp * HL, HL, 0),
+            ],
+            axis=0,
+        )
+
+    keep, give = far_part(sec), far_part(1 - sec)
     got = swap(give, "section")
     first_x = swap(jnp.where(sec == 0, keep, got), "group")
     keep, got, cot_own, first_x = lax.optimization_barrier((keep, got, cot_own, first_x))
@@ -1268,10 +1273,10 @@
     u0, proj0, ys0, st0, mix0, unused_sum, stat0 = guarded(
         lambda tokens: run_forward(0, scal, pars[0], hps[0], weights[0], tokens, None), tokens
     )
-    stat0, cot_far = lax.optimization_barrier((stat0, cots[1]))
-    cots = [cot_own, cot_far]
     stat0_far = swap(stat0, "group")
     p0 = run_project(0, scal, pars[0], wo_a, wo_b, stat0, stat0_far, mix0)
+    p0, cot_far = lax.optimization_barrier((p0, cot_far))
+    cots = [cot_own, cot_far]
     p0_far = swap(p0.astype(jnp.float16), "group").astype(f32)
     u1, proj1, ys1, st1, mix1, p_total, stat1 = run_forward(
         1, scal, pars[1], hps[1], weights[1], cots, [u0, p0, p0_far]

time: 521 us -> 519 us (level)
  no operation moved by 1% of the time
where the time goes in v2:
time: 519 us; the launch traced here: 512 us
  waiting for transfers between devices  192 us (37%)
  Pallas kernels  159 us (31%)
  starting transfers between devices  48.5 us (9%)
  other arithmetic  39.1 us (8%)
  local copies, waits for them, and re-layouts  36.8 us (7%)
  matrix products  19.3 us (4%)
  between operations  15.4 us (3%)
    pallas_call x6, Pallas kernels, call(): pl.pallas_call(kernel, in_specs=specs, out_specs=out_specs, out_shape=[ja...  159 us
    ppermute x32, waiting for transfers between devices, swap(): return lax.ppermute(block, axis, [(0, 1), (1, 0)])  97.7 us
    ppermute x15, waiting for transfers between devices, flip(): lax.ppermute(block, 'replica', [(at, at ^ mask) for at in range(size)])  88.5 us
    ppermute x32, starting transfers between devices, swap(): return lax.ppermute(block, axis, [(0, 1), (1, 0)])  21.8 us
    dot_general x8, matrix products, tn(): lax.dot_general(left, right, (((0,), (0,)), ((), ())), preferred_element_...  16.4 us
    ppermute x15, starting transfers between devices, flip(): lax.ppermute(block, 'replica', [(at, at ^ mask) for at in range(size)])  14.8 us
    ppermute x5, starting transfers between devices, to_owner(): return lax.ppermute(block, 'section', [(1 - layer, layer)])  11.9 us
    select_n x10, other arithmetic, in_order(): jnp.where(which == 0, jnp.concatenate([mine, other], axis=dim), jnp.conca...  11.4 us
  transfers between devices with their start and end apart: 54, of which 23 were waited for; matrix products, arithmetic and copies ran while one was open for 16% of the time, Pallas kernels for 23%

profile of v2, /device:TPU:0, one launch (start us, length us, event | category | flops | bytes accessed | tf_op | source)
XLA Modules:
  0.0 511.6 jit_solution(5695818628181599324)
XLA Ops:
  9.0 2.7 dynamic-slice_bitcast_fusion
  14.2 3.0 collective-permute-start.34
  17.8 1.9 dynamic-slice_bitcast_fusion.3.refs_12_
  19.7 2.6 broadcast_select_fusion.3
  23.9 1.9 collective-permute-start.28
  26.1 29.7 %collective-permute-done.28 = bf16[2,8,1152]{2,1,0:T(8,128)(2,1)S(1)} collective-permute-done((bf16[2,8,1152]{2,1,0:T(8,128)(2,1)S(1)}, bf16[2,8,1152]{2,1,0:T(8,128)(2,1)S(1)}, u32[]{:S(2)}, u32[]{:S(2)}) %collective-permute-start.28) | collective-permute-done | bytes 36896 | tf_op jit(solution)/shard_map/ppermute | solution.py:1087
  57.0 1.7 collective-permute-start.37
  59.4 2.4 collective-permute-done.32
  62.9 28.7 %conditional.3 = (bf16[512,1024]{1,0:T(8,128)(2,1)}, f32[520,2432]{1,0:T(8,128)}, f32[512,1024]{1,0:T(8,128)}, f32[128,1024]{1,0:T(8,128)}, f32[512,1024]{1,0:T(8,128)}, /*index=5*/f32[8,512]{1,0:T(8,128)S(1)}) conditional(s32[]{:T(128)} %bitcast.12, () %tuple.48, (s32[3]{0:T(128)S(1)}, f32[8,1280]{1,0:T(8,128)S(1)}, f32[8,128]{1,0:T(8,128)S(1)}, ...), branch_computations={%region_0.1_spmd, %region_1.2_spmd} | conditional | flops 35000000512 | bytes 24784204 | solution.py:1271
  63.9 27.4 %forward_0.1 = (bf16[512,1024]{1,0:T(8,128)(2,1)}, f32[520,2432]{1,0:T(8,128)}, f32[512,1024]{1,0:T(8,128)}, f32[128,1024]{1,0:T(8,128)}, f32[512,1024]{1,0:T(8,...) custom-call(s32[3]{0:T(128)S(1)} %get-tuple-element.123.refs_0_, f32[8,1280]{1,0:T(8,128)S(1)} %get-tuple-element.124.refs_1_, ...), custom_call_target="tpu_custom_call" | custom-call | flops 35000000512 | bytes 20000000 | tf_op jit(solution)/shard_map/cond/branch_1_fun/forward_0/pallas_call | solution.py:803
  91.9 1.7 collective-permute-start.36
  93.7 1.8 collective-permute-done.35.stat_far
  95.5 6.3 %project_0.1.refs_10_ = f32[512,1024]{1,0:T(8,128)} custom-call(s32[3]{0:T(128)S(1)} %pad_add_fusion.scal.refs_0_, f32[8,1280]{1,0:T(8,128)S(1)} %pad_maximum_fusion.3.par, bf16[1024,1024]{1,0:T(8,128)(2,1)} %bitcast.147, bf16[1024,1024]{1,0:T(8,128)(2,1)} %collective-permute-done.33.wo_b.refs_8_, f32[8,512]{1,0:T(8,128)S(1)} %get-tuple-element.279.stat_own, ...), custom_call_target="tpu_custom_call" | custom-call | flops 6000000000 | bytes 20000000 | tf_op jit(solution)/shard_map/project_0/pallas_call | solution.py:803
  101.8 4.4 collective-permute-done.36.refs_13_
  106.2 1.8 convert_element_type.170
  108.0 1.6 collective-permute-start.39
  109.8 22.6 %collective-permute-done.39 = f16[512,1024]{1,0:T(8,128)(2,1)S(1)} collective-permute-done((f16[512,1024]{1,0:T(8,128)(2,1)S(1)}, f16[512,1024]{1,0:T(8,128)(2,1)S(1)}, u32[]{:S(2)}, u32[]{:S(2)}) %collective-permute-start.39) | collective-permute-done | bytes 1048608 | tf_op jit(solution)/shard_map/ppermute | solution.py:1087
  132.3 1.5 convert_element_type.171.refs_11_
  133.9 30.0 %forward_1.1 = (bf16[512,1024]{1,0:T(8,128)(2,1)}, f32[520,2432]{1,0:T(8,128)}, f32[512,1024]{1,0:T(8,128)}, f32[128,1024]{1,0:T(8,128)}, f32[512,1024]{1,0:T(8,...) custom-call(s32[3]{0:T(128)S(1)} %pad_add_fusion.scal.refs_0_, f32[8,1280]{1,0:T(8,128)S(1)} %pad_maximum_fusion.4.refs_1_, ...), custom_call_target="tpu_custom_call" | custom-call | flops 35000000512 | bytes 20000000 | tf_op jit(solution)/shard_map/forward_1/pallas_call | solution.py:803
  165.2 2.0 maximum_select_fusion.9
  168.1 1.9 collective-permute-done.42
  170.0 1.5 collective-permute-done.41
  171.5 2.1 fusion.39
  176.3 67.6 %conditional.4 = (bf16[512,1024]{1,0:T(8,128)(2,1)}, bf16[512,1024]{1,0:T(8,128)(2,1)}, bf16[2432,512]{1,0:T(8,128)(2,1)}, f32[16,1280]{1,0:T(8,128)}) conditional(s32[]{:T(128)} %bitcast.12, () %tuple.51, (s32[3]{0:T(128)S(1)}, f32[8,1280]{1,0:T(8,128)S(1)}, f32[8,128]{1,0:T(8,128)S(1)}, bf16[4384,512]{1,0:T(8,128)(2,1)}, ...), branch_computations={%region_2.3_spmd, %region_3.4_spmd} | conditional | flops 57554722816 | bytes 58928640 | solution.py:1271
  176.5 41.3 %backward_1.1 = (bf16[512,1024]{1,0:T(8,128)(2,1)}, bf16[512,2432]{1,0:T(8,128)(2,1)}, bf16[512,1024]{1,0:T(8,128)(2,1)}, bf16[512,1024]{1,0:T(8,128)(2,1)}, bf1...) custom-call(s32[3]{0:T(128)S(1)} %get-tuple-element.140.refs_0_, f32[8,1280]{1,0:T(8,128)S(1)} %get-tuple-element.141.refs_1_, ...), custom_call_target="tpu_custom_call" | custom-call | flops 54999998464 | bytes 20000000 | tf_op jit(solution)/shard_map/cond/branch_1_fun/backward_1/pallas_call | solution.py:803
  220.2 3.2 fusion.1
  225.3 2.9 fusion
  228.2 15.7 %collective-permute-done = bf16[512,1024]{1,0:T(8,128)(2,1)} collective-permute-done((bf16[512,1024]{1,0:T(8,128)(2,1)}, bf16[512,1024]{1,0:T(8,128)(2,1)}, u32[]{:S(2)}, u32[]{:S(2)}) %collective-permute-start) | collective-permute-done | bytes 1048608 | tf_op jit(solution)/shard_map/cond/branch_1_fun/ppermute | solution.py:1087
  243.9 5.5 %all-reduce.11.cloned.1.call-done.refs_10_ = bf16[256,1024]{1,0:T(8,128)(2,1)} async-done(((bf16[256,1024]{1,0:T(8,128)(2,1)}), bf16[256,1024]{1,0:T(8,128)(2,1)}) %all-reduce.11.cloned.1.call-update) | async-done | bytes 524304 | tf_op jit(solution)/shard_map/psum | solution.py:1299
  249.5 208.8 %conditional.5 = (f32[1,512]{1,0:T(1,128)}, f32[4,1152]{1,0:T(4,128)}, f32[1,1152]{1,0:T(1,128)}, f32[3,16]{1,0:T(4,128)}, f32[1,1024]{1,0:T(1,128)}, /*index=5*...) conditional(s32[]{:T(128)} %bitcast.12, () %tuple.46, ...), branch_computations={%region_4.5_spmd, %region_5.9_spmd} | conditional | flops 59740913664 | bytes 217801312 | solution.py:1271
  250.0 45.1 %backward_0.1 = (bf16[512,1024]{1,0:T(8,128)(2,1)}, bf16[512,2432]{1,0:T(8,128)(2,1)}, bf16[512,1024]{1,0:T(8,128)(2,1)}, bf16[512,1024]{1,0:T(8,128)(2,1)}, bf1...) custom-call(s32[3]{0:T(128)S(1)} %get-tuple-element.165.refs_0_, f32[8,1280]{1,0:T(8,128)S(1)} %get-tuple-element.166.refs_1_, ...), custom_call_target="tpu_custom_call" | custom-call | flops 54999998464 | bytes 20000000 | tf_op jit(solution)/shard_map/cond/branch_1_fun/backward_0/pallas_call | solution.py:803
  300.2 2.3 fusion.28
  302.5 1.5 fusion.20
  305.1 2.1 add_convert_fusion
  307.3 2.9 fusion.18
  310.2 1.5 fusion.10
  315.7 2.9 fusion.11
  322.4 1.6 collective-permute-start.7
  324.7 1.5 slice_reduce_fusion
  331.5 11.8 %collective-permute-done.12 = f32[2,16,1280]{2,1,0:T(8,128)} collective-permute-done((f32[2,16,1280]{2,1,0:T(8,128)}, f32[2,16,1280]{2,1,0:T(8,128)}, u32[]{:S(2)}, u32[]{:S(2)}) %collective-permute-start.12) | collective-permute-done | bytes 163872 | tf_op jit(solution)/shard_map/cond/branch_1_fun/ppermute | solution.py:1087
  346.6 8.9 %collective-permute-done.8 = bf16[384,1024]{1,0:T(8,128)(2,1)} collective-permute-done((bf16[384,1024]{1,0:T(8,128)(2,1)}, bf16[384,1024]{1,0:T(8,128)(2,1)}, u32[]{:S(2)}, u32[]{:S(2)}) %collective-permute-start.8) | collective-permute-done | bytes 786464 | tf_op jit(solution)/shard_map/cond/branch_1_fun/ppermute | solution.py:1092
  355.5 3.0 collective-permute-done.7
  358.5 2.2 add_convert_fusion.4
  360.7 1.7 collective-permute-start.14
  362.4 2.4 add_convert_fusion.1
  365.2 1.5 select_bitcast_fusion.1
  371.6 13.0 %collective-permute-done.15 = f32[2,8,1152]{2,1,0:T(8,128)S(1)} collective-permute-done((f32[2,8,1152]{2,1,0:T(8,128)S(1)}, f32[2,8,1152]{2,1,0:T(8,128)S(1)}, u32[]{:S(2)}, u32[]{:S(2)}) %collective-permute-start.15) | collective-permute-done | bytes 73760 | tf_op jit(solution)/shard_map/cond/branch_1_fun/ppermute | solution.py:1092
  385.9 1.8 collective-permute-start.16
  390.1 2.4 maximum_select_fusion.2
  392.5 1.8 collective-permute-start.18
  395.4 17.8 %collective-permute-done.18 = f32[2,8,1152]{2,1,0:T(8,128)S(1)} collective-permute-done((f32[2,8,1152]{2,1,0:T(8,128)S(1)}, f32[2,8,1152]{2,1,0:T(8,128)S(1)}, u32[]{:S(2)}, u32[]{:S(2)}) %collective-permute-start.18) | collective-permute-done | bytes 73760 | tf_op jit(solution)/shard_map/cond/branch_1_fun/ppermute | solution.py:1092
  414.6 1.5 collective-permute-start.19
  416.3 4.1 collective-permute-done.19
  423.1 17.2 %collective-permute-done.21 = bf16[304,512]{1,0:T(8,128)(2,1)S(1)} collective-permute-done((bf16[304,512]{1,0:T(8,128)(2,1)S(1)}, bf16[304,512]{1,0:T(8,128)(2,1)S(1)}, u32[]{:S(2)}, u32[]{:S(2)}) %collective-permute-start.21) | collective-permute-done | bytes 311328 | tf_op jit(solution)/shard_map/cond/branch_1_fun/ppermute | solution.py:1092
  442.4 9.5 %collective-permute-done.24 = bf16[192,1024]{1,0:T(8,128)(2,1)S(1)} collective-permute-done((bf16[192,1024]{1,0:T(8,128)(2,1)S(1)}, bf16[192,1024]{1,0:T(8,128)(2,1)S(1)}, u32[]{:S(2)}, u32[]{:S(2)}) %collective-permute-start.24) | collective-permute-done | bytes 393248 | tf_op jit(solution)/shard_map/cond/branch_1_fun/ppermute | solution.py:1092
  453.0 3.6 collective-permute-done.22
  456.6 1.5 maximum_select_fusion
  461.7 2.8 collective-permute-start.48
  464.4 2.1 collective-permute-start.51
  466.5 10.8 %collective-permute-done.46 = bf16[384,1024]{1,0:T(8,128)(2,1)} collective-permute-done((bf16[384,1024]{1,0:T(8,128)(2,1)}, bf16[384,1024]{1,0:T(8,128)(2,1)}, u32[]{:S(2)}, u32[]{:S(2)}) %collective-permute-start.46) | collective-permute-done | bytes 786464 | tf_op jit(solution)/shard_map/ppermute | solution.py:1092
  477.3 2.7 maximum_select_fusion.8.refs_5_
  482.6 4.9 collective-permute-done.44.refs_4_
  489.4 4.5 collective-permute-start.50
  495.7 8.8 %assemble.1 = (f32[4384,512]{1,0:T(8,128)}, f32[1024,1024]{1,0:T(8,128)}) custom-call(s32[3]{0:T(128)} %pad_add_fusion.2.scal, bf16[1216,512]{1,0:T(8,128)(2,1)} %collective-permute-done.43.refs_0_, bf16[1216,512]{1,0:T(8,128)(2,1)} %collective-permute-done.45.refs_1_, bf16[768,1024]{1,0:T(8,128)(2,1)} %collective-permute-done.47.refs_2_, ...), custom_call_target="tpu_custom_call" | custom-call | flops 6000000000 | bytes 20000000 | tf_op jit(solution)/shard_map/assemble/pallas_call | solution.py:803
  (230 shorter events, 69.9 us)
Async XLA Ops:
  7.2 242.3 %all-reduce.11.cloned.1.call-start = ((), (), s32[]{:S(2)}) async-start(), calls=%async_computation | async-start | bytes 1048576 | tf_op jit(solution)/shard_map/psum | solution.py:1299
  11.6 5.6 %copy-start.21 = (s32[2,1]{0,1:T(1,128)S(1)}, s32[2,1]{0,1:T(1,128)}, u32[]{:S(2)}) copy-start(s32[2,1]{0,1:T(1,128)} %param.17) | copy-start | bytes 28
  11.7 8.0 %collective-permute-start.30 = (bf16[1168,512]{1,0:T(8,128)(2,1)S(1)}, bf16[1168,512]{1,0:T(8,128)(2,1)S(1)}, u32[]{:S(2)}, u32[]{:S(2)}) collective-permute-start(bf16[1168,512]{1,0:T(8,128)(2,1)S(1)} %pad_maximum_fusion.1), channel_id=1, source_target_pairs={{0,16},{16,0},{1,17},{17,1},{2,18},{18,2},{3,19},{19,3},{4,20},{20... | collective-permute-start | bytes 3588104 | tf_op jit(solution)/shard_map/ppermute | solution.py:1087
  12.6 11.3 %collective-permute-start.27 = (bf16[8,1152]{1,0:T(8,128)(2,1)S(1)}, bf16[8,1152]{1,0:T(8,128)(2,1)S(1)}, u32[]{:S(2)}, u32[]{:S(2)}) collective-permute-start(bf16[8,1152]{1,0:T(8,128)(2,1)S(1)} %concatenate.152), channel_id=1, source_target_pairs={{0,16},{16,0},{1,17},{17,1},{2,18},{18,2},{3,19},{19,3},{4,20},{20... | collective-permute-start | bytes 55304 | tf_op jit(solution)/shard_map/ppermute | solution.py:1087
  13.1 48.7 %collective-permute-start.29 = (bf16[4384,512]{1,0:T(8,128)(2,1)}, bf16[4384,512]{1,0:T(8,128)(2,1)}, u32[]{:S(2)}, u32[]{:S(2)}) collective-permute-start(bf16[4384,512]{1,0:T(8,128)(2,1)} %bitcast.120), channel_id=1, source_target_pairs={{0,16},{16,0},{1,17},{17,1},{2,18},{18,2},{3,19},{19,3},{4,20},{20... | collective-permute-start | bytes 13467656 | tf_op jit(solution)/shard_map/ppermute | solution.py:1087
  14.2 44.6 %collective-permute-start.34 = (bf16[256,1024]{1,0:T(8,128)(2,1)S(1)}, bf16[256,1024]{1,0:T(8,128)(2,1)}, u32[]{:S(2)}, u32[]{:S(2)}) collective-permute-start(bf16[256,1024]{1,0:T(8,128)(2,1)S(1)} %dynamic-slice_bitcast_fusion.2), channel_id=1, source_target_pairs={{0,8},{8,0},{1,9},{9,1},{2,10},{10,2},{3,11},{11,3},{4,12},{12,4},... | collective-permute-start | bytes 1572872 | tf_op jit(solution)/shard_map/ppermute | solution.py:1087
  17.2 42.2 %collective-permute-start.33 = (bf16[1024,1024]{1,0:T(8,128)(2,1)}, bf16[1024,1024]{1,0:T(8,128)(2,1)}, u32[]{:S(2)}, u32[]{:S(2)}) collective-permute-start(bf16[1024,1024]{1,0:T(8,128)(2,1)} %bitcast.145), channel_id=1, source_target_pairs={{0,16},{16,0},{1,17},{17,1},{2,18},{18,2},{3,19},{19,3},{4,20},{20... | collective-permute-start | bytes 6291464 | tf_op jit(solution)/shard_map/ppermute | solution.py:1087
  22.3 33.5 %collective-permute-start.31 = (bf16[1168,512]{1,0:T(8,128)(2,1)}, bf16[1168,512]{1,0:T(8,128)(2,1)}, u32[]{:S(2)}, u32[]{:S(2)}) collective-permute-start(bf16[1168,512]{1,0:T(8,128)(2,1)} %get-tuple-element.361), channel_id=1, source_target_pairs={{0,8},{8,0},{1,9},{9,1},{2,10},{10,2},{3,11},{11,3},{4,12},{12,4},... | collective-permute-start | bytes 3588104 | tf_op jit(solution)/shard_map/ppermute | solution.py:1087
  23.9 31.9 %collective-permute-start.28 = (bf16[2,8,1152]{2,1,0:T(8,128)(2,1)S(1)}, bf16[2,8,1152]{2,1,0:T(8,128)(2,1)S(1)}, u32[]{:S(2)}, u32[]{:S(2)}) collective-permute-start(bf16[2,8,1152]{2,1,0:T(8,128)(2,1)S(1)} %get-tuple-element.328), channel_id=1, source_target_pairs={{0,8},{8,0},{1,9},{9,1},{2,10},{10,2},{3,11},{11,3},{4,12},{12,4},... | collective-permute-start | bytes 110600 | tf_op jit(solution)/shard_map/ppermute | solution.py:1087
  57.0 36.7 %collective-permute-start.37 = (bf16[1168,512]{1,0:T(8,128)(2,1)}, bf16[1168,512]{1,0:T(8,128)(2,1)}, u32[]{:S(2)}, u32[]{:S(2)}) collective-permute-start(bf16[1168,512]{1,0:T(8,128)(2,1)} %broadcast_select_fusion.2), channel_id=1, source_target_pairs={{0,8},{8,0},{1,9},{9,1},{2,10},{10,2},{3,11},{11,3},{4,12},{12,4},... | collective-permute-start | bytes 3588104 | tf_op jit(solution)/shard_map/ppermute | solution.py:1087
  58.7 3.1 collective-permute-start.32
  91.6 3.9 collective-permute-start.35
  91.9 14.3 %collective-permute-start.36 = (bf16[256,1024]{1,0:T(8,128)(2,1)}, bf16[256,1024]{1,0:T(8,128)(2,1)}, u32[]{:S(2)}, u32[]{:S(2)}) collective-permute-start(bf16[256,1024]{1,0:T(8,128)(2,1)} %dynamic-slice_bitcast_fusion.3.refs_12_), channel_id=1, source_target_pairs={{0,8},{8,0},{1,9},{9,1},{2,10},{10,2},{3,11},{11,3},{4,12},{12,4},... | collective-permute-start | bytes 1572872 | tf_op jit(solution)/shard_map/ppermute | solution.py:1087
  93.7 40.2 %collective-permute-start.38 = (bf16[1168,512]{1,0:T(8,128)(2,1)}, bf16[1168,512]{1,0:T(8,128)(2,1)}, u32[]{:S(2)}, u32[]{:S(2)}) collective-permute-start(bf16[1168,512]{1,0:T(8,128)(2,1)} %collective-permute-done.37.refs_5_), channel_id=1, source_target_pairs={{0,16},{16,0},{1,17},{17,1},{2,18},{18,2},{3,19},{19,3},{4,20},{20... | collective-permute-start | bytes 3588104 | tf_op jit(solution)/shard_map/ppermute | solution.py:1087
  108.0 24.4 %collective-permute-start.39 = (f16[512,1024]{1,0:T(8,128)(2,1)S(1)}, f16[512,1024]{1,0:T(8,128)(2,1)S(1)}, u32[]{:S(2)}, u32[]{:S(2)}) collective-permute-start(f16[512,1024]{1,0:T(8,128)(2,1)S(1)} %convert_element_type.170), channel_id=1, source_target_pairs={{0,8},{8,0},{1,9},{9,1},{2,10},{10,2},{3,11},{11,3},{4,12},{12,4},... | collective-permute-start | bytes 3145736 | tf_op jit(solution)/shard_map/ppermute | solution.py:1087
  163.9 3.8 copy-start.8
  163.9 3.8 collective-permute-start.40
  167.1 2.9 collective-permute-start.42
  167.9 5.7 %copy-start.4 = (bf16[512,1024]{1,0:T(8,128)(2,1)}, bf16[512,1024]{1,0:T(8,128)(2,1)S(1)}, u32[]{:S(2)}) copy-start(bf16[512,1024]{1,0:T(8,128)(2,1)S(1)} %multiply_convert_fusion) | copy-start | bytes 3145732
  168.0 3.5 collective-permute-start.41
  176.2 283.4 %all-reduce.13.cloned.1.call-start = ((), (), s32[]{:S(2)}) async-start(), calls=%async_computation.1 | async-start | bytes 4980736 | tf_op jit(solution)/shard_map/psum | solution.py:1312
  217.8 7.5 %collective-permute-start.1 = (bf16[512,2432]{1,0:T(8,128)(2,1)}, bf16[512,2432]{1,0:T(8,128)(2,1)S(1)}, u32[]{:S(2)}, u32[]{:S(2)}) collective-permute-start(bf16[512,2432]{1,0:T(8,128)(2,1)} %get-tuple-element.158), channel_id=1, source_target_pairs={{0,16},{16,0},{1,17},{17,1},{2,18},{18,2},{3,19},{19,3},{4,20},{20... | collective-permute-start | bytes 7471112 | tf_op jit(solution)/shard_map/cond/branch_1_fun/ppermute | solution.py:1087
  218.0 6.2 %collective-permute-start.2 = (bf16[512,1024]{1,0:T(8,128)(2,1)}, bf16[512,1024]{1,0:T(8,128)(2,1)}, u32[]{:S(2)}, u32[]{:S(2)}) collective-permute-start(bf16[512,1024]{1,0:T(8,128)(2,1)} %get-tuple-element.159), channel_id=1, source_target_pairs={{0,16},{16,0},{1,17},{17,1},{2,18},{18,2},{3,19},{19,3},{4,20},{20... | collective-permute-start | bytes 3145736 | tf_op jit(solution)/shard_map/cond/branch_1_fun/ppermute | solution.py:1087
  218.4 25.5 %collective-permute-start = (bf16[512,1024]{1,0:T(8,128)(2,1)}, bf16[512,1024]{1,0:T(8,128)(2,1)}, u32[]{:S(2)}, u32[]{:S(2)}) collective-permute-start(bf16[512,1024]{1,0:T(8,128)(2,1)} %get-tuple-element.399), channel_id=1, source_target_pairs={{0,8},{8,0},{1,9},{9,1},{2,10},{10,2},{3,11},{11,3},{4,12},{12,4},... | collective-permute-start | bytes 3145736 | tf_op jit(solution)/shard_map/cond/branch_1_fun/ppermute | solution.py:1087
  295.1 15.1 %collective-permute-start.3 = (bf16[512,2432]{1,0:T(8,128)(2,1)}, bf16[512,2432]{1,0:T(8,128)(2,1)S(1)}, u32[]{:S(2)}, u32[]{:S(2)}) collective-permute-start(bf16[512,2432]{1,0:T(8,128)(2,1)} %get-tuple-element.187), channel_id=1, source_target_pairs={{0,16},{16,0},{1,17},{17,1},{2,18},{18,2},{3,19},{19,3},{4,20},{20... | collective-permute-start | bytes 7471112 | tf_op jit(solution)/shard_map/cond/branch_1_fun/ppermute | solution.py:1087
  295.2 8.9 %collective-permute-start.4 = (bf16[512,1024]{1,0:T(8,128)(2,1)}, bf16[512,1024]{1,0:T(8,128)(2,1)}, u32[]{:S(2)}, u32[]{:S(2)}) collective-permute-start(bf16[512,1024]{1,0:T(8,128)(2,1)} %get-tuple-element.188), channel_id=1, source_target_pairs={{0,16},{16,0},{1,17},{17,1},{2,18},{18,2},{3,19},{19,3},{4,20},{20... | collective-permute-start | bytes 3145736 | tf_op jit(solution)/shard_map/cond/branch_1_fun/ppermute | solution.py:1087
  295.7 9.5 %collective-permute-start.5 = (bf16[512,1024]{1,0:T(8,128)(2,1)}, bf16[512,1024]{1,0:T(8,128)(2,1)}, u32[]{:S(2)}, u32[]{:S(2)}) collective-permute-start(bf16[512,1024]{1,0:T(8,128)(2,1)} %get-tuple-element.190), channel_id=1, source_target_pairs={{0,16},{16,0},{1,17},{17,1},{2,18},{18,2},{3,19},{19,3},{4,20},{20... | collective-permute-start | bytes 3145736 | tf_op jit(solution)/shard_map/cond/branch_1_fun/ppermute | solution.py:1087
  295.7 9.4 %collective-permute-start.6 = (bf16[512,1024]{1,0:T(8,128)(2,1)}, bf16[512,1024]{1,0:T(8,128)(2,1)}, u32[]{:S(2)}, u32[]{:S(2)}) collective-permute-start(bf16[512,1024]{1,0:T(8,128)(2,1)} %get-tuple-element.223), channel_id=1, source_target_pairs={{0,16},{16,0},{1,17},{17,1},{2,18},{18,2},{3,19},{19,3},{4,20},{20... | collective-permute-start | bytes 3145736 | tf_op jit(solution)/shard_map/cond/branch_1_fun/ppermute | solution.py:1087
  311.7 4.0 copy-start.5
  311.7 4.0 copy-start.22
  313.0 10.9 %collective-permute-start.11 = (f32[2,16,1280]{2,1,0:T(8,128)S(1)}, f32[2,16,1280]{2,1,0:T(8,128)S(1)}, u32[]{:S(2)}, u32[]{:S(2)}) collective-permute-start(f32[2,16,1280]{2,1,0:T(8,128)S(1)} %pad_maximum_fusion), channel_id=1, source_target_pairs={{0,16},{16,0},{1,17},{17,1},{2,18},{18,2},{3,19},{19,3},{4,20},{20... | collective-permute-start | bytes 491528 | tf_op jit(solution)/shard_map/cond/branch_1_fun/ppermute | solution.py:1087
  314.2 32.3 %collective-permute-start.9 = (bf16[256,1024]{1,0:T(8,128)(2,1)}, bf16[256,1024]{1,0:T(8,128)(2,1)S(1)}, u32[]{:S(2)}, u32[]{:S(2)}) collective-permute-start(bf16[256,1024]{1,0:T(8,128)(2,1)} %constant_dynamic-slice_fusion.7), channel_id=1, source_target_pairs={{0,8},{8,0},{1,9},{9,1},{2,10},{10,2},{3,11},{11,3},{4,12},{12,4},... | collective-permute-start | bytes 1572872 | tf_op jit(solution)/shard_map/cond/branch_1_fun/ppermute | solution.py:1087
  320.0 38.5 %copy-start.2 = (bf16[384,1024]{1,0:T(8,128)(2,1)S(1)}, bf16[384,1024]{1,0:T(8,128)(2,1)}, u32[]{:S(2)}) copy-start(bf16[384,1024]{1,0:T(8,128)(2,1)} %get-tuple-element.207) | copy-start | bytes 2359300 | tf_op jit(solution)/shard_map/cond
  320.9 25.7 %collective-permute-start.10 = (bf16[256,1024]{1,0:T(8,128)(2,1)}, bf16[256,1024]{1,0:T(8,128)(2,1)}, u32[]{:S(2)}, u32[]{:S(2)}) collective-permute-start(bf16[256,1024]{1,0:T(8,128)(2,1)} %dynamic-slice_convert_fusion), channel_id=1, source_target_pairs={{0,8},{8,0},{1,9},{9,1},{2,10},{10,2},{3,11},{11,3},{4,12},{12,4},... | collective-permute-start | bytes 1572872 | tf_op jit(solution)/shard_map/cond/branch_1_fun/ppermute | solution.py:1087
  321.5 34.0 %collective-permute-start.8 = (bf16[384,1024]{1,0:T(8,128)(2,1)}, bf16[384,1024]{1,0:T(8,128)(2,1)}, u32[]{:S(2)}, u32[]{:S(2)}) collective-permute-start(bf16[384,1024]{1,0:T(8,128)(2,1)} %get-tuple-element.198), channel_id=1, source_target_pairs={{0,2},{1,3},{2,0},{3,1},{4,6},{5,7},{6,4},{7,5},{8,10},{9,11},{10,... | collective-permute-start | bytes 2359304 | tf_op jit(solution)/shard_map/cond/branch_1_fun/ppermute | solution.py:1092
  322.4 36.1 %collective-permute-start.7 = (bf16[1216,512]{1,0:T(8,128)(2,1)}, bf16[1216,512]{1,0:T(8,128)(2,1)}, u32[]{:S(2)}, u32[]{:S(2)}) collective-permute-start(bf16[1216,512]{1,0:T(8,128)(2,1)} %get-tuple-element.197), channel_id=1, source_target_pairs={{0,1},{1,0},{2,3},{3,2},{4,5},{5,4},{6,7},{7,6},{8,9},{9,8},{10,11... | collective-permute-start | bytes 3735560 | tf_op jit(solution)/shard_map/cond/branch_1_fun/ppermute | solution.py:1092
  327.9 15.5 %collective-permute-start.12 = (f32[2,16,1280]{2,1,0:T(8,128)}, f32[2,16,1280]{2,1,0:T(8,128)}, u32[]{:S(2)}, u32[]{:S(2)}) collective-permute-start(f32[2,16,1280]{2,1,0:T(8,128)} %fusion.38), channel_id=1, source_target_pairs={{0,8},{8,0},{1,9},{9,1},{2,10},{10,2},{3,11},{11,3},{4,12},{12,4},... | collective-permute-start | bytes 491528 | tf_op jit(solution)/shard_map/cond/branch_1_fun/ppermute | solution.py:1087
  360.7 4.6 copy-start.12
  360.7 4.6 copy-start.13
  360.7 24.0 %collective-permute-start.14 = (bf16[192,1024]{1,0:T(8,128)(2,1)}, bf16[192,1024]{1,0:T(8,128)(2,1)}, u32[]{:S(2)}, u32[]{:S(2)}) collective-permute-start(bf16[192,1024]{1,0:T(8,128)(2,1)} %get-tuple-element.337), channel_id=1, source_target_pairs={{0,1},{1,0},{2,3},{3,2},{4,5},{5,4},{6,7},{7,6},{8,9},{9,8},{10,11... | collective-permute-start | bytes 1179656 | tf_op jit(solution)/shard_map/cond/branch_1_fun/ppermute | solution.py:1092
  364.8 2.4 copy-start.1
  364.8 19.8 %collective-permute-start.13 = (bf16[608,512]{1,0:T(8,128)(2,1)}, bf16[608,512]{1,0:T(8,128)(2,1)}, u32[]{:S(2)}, u32[]{:S(2)}) collective-permute-start(bf16[608,512]{1,0:T(8,128)(2,1)} %get-tuple-element.333), channel_id=1, source_target_pairs={{0,2},{1,3},{2,0},{3,1},{4,6},{5,7},{6,4},{7,5},{8,10},{9,11},{10,... | collective-permute-start | bytes 1867784 | tf_op jit(solution)/shard_map/cond/branch_1_fun/ppermute | solution.py:1092
  368.7 21.4 %collective-permute-start.26 = (bf16[256,1024]{1,0:T(8,128)(2,1)}, bf16[256,1024]{1,0:T(8,128)(2,1)}, u32[]{:S(2)}, u32[]{:S(2)}) collective-permute-start(bf16[256,1024]{1,0:T(8,128)(2,1)} %broadcast_select_fusion), channel_id=1, source_target_pairs={{0,16},{16,0},{1,17},{17,1},{2,18},{18,2},{3,19},{19,3},{4,20},{20... | collective-permute-start | bytes 1572872 | tf_op jit(solution)/shard_map/cond/branch_1_fun/ppermute | solution.py:1087
  369.7 24.6 %collective-permute-start.25 = (bf16[256,1024]{1,0:T(8,128)(2,1)}, bf16[256,1024]{1,0:T(8,128)(2,1)S(1)}, u32[]{:S(2)}, u32[]{:S(2)}) collective-permute-start(bf16[256,1024]{1,0:T(8,128)(2,1)} %broadcast_select_fusion.1), channel_id=1, source_target_pairs={{0,16},{16,0},{1,17},{17,1},{2,18},{18,2},{3,19},{19,3},{4,20},{20... | collective-permute-start | bytes 1572872 | tf_op jit(solution)/shard_map/cond/branch_1_fun/ppermute | solution.py:1087
  370.2 14.4 %collective-permute-start.15 = (f32[2,8,1152]{2,1,0:T(8,128)S(1)}, f32[2,8,1152]{2,1,0:T(8,128)S(1)}, u32[]{:S(2)}, u32[]{:S(2)}) collective-permute-start(f32[2,8,1152]{2,1,0:T(8,128)S(1)} %fusion.31), channel_id=1, source_target_pairs={{0,2},{1,3},{2,0},{3,1},{4,6},{5,7},{6,4},{7,5},{8,10},{9,11},{10,... | collective-permute-start | bytes 221192 | tf_op jit(solution)/shard_map/cond/branch_1_fun/ppermute | solution.py:1092
  385.9 27.3 %collective-permute-start.16 = (bf16[304,512]{1,0:T(8,128)(2,1)S(1)}, bf16[304,512]{1,0:T(8,128)(2,1)S(1)}, u32[]{:S(2)}, u32[]{:S(2)}) collective-permute-start(bf16[304,512]{1,0:T(8,128)(2,1)S(1)} %get-tuple-element.341), channel_id=1, source_target_pairs={{0,4},{1,5},{2,6},{3,7},{4,0},{5,1},{6,2},{7,3},{8,12},{9,13},{10,... | collective-permute-start | bytes 933896 | tf_op jit(solution)/shard_map/cond/branch_1_fun/ppermute | solution.py:1092
  388.9 24.3 %collective-permute-start.17 = (bf16[96,1024]{1,0:T(8,128)(2,1)S(1)}, bf16[96,1024]{1,0:T(8,128)(2,1)S(1)}, u32[]{:S(2)}, u32[]{:S(2)}) collective-permute-start(bf16[96,1024]{1,0:T(8,128)(2,1)S(1)} %get-tuple-element.347), channel_id=1, source_target_pairs={{0,4},{1,5},{2,6},{3,7},{4,0},{5,1},{6,2},{7,3},{8,12},{9,13},{10,... | collective-permute-start | bytes 589832 | tf_op jit(solution)/shard_map/cond/branch_1_fun/ppermute | solution.py:1092
  392.5 20.7 %collective-permute-start.18 = (f32[2,8,1152]{2,1,0:T(8,128)S(1)}, f32[2,8,1152]{2,1,0:T(8,128)S(1)}, u32[]{:S(2)}, u32[]{:S(2)}) collective-permute-start(f32[2,8,1152]{2,1,0:T(8,128)S(1)} %add.213), channel_id=1, source_target_pairs={{0,4},{1,5},{2,6},{3,7},{4,0},{5,1},{6,2},{7,3},{8,12},{9,13},{10,... | collective-permute-start | bytes 221192 | tf_op jit(solution)/shard_map/cond/branch_1_fun/ppermute | solution.py:1092
  413.2 7.3 %collective-permute-start.20 = (f32[2,8,1152]{2,1,0:T(8,128)S(1)}, f32[2,8,1152]{2,1,0:T(8,128)S(1)}, u32[]{:S(2)}, u32[]{:S(2)}) collective-permute-start(f32[2,8,1152]{2,1,0:T(8,128)S(1)} %add.222), channel_id=1, source_target_pairs={{0,1},{1,0},{2,3},{3,2},{4,5},{5,4},{6,7},{7,6},{8,9},{9,8},{10,11... | collective-permute-start | bytes 221192 | tf_op jit(solution)/shard_map/cond/branch_1_fun/ppermute | solution.py:1092
  414.6 5.7 %collective-permute-start.19 = (bf16[304,256]{1,0:T(8,128)(2,1)S(1)}, bf16[304,256]{1,0:T(8,128)(2,1)S(1)}, u32[]{:S(2)}, u32[]{:S(2)}) collective-permute-start(bf16[304,256]{1,0:T(8,128)(2,1)S(1)} %get-tuple-element.350), channel_id=1, source_target_pairs={{0,8},{8,0},{1,9},{9,1},{2,10},{10,2},{3,11},{11,3},{4,12},{12,4},... | collective-permute-start | bytes 466952 | tf_op jit(solution)/shard_map/cond/branch_1_fun/ppermute | solution.py:1087
  416.2 24.5 %collective-permute-start.23 = (bf16[96,1024]{1,0:T(8,128)(2,1)S(1)}, bf16[96,1024]{1,0:T(8,128)(2,1)S(1)}, u32[]{:S(2)}, u32[]{:S(2)}) collective-permute-start(bf16[96,1024]{1,0:T(8,128)(2,1)S(1)} %add_convert_fusion.9), channel_id=1, source_target_pairs={{0,4},{1,5},{2,6},{3,7},{4,0},{5,1},{6,2},{7,3},{8,12},{9,13},{10,... | collective-permute-start | bytes 589832 | tf_op jit(solution)/shard_map/cond/branch_1_fun/ppermute | solution.py:1092
  420.6 19.8 %collective-permute-start.21 = (bf16[304,512]{1,0:T(8,128)(2,1)S(1)}, bf16[304,512]{1,0:T(8,128)(2,1)S(1)}, u32[]{:S(2)}, u32[]{:S(2)}) collective-permute-start(bf16[304,512]{1,0:T(8,128)(2,1)S(1)} %maximum_select_fusion.6), channel_id=1, source_target_pairs={{0,4},{1,5},{2,6},{3,7},{4,0},{5,1},{6,2},{7,3},{8,12},{9,13},{10,... | collective-permute-start | bytes 933896 | tf_op jit(solution)/shard_map/cond/branch_1_fun/ppermute | solution.py:1092
  440.6 16.0 %collective-permute-start.22 = (bf16[608,512]{1,0:T(8,128)(2,1)S(1)}, bf16[608,512]{1,0:T(8,128)(2,1)S(1)}, u32[]{:S(2)}, u32[]{:S(2)}) collective-permute-start(bf16[608,512]{1,0:T(8,128)(2,1)S(1)} %maximum_select_fusion.4), channel_id=1, source_target_pairs={{0,2},{1,3},{2,0},{3,1},{4,6},{5,7},{6,4},{7,5},{8,10},{9,11},{10,... | collective-permute-start | bytes 1867784 | tf_op jit(solution)/shard_map/cond/branch_1_fun/ppermute | solution.py:1092
  440.7 11.1 %collective-permute-start.24 = (bf16[192,1024]{1,0:T(8,128)(2,1)S(1)}, bf16[192,1024]{1,0:T(8,128)(2,1)S(1)}, u32[]{:S(2)}, u32[]{:S(2)}) collective-permute-start(bf16[192,1024]{1,0:T(8,128)(2,1)S(1)} %maximum_select_fusion.5), channel_id=1, source_target_pairs={{0,1},{1,0},{2,3},{3,2},{4,5},{5,4},{6,7},{7,6},{8,9},{9,8},{10,11... | collective-permute-start | bytes 1179656 | tf_op jit(solution)/shard_map/cond/branch_1_fun/ppermute | solution.py:1092
  458.3 6.1 %copy-start.25 = (bf16[256,1024]{1,0:T(8,128)(2,1)S(1)}, bf16[256,1024]{1,0:T(8,128)(2,1)}, u32[]{:S(2)}) copy-start(bf16[256,1024]{1,0:T(8,128)(2,1)} %all-reduce.11.cloned.1.call-done.refs_10_) | copy-start | bytes 1572868
  458.3 19.0 %collective-permute-start.46 = (bf16[384,1024]{1,0:T(8,128)(2,1)}, bf16[384,1024]{1,0:T(8,128)(2,1)}, u32[]{:S(2)}, u32[]{:S(2)}) collective-permute-start(bf16[384,1024]{1,0:T(8,128)(2,1)} %get-tuple-element.302), channel_id=1, source_target_pairs={{0,2},{1,3},{2,0},{3,1},{4,6},{5,7},{6,4},{7,5},{8,10},{9,11},{10,... | collective-permute-start | bytes 2359304 | tf_op jit(solution)/shard_map/ppermute | solution.py:1092
  458.6 28.8 %collective-permute-start.44 = (bf16[1216,512]{1,0:T(8,128)(2,1)}, bf16[1216,512]{1,0:T(8,128)(2,1)}, u32[]{:S(2)}, u32[]{:S(2)}) collective-permute-start(bf16[1216,512]{1,0:T(8,128)(2,1)} %get-tuple-element.301.refs_3_), channel_id=1, source_target_pairs={{0,1},{1,0},{2,3},{3,2},{4,5},{5,4},{6,7},{7,6},{8,9},{9,8},{10,11... | collective-permute-start | bytes 3735560 | tf_op jit(solution)/shard_map/ppermute | solution.py:1092
  461.0 28.4 %collective-permute-start.49 = (bf16[2432,256]{1,0:T(8,128)(2,1)S(1)}, bf16[2432,256]{1,0:T(8,128)(2,1)}, u32[]{:S(2)}, u32[]{:S(2)}) collective-permute-start(bf16[2432,256]{1,0:T(8,128)(2,1)S(1)} %constant_dynamic-slice_fusion.14), channel_id=1, source_target_pairs={{0,8},{8,0},{1,9},{9,1},{2,10},{10,2},{3,11},{11,3},{4,12},{12,4},... | collective-permute-start | bytes 3735560 | tf_op jit(solution)/shard_map/ppermute | solution.py:1087
  461.7 34.1 %collective-permute-start.48 = (bf16[2432,512]{1,0:T(8,128)(2,1)}, bf16[2432,512]{1,0:T(8,128)(2,1)}, u32[]{:S(2)}, u32[]{:S(2)}) collective-permute-start(bf16[2432,512]{1,0:T(8,128)(2,1)} %all-reduce.13.cloned.1.call-done.refs_6_), channel_id=1, source_target_pairs={{0,16},{1,17},{2,18},{3,19},{4,20},{5,21},{6,22},{7,23},{8,24},{9,... | collective-permute-start | bytes 7471112 | tf_op jit(solution)/shard_map/ppermute | solution.py:1325
  464.4 16.9 %collective-permute-start.51 = (bf16[256,1024]{1,0:T(8,128)(2,1)S(1)}, bf16[256,1024]{1,0:T(8,128)(2,1)}, u32[]{:S(2)}, u32[]{:S(2)}) collective-permute-start(bf16[256,1024]{1,0:T(8,128)(2,1)S(1)} %copy-done.25), channel_id=1, source_target_pairs={{0,16},{1,17},{2,18},{3,19},{4,20},{5,21},{6,22},{7,23},{8,24},{9,... | collective-permute-start | bytes 1572872 | tf_op jit(solution)/shard_map/ppermute | solution.py:1325
  481.3 14.4 %collective-permute-start.47 = (bf16[768,1024]{1,0:T(8,128)(2,1)S(1)}, bf16[768,1024]{1,0:T(8,128)(2,1)}, u32[]{:S(2)}, u32[]{:S(2)}) collective-permute-start(bf16[768,1024]{1,0:T(8,128)(2,1)S(1)} %maximum_select_fusion.8.refs_5_), channel_id=1, source_target_pairs={{0,16},{16,0},{1,17},{17,1},{2,18},{18,2},{3,19},{19,3},{4,20},{20... | collective-permute-start | bytes 4718600 | tf_op jit(solution)/shard_map/ppermute | solution.py:1087
  481.3 14.4 %collective-permute-start.43 = (bf16[1216,512]{1,0:T(8,128)(2,1)}, bf16[1216,512]{1,0:T(8,128)(2,1)}, u32[]{:S(2)}, u32[]{:S(2)}) collective-permute-start(bf16[1216,512]{1,0:T(8,128)(2,1)} %get-tuple-element.301.refs_3_), channel_id=1, source_target_pairs={{16,0},{17,1},{18,2},{19,3},{20,4},{21,5},{22,6},{23,7},{24,8},{25... | collective-permute-start | bytes 3735560 | tf_op jit(solution)/shard_map/ppermute | solution.py:1325
  487.4 8.3 %collective-permute-start.45 = (bf16[1216,512]{1,0:T(8,128)(2,1)}, bf16[1216,512]{1,0:T(8,128)(2,1)}, u32[]{:S(2)}, u32[]{:S(2)}) collective-permute-start(bf16[1216,512]{1,0:T(8,128)(2,1)} %collective-permute-done.44.refs_4_), channel_id=1, source_target_pairs={{16,0},{17,1},{18,2},{19,3},{20,4},{21,5},{22,6},{23,7},{24,8},{25... | collective-permute-start | bytes 3735560 | tf_op jit(solution)/shard_map/ppermute | solution.py:1325
  489.4 6.3 %collective-permute-start.50 = (bf16[2432,256]{1,0:T(8,128)(2,1)}, bf16[2432,256]{1,0:T(8,128)(2,1)}, u32[]{:S(2)}, u32[]{:S(2)}) collective-permute-start(bf16[2432,256]{1,0:T(8,128)(2,1)} %collective-permute-done.49.refs_8_), channel_id=1, source_target_pairs={{0,16},{1,17},{2,18},{3,19},{4,20},{5,21},{6,22},{7,23},{8,24},{9,... | collective-permute-start | bytes 3735560 | tf_op jit(solution)/shard_map/ppermute | solution.py:1325
  (17 other events, 20.7 us)
Sparse Core Ops, SparseCore 0:
  176.3 73.0 all-reduce.10
  254.1 118.4 all-reduce.12

commit v3 on v2

--- a/solution.py
+++ b/solution.py
@@ -107,16 +107,26 @@
     return both[:rows] + both[rows:]
 
 
-def fill_masks(mask_s, bound, count):
-    rows = mask_s.shape[1]
-    pos = iota((rows, LANE), 0)
+def seam(bound, back, rows, align, count):
+    first = jnp.clip(bound - back, 0, count - rows)
+    return pl.multiple_of(first - lax.rem(first, align), align)
+
+
+def seam_masks(first, rows, bound):
+    pos = iota((rows, LANE), 0) + first
+    masks = []
     for lag in range(1, KW):
         anchor = pos - lag
-        dropped = (anchor < 0) | ((anchor < bound) & (bound <= pos)) | (pos >= count)
-        mask_s[lag - 1] = jnp.where(dropped, 0.0, 1.0)
-
-
-def conv_phase(proj_s, par, mask_s, conv_s, pre_s, count):
+        dropped = (anchor < 0) | ((anchor < bound) & (bound <= pos))
+        masks.append(jnp.where(dropped, 0.0, 1.0))
+    return masks
+
+
+def conv_phase(proj_s, par, bound, conv_s, pre_s, count):
+    first = seam(bound, 0, 16, 8, count)
+    masks = seam_masks(first, 16, bound)
+    seam_rows = pl.ds(first, 16)
+
     def body(index):
         src = pl.ds(pl.multiple_of(DH + index * LANE, LANE), LANE)
         dst = tile_at(index, LANE)
@@ -125,11 +135,18 @@
             pre = taps[4:5] + taps[3:4] * proj_s[HEAD_ROWS + at : HEAD_ROWS + at + 64, src]
             for lag in range(1, KW):
                 begin = HEAD_ROWS + at - lag
-                part = proj_s[begin : begin + 64, src] * mask_s[lag - 1, at : at + 64]
-                pre = pre + taps[3 - lag : 4 - lag] * part
+                pre = pre + taps[3 - lag : 4 - lag] * proj_s[begin : begin + 64, src]
             if pre_s is not None:
                 pre_s[at : at + 64, dst] = pre
             conv_s[at : at + 64, dst] = pre * sigmoid(pre)
+        window = proj_s[pl.ds(first, 16 + HEAD_ROWS), src]
+        pre = taps[4:5] + taps[3:4] * window[HEAD_ROWS:]
+        for lag in range(1, KW):
+            part = window[HEAD_ROWS - lag : HEAD_ROWS - lag + 16] * masks[lag - 1]
+            pre = pre + taps[3 - lag : 4 - lag] * part
+        if pre_s is not None:
+            pre_s[seam_rows, dst] = pre
+        conv_s[seam_rows, dst] = pre * sigmoid(pre)
 
     loop(CH // LANE, body)
 
@@ -302,7 +319,7 @@
         u_prev, p_own, p_far, in_own, in_far = refs[9:14]
         rest = refs[14:]
     (u_out, proj_out, ys_out, st_out, mix_out, sum_out, stat_out) = rest[:7]
-    (w_s, wo_s, u_s, n_s, proj_s, conv_s, mask_s, dt_s, rate_s, cs_s, cst_s, xdt_s,
+    (w_s, wo_s, u_s, n_s, proj_s, conv_s, dt_s, rate_s, cs_s, cst_s, xdt_s,
      y_s, mix_s, st_s, pp_s, g_s, spread_s, stat_s, hold_s, in_s, xlo_s, sems) = rest[7:]
     sec, grp, bound = scal[0], scal[1], scal[2]
     count = u_s.shape[0]
@@ -326,7 +343,6 @@
         for copy in token_in:
             copy.start()
         wo_in = load_outer(layer, sec, wo_a, wo_b, wo_s, sems.at[4])
-    fill_masks(mask_s, bound, count)
     fill_spread(spread_s, HDIM)
     proj_s[0:HEAD_ROWS] = jnp.zeros((HEAD_ROWS, CP), f32)
     gain_in = par[6:7, :DM]
@@ -370,7 +386,7 @@
     out_proj = pltpu.make_async_copy(proj_s, proj_out, sems.at[14])
     out_proj.start()
 
-    conv_phase(proj_s, par, mask_s, conv_s, None, count)
+    conv_phase(proj_s, par, bound, conv_s, None, count)
     step_phase(proj_s, hp, dt_s, rate_s, cs_s, cst_s, count)
     scaled_inputs(conv_s, dt_s, spread_s, xdt_s, xlo_s, count)
 
@@ -479,7 +495,7 @@
         p_sum, up_in, dn_own, dn_far, par_up = refs[17:22]
         rest = refs[22:]
     (n_out, dp_out, gated_out, g_out, dn_out, small_out) = rest[:6]
-    (w_s, wo_s, u_s, n_s, proj_s, conv_s, pre_s, mask_s, dt_s, rate_s, cs_s, cst_s, grad_cs_s, xdt_s,
+    (w_s, wo_s, u_s, n_s, proj_s, conv_s, pre_s, dt_s, rate_s, cs_s, cst_s, grad_cs_s, xdt_s,
      y_s, st_s, ad_s, pp_s, dn_s, g_s, up_s, gg_s, dys_s, dx_s, dpre_s, dp_s, gm_s, dg_s,
      spread_s, gather_s, stat_s, hold_s, xlo_s, dlo_s, sems) = rest[6:]
     sec, grp, bound = scal[0], scal[1], scal[2]
@@ -508,7 +524,6 @@
     wo_in = load_outer(layer, sec, wo_a, wo_b, wo_s, sems.at[4])
     for copy in saved_in[1:]:
         copy.start()
-    fill_masks(mask_s, bound, count)
     fill_spread(spread_s, HDIM)
     fill_gather(gather_s)
     stats = column_of(stat_own, hold_s) + column_of(stat_far, hold_s)
@@ -548,7 +563,7 @@
     w_in = load_weights(layer, sec, grp, w_a, w_b, w_x, w_y, w_s, sems)
     saved_in[0].start()
 
-    conv_phase(proj_s, par, mask_s, conv_s, pre_s, count)
+    conv_phase(proj_s, par, bound, conv_s, pre_s, count)
     step_phase(proj_s, hp, dt_s, rate_s, cs_s, cst_s, count)
     scaled_inputs(conv_s, dt_s, spread_s, xdt_s, xlo_s, count)
 
@@ -701,6 +716,11 @@
 
     dpre_s[count : count + 8] = jnp.zeros((8, CH), f32)
 
+    first = seam(bound, 0, 16, 8, count)
+    masks = seam_masks(first, 16, bound)
+    back = seam(bound, KW - 1, 32, 16, count)
+    back_masks = seam_masks(back, 40, bound)
+
     def conv_back(index):
         src = pl.ds(pl.multiple_of(DH + index * LANE, LANE), LANE)
         dst = tile_at(index, LANE)
@@ -714,17 +734,24 @@
             sums[4] = sums[4] + fold(grad)
             for lag in range(KW):
                 begin = HEAD_ROWS + at - lag
-                part = proj_s[begin : begin + 64, src]
-                if lag:
-                    part = part * mask_s[lag - 1, at : at + 64]
-                sums[3 - lag] = sums[3 - lag] + fold(grad * part)
+                sums[3 - lag] = sums[3 - lag] + fold(grad * proj_s[begin : begin + 64, src])
+        window = proj_s[pl.ds(first, 16 + HEAD_ROWS), src]
+        grad = dpre_s[pl.ds(first, 16), dst]
+        for lag in range(1, KW):
+            part = window[HEAD_ROWS - lag : HEAD_ROWS - lag + 16] * (1.0 - masks[lag - 1])
+            sums[3 - lag] = sums[3 - lag] - fold(grad * part)
         for at in range(0, count, 64):
             total = taps[3:4] * dpre_s[at : at + 64, dst]
             for lag in range(1, KW):
                 begin = at + lag
-                part = dpre_s[begin : begin + 64, dst] * mask_s[lag - 1, begin : begin + 64]
-                total = total + taps[3 - lag : 4 - lag] * part
+                total = total + taps[3 - lag : 4 - lag] * dpre_s[begin : begin + 64, dst]
             dp_s[at : at + 64, src] = total.astype(bf16)
+        window = dpre_s[pl.ds(back, 40), dst]
+        total = taps[3:4] * window[:32]
+        for lag in range(1, KW):
+            part = window[lag : lag + 32] * back_masks[lag - 1][lag : lag + 32]
+            total = total + taps[3 - lag : 4 - lag] * part
+        dp_s[pl.ds(back, 32), src] = total.astype(bf16)
         for at in range(KW + 1):
             small_out[at : at + 1, dst] = jnp.sum(sums[at], axis=0, keepdims=True)
 
@@ -845,7 +872,6 @@
         vm((count, DM), bf16),
         vm((count + HEAD_ROWS, CP), f32),
         vm((count, CH), f32),
-        vm((KW - 1, count + 8, LANE), f32),
         vm((count, LANE), f32),
         vm((count, LANE), f32),
         vm((count, LANE), f32),
@@ -1042,7 +1068,6 @@
         vm((count + HEAD_ROWS, CP), f32),
         vm((count, CH), f32),
         vm((count, CH), f32),
-        vm((KW - 1, count + 8, LANE), f32),
         vm((count, LANE), f32),
         vm((count, LANE), f32),
         vm((count, LANE), f32),

time: 519 us -> 518 us (level)
  Pallas kernels: 159 us -> 153 us
    pallas_call x6, Pallas kernels: 159 us -> 153 us  [call(): pl.pallas_call(kernel, in_specs=specs, out_specs=out_specs, out_shape=[ja...]
where the time goes in v3:
time: 518 us; the launch traced here: 511 us
  waiting for transfers between devices  197 us (38%)
  Pallas kernels  153 us (30%)
  starting transfers between devices  48.5 us (9%)
  other arithmetic  39.2 us (8%)
  local copies, waits for them, and re-layouts  36.8 us (7%)
  matrix products  19.3 us (4%)
  between operations  15.4 us (3%)
    pallas_call x6, Pallas kernels, call(): pl.pallas_call(kernel, in_specs=specs, out_specs=out_specs, out_shape=[ja...  153 us
    ppermute x32, waiting for transfers between devices, swap(): return lax.ppermute(block, axis, [(0, 1), (1, 0)])  97.9 us
    ppermute x15, waiting for transfers between devices, flip(): lax.ppermute(block, 'replica', [(at, at ^ mask) for at in range(size)])  91.6 us
    ppermute x32, starting transfers between devices, swap(): return lax.ppermute(block, axis, [(0, 1), (1, 0)])  21.9 us
    dot_general x8, matrix products, tn(): lax.dot_general(left, right, (((0,), (0,)), ((), ())), preferred_element_...  16.4 us
    ppermute x15, starting transfers between devices, flip(): lax.ppermute(block, 'replica', [(at, at ^ mask) for at in range(size)])  14.9 us
    ppermute x5, starting transfers between devices, to_owner(): return lax.ppermute(block, 'section', [(1 - layer, layer)])  11.7 us
    select_n x10, other arithmetic, in_order(): jnp.where(which == 0, jnp.concatenate([mine, other], axis=dim), jnp.conca...  11.4 us
  transfers between devices with their start and end apart: 54, of which 23 were waited for; matrix products, arithmetic and copies ran while one was open for 16% of the time, Pallas kernels for 23%

profile of v3, /device:TPU:0, one launch (start us, length us, event | category | flops | bytes accessed | tf_op | source)
XLA Modules:
  0.0 511.2 jit_solution(15539343465609073080)
XLA Ops:
  9.0 2.7 dynamic-slice_bitcast_fusion
  14.2 3.0 collective-permute-start.34
  17.8 1.9 dynamic-slice_bitcast_fusion.3.refs_12_
  19.7 2.6 broadcast_select_fusion.3
  23.9 1.9 collective-permute-start.28
  26.1 29.7 %collective-permute-done.28 = bf16[2,8,1152]{2,1,0:T(8,128)(2,1)S(1)} collective-permute-done((bf16[2,8,1152]{2,1,0:T(8,128)(2,1)S(1)}, bf16[2,8,1152]{2,1,0:T(8,128)(2,1)S(1)}, u32[]{:S(2)}, u32[]{:S(2)}) %collective-permute-start.28) | collective-permute-done | bytes 36896 | tf_op jit(solution)/shard_map/ppermute | solution.py:1112
  57.0 1.7 collective-permute-start.37
  59.4 2.4 collective-permute-done.32
  62.9 27.9 %conditional.3 = (bf16[512,1024]{1,0:T(8,128)(2,1)}, f32[520,2432]{1,0:T(8,128)}, f32[512,1024]{1,0:T(8,128)}, f32[128,1024]{1,0:T(8,128)}, f32[512,1024]{1,0:T(8,128)}, /*index=5*/f32[8,512]{1,0:T(8,128)S(1)}) conditional(s32[]{:T(128)} %bitcast.12, () %tuple.48, (s32[3]{0:T(128)S(1)}, f32[8,1280]{1,0:T(8,128)S(1)}, f32[8,128]{1,0:T(8,128)S(1)}, ...), branch_computations={%region_0.1_spmd, %region_1.2_spmd} | conditional | flops 35000000512 | bytes 24784204 | solution.py:1296
  63.9 26.6 %forward_0.1 = (bf16[512,1024]{1,0:T(8,128)(2,1)}, f32[520,2432]{1,0:T(8,128)}, f32[512,1024]{1,0:T(8,128)}, f32[128,1024]{1,0:T(8,128)}, f32[512,1024]{1,0:T(8,...) custom-call(s32[3]{0:T(128)S(1)} %get-tuple-element.123.refs_0_, f32[8,1280]{1,0:T(8,128)S(1)} %get-tuple-element.124.refs_1_, ...), custom_call_target="tpu_custom_call" | custom-call | flops 35000000512 | bytes 20000000 | tf_op jit(solution)/shard_map/cond/branch_1_fun/forward_0/pallas_call | solution.py:830
  91.2 1.7 collective-permute-start.36
  92.9 1.8 collective-permute-done.35.stat_far
  94.7 6.3 %project_0.1.refs_10_ = f32[512,1024]{1,0:T(8,128)} custom-call(s32[3]{0:T(128)S(1)} %pad_add_fusion.scal.refs_0_, f32[8,1280]{1,0:T(8,128)S(1)} %pad_maximum_fusion.3.par, bf16[1024,1024]{1,0:T(8,128)(2,1)} %bitcast.147, bf16[1024,1024]{1,0:T(8,128)(2,1)} %collective-permute-done.33.wo_b.refs_8_, f32[8,512]{1,0:T(8,128)S(1)} %get-tuple-element.279.stat_own, ...), custom_call_target="tpu_custom_call" | custom-call | flops 6000000000 | bytes 20000000 | tf_op jit(solution)/shard_map/project_0/pallas_call | solution.py:830
  101.0 4.4 collective-permute-done.36.refs_13_
  105.4 1.8 convert_element_type.170
  107.2 1.6 collective-permute-start.39
  109.0 22.5 %collective-permute-done.39 = f16[512,1024]{1,0:T(8,128)(2,1)S(1)} collective-permute-done((f16[512,1024]{1,0:T(8,128)(2,1)S(1)}, f16[512,1024]{1,0:T(8,128)(2,1)S(1)}, u32[]{:S(2)}, u32[]{:S(2)}) %collective-permute-start.39) | collective-permute-done | bytes 1048608 | tf_op jit(solution)/shard_map/ppermute | solution.py:1112
  131.5 1.5 convert_element_type.171.refs_11_
  133.1 29.2 %forward_1.1 = (bf16[512,1024]{1,0:T(8,128)(2,1)}, f32[520,2432]{1,0:T(8,128)}, f32[512,1024]{1,0:T(8,128)}, f32[128,1024]{1,0:T(8,128)}, f32[512,1024]{1,0:T(8,...) custom-call(s32[3]{0:T(128)S(1)} %pad_add_fusion.scal.refs_0_, f32[8,1280]{1,0:T(8,128)S(1)} %pad_maximum_fusion.4.refs_1_, ...), custom_call_target="tpu_custom_call" | custom-call | flops 35000000512 | bytes 20000000 | tf_op jit(solution)/shard_map/forward_1/pallas_call | solution.py:830
  163.7 2.0 maximum_select_fusion.9
  166.6 1.9 collective-permute-done.42
  168.5 1.5 collective-permute-done.41
  170.0 2.1 fusion.39
  174.8 65.5 %conditional.4 = (bf16[512,1024]{1,0:T(8,128)(2,1)}, bf16[512,1024]{1,0:T(8,128)(2,1)}, bf16[2432,512]{1,0:T(8,128)(2,1)}, f32[16,1280]{1,0:T(8,128)}) conditional(s32[]{:T(128)} %bitcast.12, () %tuple.51, (s32[3]{0:T(128)S(1)}, f32[8,1280]{1,0:T(8,128)S(1)}, f32[8,128]{1,0:T(8,128)S(1)}, bf16[4384,512]{1,0:T(8,128)(2,1)}, ...), branch_computations={%region_2.3_spmd, %region_3.4_spmd} | conditional | flops 57554722816 | bytes 58928640 | solution.py:1296
  175.0 39.1 %backward_1.1 = (bf16[512,1024]{1,0:T(8,128)(2,1)}, bf16[512,2432]{1,0:T(8,128)(2,1)}, bf16[512,1024]{1,0:T(8,128)(2,1)}, bf16[512,1024]{1,0:T(8,128)(2,1)}, bf1...) custom-call(s32[3]{0:T(128)S(1)} %get-tuple-element.140.refs_0_, f32[8,1280]{1,0:T(8,128)S(1)} %get-tuple-element.141.refs_1_, ...), custom_call_target="tpu_custom_call" | custom-call | flops 54999998464 | bytes 20000000 | tf_op jit(solution)/shard_map/cond/branch_1_fun/backward_1/pallas_call | solution.py:830
  216.6 3.2 fusion.1
  221.7 2.9 fusion
  224.6 15.7 %collective-permute-done = bf16[512,1024]{1,0:T(8,128)(2,1)} collective-permute-done((bf16[512,1024]{1,0:T(8,128)(2,1)}, bf16[512,1024]{1,0:T(8,128)(2,1)}, u32[]{:S(2)}, u32[]{:S(2)}) %collective-permute-start) | collective-permute-done | bytes 1048608 | tf_op jit(solution)/shard_map/cond/branch_1_fun/ppermute | solution.py:1112
  240.3 7.7 %all-reduce.11.cloned.1.call-done.refs_10_ = bf16[256,1024]{1,0:T(8,128)(2,1)} async-done(((bf16[256,1024]{1,0:T(8,128)(2,1)}), bf16[256,1024]{1,0:T(8,128)(2,1)}) %all-reduce.11.cloned.1.call-update) | async-done | bytes 524304 | tf_op jit(solution)/shard_map/psum | solution.py:1324
  248.0 209.8 %conditional.5 = (f32[1,512]{1,0:T(1,128)}, f32[4,1152]{1,0:T(4,128)}, f32[1,1152]{1,0:T(1,128)}, f32[3,16]{1,0:T(4,128)}, f32[1,1024]{1,0:T(1,128)}, /*index=5*...) conditional(s32[]{:T(128)} %bitcast.12, () %tuple.46, ...), branch_computations={%region_4.5_spmd, %region_5.9_spmd} | conditional | flops 59740913664 | bytes 217801312 | solution.py:1296
  248.5 43.0 %backward_0.1 = (bf16[512,1024]{1,0:T(8,128)(2,1)}, bf16[512,2432]{1,0:T(8,128)(2,1)}, bf16[512,1024]{1,0:T(8,128)(2,1)}, bf16[512,1024]{1,0:T(8,128)(2,1)}, bf1...) custom-call(s32[3]{0:T(128)S(1)} %get-tuple-element.165.refs_0_, f32[8,1280]{1,0:T(8,128)S(1)} %get-tuple-element.166.refs_1_, ...), custom_call_target="tpu_custom_call" | custom-call | flops 54999998464 | bytes 20000000 | tf_op jit(solution)/shard_map/cond/branch_1_fun/backward_0/pallas_call | solution.py:830
  296.6 2.3 fusion.28
  298.9 1.5 fusion.20
  301.6 2.1 add_convert_fusion
  303.7 2.9 fusion.18
  306.6 1.5 fusion.10
  312.1 2.9 fusion.11
  318.7 1.5 collective-permute-start.7
  320.9 1.5 slice_reduce_fusion
  324.2 1.5 collective-permute-start.12
  327.9 11.9 %collective-permute-done.12 = f32[2,16,1280]{2,1,0:T(8,128)} collective-permute-done((f32[2,16,1280]{2,1,0:T(8,128)}, f32[2,16,1280]{2,1,0:T(8,128)}, u32[]{:S(2)}, u32[]{:S(2)}) %collective-permute-start.12) | collective-permute-done | bytes 163872 | tf_op jit(solution)/shard_map/cond/branch_1_fun/ppermute | solution.py:1112
  343.0 7.1 %collective-permute-done.8 = bf16[384,1024]{1,0:T(8,128)(2,1)} collective-permute-done((bf16[384,1024]{1,0:T(8,128)(2,1)}, bf16[384,1024]{1,0:T(8,128)(2,1)}, u32[]{:S(2)}, u32[]{:S(2)}) %collective-permute-start.8) | collective-permute-done | bytes 786464 | tf_op jit(solution)/shard_map/cond/branch_1_fun/ppermute | solution.py:1117
  350.1 6.0 %collective-permute-done.7 = bf16[1216,512]{1,0:T(8,128)(2,1)} collective-permute-done((bf16[1216,512]{1,0:T(8,128)(2,1)}, bf16[1216,512]{1,0:T(8,128)(2,1)}, u32[]{:S(2)}, u32[]{:S(2)}) %collective-permute-start.7) | collective-permute-done | bytes 1245216 | tf_op jit(solution)/shard_map/cond/branch_1_fun/ppermute | solution.py:1117
  356.1 2.2 add_convert_fusion.4
  358.9 2.7 add_convert_fusion.1
  361.6 1.5 collective-permute-start.13
  368.5 15.3 %collective-permute-done.15 = f32[2,8,1152]{2,1,0:T(8,128)S(1)} collective-permute-done((f32[2,8,1152]{2,1,0:T(8,128)S(1)}, f32[2,8,1152]{2,1,0:T(8,128)S(1)}, u32[]{:S(2)}, u32[]{:S(2)}) %collective-permute-start.15) | collective-permute-done | bytes 73760 | tf_op jit(solution)/shard_map/cond/branch_1_fun/ppermute | solution.py:1117
  385.0 2.8 collective-permute-start.16
  389.3 2.4 maximum_select_fusion.2
  391.6 2.8 collective-permute-start.18
  395.6 17.4 %collective-permute-done.18 = f32[2,8,1152]{2,1,0:T(8,128)S(1)} collective-permute-done((f32[2,8,1152]{2,1,0:T(8,128)S(1)}, f32[2,8,1152]{2,1,0:T(8,128)S(1)}, u32[]{:S(2)}, u32[]{:S(2)}) %collective-permute-start.18) | collective-permute-done | bytes 73760 | tf_op jit(solution)/shard_map/cond/branch_1_fun/ppermute | solution.py:1117
  413.9 1.5 collective-permute-start.19
  415.6 4.0 collective-permute-done.19
  422.3 17.6 %collective-permute-done.21 = bf16[304,512]{1,0:T(8,128)(2,1)S(1)} collective-permute-done((bf16[304,512]{1,0:T(8,128)(2,1)S(1)}, bf16[304,512]{1,0:T(8,128)(2,1)S(1)}, u32[]{:S(2)}, u32[]{:S(2)}) %collective-permute-start.21) | collective-permute-done | bytes 311328 | tf_op jit(solution)/shard_map/cond/branch_1_fun/ppermute | solution.py:1117
  442.2 9.2 %collective-permute-done.24 = bf16[192,1024]{1,0:T(8,128)(2,1)S(1)} collective-permute-done((bf16[192,1024]{1,0:T(8,128)(2,1)S(1)}, bf16[192,1024]{1,0:T(8,128)(2,1)S(1)}, u32[]{:S(2)}, u32[]{:S(2)}) %collective-permute-start.24) | collective-permute-done | bytes 393248 | tf_op jit(solution)/shard_map/cond/branch_1_fun/ppermute | solution.py:1117
  452.6 3.6 collective-permute-done.22
  456.1 1.5 maximum_select_fusion
  461.4 2.8 collective-permute-start.48
  464.2 2.1 collective-permute-start.51
  466.3 10.5 %collective-permute-done.46 = bf16[384,1024]{1,0:T(8,128)(2,1)} collective-permute-done((bf16[384,1024]{1,0:T(8,128)(2,1)}, bf16[384,1024]{1,0:T(8,128)(2,1)}, u32[]{:S(2)}, u32[]{:S(2)}) %collective-permute-start.46) | collective-permute-done | bytes 786464 | tf_op jit(solution)/shard_map/ppermute | solution.py:1117
  476.9 2.7 maximum_select_fusion.8.refs_5_
  482.1 4.9 collective-permute-done.44.refs_4_
  489.2 4.2 collective-permute-start.50
  495.3 8.8 %assemble.1 = (f32[4384,512]{1,0:T(8,128)}, f32[1024,1024]{1,0:T(8,128)}) custom-call(s32[3]{0:T(128)} %pad_add_fusion.2.scal, bf16[1216,512]{1,0:T(8,128)(2,1)} %collective-permute-done.43.refs_0_, bf16[1216,512]{1,0:T(8,128)(2,1)} %collective-permute-done.45.refs_1_, bf16[768,1024]{1,0:T(8,128)(2,1)} %collective-permute-done.47.refs_2_, ...), custom_call_target="tpu_custom_call" | custom-call | flops 6000000000 | bytes 20000000 | tf_op jit(solution)/shard_map/assemble/pallas_call | solution.py:830
  (230 shorter events, 68.4 us)
Async XLA Ops:
  7.2 240.8 %all-reduce.11.cloned.1.call-start = ((), (), s32[]{:S(2)}) async-start(), calls=%async_computation | async-start | bytes 1048576 | tf_op jit(solution)/shard_map/psum | solution.py:1324
  11.6 5.6 %copy-start.21 = (s32[2,1]{0,1:T(1,128)S(1)}, s32[2,1]{0,1:T(1,128)}, u32[]{:S(2)}) copy-start(s32[2,1]{0,1:T(1,128)} %param.17) | copy-start | bytes 28
  11.7 8.0 %collective-permute-start.30 = (bf16[1168,512]{1,0:T(8,128)(2,1)S(1)}, bf16[1168,512]{1,0:T(8,128)(2,1)S(1)}, u32[]{:S(2)}, u32[]{:S(2)}) collective-permute-start(bf16[1168,512]{1,0:T(8,128)(2,1)S(1)} %pad_maximum_fusion.1), channel_id=1, source_target_pairs={{0,16},{16,0},{1,17},{17,1},{2,18},{18,2},{3,19},{19,3},{4,20},{20... | collective-permute-start | bytes 3588104 | tf_op jit(solution)/shard_map/ppermute | solution.py:1112
  12.6 11.3 %collective-permute-start.27 = (bf16[8,1152]{1,0:T(8,128)(2,1)S(1)}, bf16[8,1152]{1,0:T(8,128)(2,1)S(1)}, u32[]{:S(2)}, u32[]{:S(2)}) collective-permute-start(bf16[8,1152]{1,0:T(8,128)(2,1)S(1)} %concatenate.152), channel_id=1, source_target_pairs={{0,16},{16,0},{1,17},{17,1},{2,18},{18,2},{3,19},{19,3},{4,20},{20... | collective-permute-start | bytes 55304 | tf_op jit(solution)/shard_map/ppermute | solution.py:1112
  13.1 48.7 %collective-permute-start.29 = (bf16[4384,512]{1,0:T(8,128)(2,1)}, bf16[4384,512]{1,0:T(8,128)(2,1)}, u32[]{:S(2)}, u32[]{:S(2)}) collective-permute-start(bf16[4384,512]{1,0:T(8,128)(2,1)} %bitcast.120), channel_id=1, source_target_pairs={{0,16},{16,0},{1,17},{17,1},{2,18},{18,2},{3,19},{19,3},{4,20},{20... | collective-permute-start | bytes 13467656 | tf_op jit(solution)/shard_map/ppermute | solution.py:1112
  14.2 44.6 %collective-permute-start.34 = (bf16[256,1024]{1,0:T(8,128)(2,1)S(1)}, bf16[256,1024]{1,0:T(8,128)(2,1)}, u32[]{:S(2)}, u32[]{:S(2)}) collective-permute-start(bf16[256,1024]{1,0:T(8,128)(2,1)S(1)} %dynamic-slice_bitcast_fusion.2), channel_id=1, source_target_pairs={{0,8},{8,0},{1,9},{9,1},{2,10},{10,2},{3,11},{11,3},{4,12},{12,4},... | collective-permute-start | bytes 1572872 | tf_op jit(solution)/shard_map/ppermute | solution.py:1112
  17.2 42.2 %collective-permute-start.33 = (bf16[1024,1024]{1,0:T(8,128)(2,1)}, bf16[1024,1024]{1,0:T(8,128)(2,1)}, u32[]{:S(2)}, u32[]{:S(2)}) collective-permute-start(bf16[1024,1024]{1,0:T(8,128)(2,1)} %bitcast.145), channel_id=1, source_target_pairs={{0,16},{16,0},{1,17},{17,1},{2,18},{18,2},{3,19},{19,3},{4,20},{20... | collective-permute-start | bytes 6291464 | tf_op jit(solution)/shard_map/ppermute | solution.py:1112
  22.3 33.5 %collective-permute-start.31 = (bf16[1168,512]{1,0:T(8,128)(2,1)}, bf16[1168,512]{1,0:T(8,128)(2,1)}, u32[]{:S(2)}, u32[]{:S(2)}) collective-permute-start(bf16[1168,512]{1,0:T(8,128)(2,1)} %get-tuple-element.361), channel_id=1, source_target_pairs={{0,8},{8,0},{1,9},{9,1},{2,10},{10,2},{3,11},{11,3},{4,12},{12,4},... | collective-permute-start | bytes 3588104 | tf_op jit(solution)/shard_map/ppermute | solution.py:1112
  23.9 31.9 %collective-permute-start.28 = (bf16[2,8,1152]{2,1,0:T(8,128)(2,1)S(1)}, bf16[2,8,1152]{2,1,0:T(8,128)(2,1)S(1)}, u32[]{:S(2)}, u32[]{:S(2)}) collective-permute-start(bf16[2,8,1152]{2,1,0:T(8,128)(2,1)S(1)} %get-tuple-element.328), channel_id=1, source_target_pairs={{0,8},{8,0},{1,9},{9,1},{2,10},{10,2},{3,11},{11,3},{4,12},{12,4},... | collective-permute-start | bytes 110600 | tf_op jit(solution)/shard_map/ppermute | solution.py:1112
  57.0 35.9 %collective-permute-start.37 = (bf16[1168,512]{1,0:T(8,128)(2,1)}, bf16[1168,512]{1,0:T(8,128)(2,1)}, u32[]{:S(2)}, u32[]{:S(2)}) collective-permute-start(bf16[1168,512]{1,0:T(8,128)(2,1)} %broadcast_select_fusion.2), channel_id=1, source_target_pairs={{0,8},{8,0},{1,9},{9,1},{2,10},{10,2},{3,11},{11,3},{4,12},{12,4},... | collective-permute-start | bytes 3588104 | tf_op jit(solution)/shard_map/ppermute | solution.py:1112
  58.7 3.1 collective-permute-start.32
  90.8 3.9 collective-permute-start.35
  91.2 14.2 %collective-permute-start.36 = (bf16[256,1024]{1,0:T(8,128)(2,1)}, bf16[256,1024]{1,0:T(8,128)(2,1)}, u32[]{:S(2)}, u32[]{:S(2)}) collective-permute-start(bf16[256,1024]{1,0:T(8,128)(2,1)} %dynamic-slice_bitcast_fusion.3.refs_12_), channel_id=1, source_target_pairs={{0,8},{8,0},{1,9},{9,1},{2,10},{10,2},{3,11},{11,3},{4,12},{12,4},... | collective-permute-start | bytes 1572872 | tf_op jit(solution)/shard_map/ppermute | solution.py:1112
  92.9 40.2 %collective-permute-start.38 = (bf16[1168,512]{1,0:T(8,128)(2,1)}, bf16[1168,512]{1,0:T(8,128)(2,1)}, u32[]{:S(2)}, u32[]{:S(2)}) collective-permute-start(bf16[1168,512]{1,0:T(8,128)(2,1)} %collective-permute-done.37.refs_5_), channel_id=1, source_target_pairs={{0,16},{16,0},{1,17},{17,1},{2,18},{18,2},{3,19},{19,3},{4,20},{20... | collective-permute-start | bytes 3588104 | tf_op jit(solution)/shard_map/ppermute | solution.py:1112
  107.2 24.4 %collective-permute-start.39 = (f16[512,1024]{1,0:T(8,128)(2,1)S(1)}, f16[512,1024]{1,0:T(8,128)(2,1)S(1)}, u32[]{:S(2)}, u32[]{:S(2)}) collective-permute-start(f16[512,1024]{1,0:T(8,128)(2,1)S(1)} %convert_element_type.170), channel_id=1, source_target_pairs={{0,8},{8,0},{1,9},{9,1},{2,10},{10,2},{3,11},{11,3},{4,12},{12,4},... | collective-permute-start | bytes 3145736 | tf_op jit(solution)/shard_map/ppermute | solution.py:1112
  162.3 3.8 copy-start.8
  162.3 3.8 collective-permute-start.40
  165.6 2.9 collective-permute-start.42
  166.4 5.7 %copy-start.4 = (bf16[512,1024]{1,0:T(8,128)(2,1)}, bf16[512,1024]{1,0:T(8,128)(2,1)S(1)}, u32[]{:S(2)}) copy-start(bf16[512,1024]{1,0:T(8,128)(2,1)S(1)} %multiply_convert_fusion) | copy-start | bytes 3145732
  166.4 3.6 collective-permute-start.41
  174.7 284.7 %all-reduce.13.cloned.1.call-start = ((), (), s32[]{:S(2)}) async-start(), calls=%async_computation.1 | async-start | bytes 4980736 | tf_op jit(solution)/shard_map/psum | solution.py:1337
  214.2 7.5 %collective-permute-start.1 = (bf16[512,2432]{1,0:T(8,128)(2,1)}, bf16[512,2432]{1,0:T(8,128)(2,1)S(1)}, u32[]{:S(2)}, u32[]{:S(2)}) collective-permute-start(bf16[512,2432]{1,0:T(8,128)(2,1)} %get-tuple-element.158), channel_id=1, source_target_pairs={{0,16},{16,0},{1,17},{17,1},{2,18},{18,2},{3,19},{19,3},{4,20},{20... | collective-permute-start | bytes 7471112 | tf_op jit(solution)/shard_map/cond/branch_1_fun/ppermute | solution.py:1112
  214.4 6.2 %collective-permute-start.2 = (bf16[512,1024]{1,0:T(8,128)(2,1)}, bf16[512,1024]{1,0:T(8,128)(2,1)}, u32[]{:S(2)}, u32[]{:S(2)}) collective-permute-start(bf16[512,1024]{1,0:T(8,128)(2,1)} %get-tuple-element.159), channel_id=1, source_target_pairs={{0,16},{16,0},{1,17},{17,1},{2,18},{18,2},{3,19},{19,3},{4,20},{20... | collective-permute-start | bytes 3145736 | tf_op jit(solution)/shard_map/cond/branch_1_fun/ppermute | solution.py:1112
  214.8 25.5 %collective-permute-start = (bf16[512,1024]{1,0:T(8,128)(2,1)}, bf16[512,1024]{1,0:T(8,128)(2,1)}, u32[]{:S(2)}, u32[]{:S(2)}) collective-permute-start(bf16[512,1024]{1,0:T(8,128)(2,1)} %get-tuple-element.399), channel_id=1, source_target_pairs={{0,8},{8,0},{1,9},{9,1},{2,10},{10,2},{3,11},{11,3},{4,12},{12,4},... | collective-permute-start | bytes 3145736 | tf_op jit(solution)/shard_map/cond/branch_1_fun/ppermute | solution.py:1112
  291.5 15.1 %collective-permute-start.3 = (bf16[512,2432]{1,0:T(8,128)(2,1)}, bf16[512,2432]{1,0:T(8,128)(2,1)S(1)}, u32[]{:S(2)}, u32[]{:S(2)}) collective-permute-start(bf16[512,2432]{1,0:T(8,128)(2,1)} %get-tuple-element.187), channel_id=1, source_target_pairs={{0,16},{16,0},{1,17},{17,1},{2,18},{18,2},{3,19},{19,3},{4,20},{20... | collective-permute-start | bytes 7471112 | tf_op jit(solution)/shard_map/cond/branch_1_fun/ppermute | solution.py:1112
  291.6 8.9 %collective-permute-start.4 = (bf16[512,1024]{1,0:T(8,128)(2,1)}, bf16[512,1024]{1,0:T(8,128)(2,1)}, u32[]{:S(2)}, u32[]{:S(2)}) collective-permute-start(bf16[512,1024]{1,0:T(8,128)(2,1)} %get-tuple-element.188), channel_id=1, source_target_pairs={{0,16},{16,0},{1,17},{17,1},{2,18},{18,2},{3,19},{19,3},{4,20},{20... | collective-permute-start | bytes 3145736 | tf_op jit(solution)/shard_map/cond/branch_1_fun/ppermute | solution.py:1112
  292.1 9.5 %collective-permute-start.5 = (bf16[512,1024]{1,0:T(8,128)(2,1)}, bf16[512,1024]{1,0:T(8,128)(2,1)}, u32[]{:S(2)}, u32[]{:S(2)}) collective-permute-start(bf16[512,1024]{1,0:T(8,128)(2,1)} %get-tuple-element.190), channel_id=1, source_target_pairs={{0,16},{16,0},{1,17},{17,1},{2,18},{18,2},{3,19},{19,3},{4,20},{20... | collective-permute-start | bytes 3145736 | tf_op jit(solution)/shard_map/cond/branch_1_fun/ppermute | solution.py:1112
  292.2 9.4 %collective-permute-start.6 = (bf16[512,1024]{1,0:T(8,128)(2,1)}, bf16[512,1024]{1,0:T(8,128)(2,1)}, u32[]{:S(2)}, u32[]{:S(2)}) collective-permute-start(bf16[512,1024]{1,0:T(8,128)(2,1)} %get-tuple-element.223), channel_id=1, source_target_pairs={{0,16},{16,0},{1,17},{17,1},{2,18},{18,2},{3,19},{19,3},{4,20},{20... | collective-permute-start | bytes 3145736 | tf_op jit(solution)/shard_map/cond/branch_1_fun/ppermute | solution.py:1112
  308.1 4.0 copy-start.5
  308.2 4.0 copy-start.22
  309.4 10.8 %collective-permute-start.11 = (f32[2,16,1280]{2,1,0:T(8,128)S(1)}, f32[2,16,1280]{2,1,0:T(8,128)S(1)}, u32[]{:S(2)}, u32[]{:S(2)}) collective-permute-start(f32[2,16,1280]{2,1,0:T(8,128)S(1)} %pad_maximum_fusion), channel_id=1, source_target_pairs={{0,16},{16,0},{1,17},{17,1},{2,18},{18,2},{3,19},{19,3},{4,20},{20... | collective-permute-start | bytes 491528 | tf_op jit(solution)/shard_map/cond/branch_1_fun/ppermute | solution.py:1112
  310.7 32.3 %collective-permute-start.9 = (bf16[256,1024]{1,0:T(8,128)(2,1)}, bf16[256,1024]{1,0:T(8,128)(2,1)S(1)}, u32[]{:S(2)}, u32[]{:S(2)}) collective-permute-start(bf16[256,1024]{1,0:T(8,128)(2,1)} %constant_dynamic-slice_fusion.7), channel_id=1, source_target_pairs={{0,8},{8,0},{1,9},{9,1},{2,10},{10,2},{3,11},{11,3},{4,12},{12,4},... | collective-permute-start | bytes 1572872 | tf_op jit(solution)/shard_map/cond/branch_1_fun/ppermute | solution.py:1112
  316.4 39.7 %copy-start.2 = (bf16[384,1024]{1,0:T(8,128)(2,1)S(1)}, bf16[384,1024]{1,0:T(8,128)(2,1)}, u32[]{:S(2)}) copy-start(bf16[384,1024]{1,0:T(8,128)(2,1)} %get-tuple-element.207) | copy-start | bytes 2359300 | tf_op jit(solution)/shard_map/cond
  317.3 25.7 %collective-permute-start.10 = (bf16[256,1024]{1,0:T(8,128)(2,1)}, bf16[256,1024]{1,0:T(8,128)(2,1)}, u32[]{:S(2)}, u32[]{:S(2)}) collective-permute-start(bf16[256,1024]{1,0:T(8,128)(2,1)} %dynamic-slice_convert_fusion), channel_id=1, source_target_pairs={{0,8},{8,0},{1,9},{9,1},{2,10},{10,2},{3,11},{11,3},{4,12},{12,4},... | collective-permute-start | bytes 1572872 | tf_op jit(solution)/shard_map/cond/branch_1_fun/ppermute | solution.py:1112
  317.8 32.3 %collective-permute-start.8 = (bf16[384,1024]{1,0:T(8,128)(2,1)}, bf16[384,1024]{1,0:T(8,128)(2,1)}, u32[]{:S(2)}, u32[]{:S(2)}) collective-permute-start(bf16[384,1024]{1,0:T(8,128)(2,1)} %get-tuple-element.198), channel_id=1, source_target_pairs={{0,2},{1,3},{2,0},{3,1},{4,6},{5,7},{6,4},{7,5},{8,10},{9,11},{10,... | collective-permute-start | bytes 2359304 | tf_op jit(solution)/shard_map/cond/branch_1_fun/ppermute | solution.py:1117
  318.7 37.4 %collective-permute-start.7 = (bf16[1216,512]{1,0:T(8,128)(2,1)}, bf16[1216,512]{1,0:T(8,128)(2,1)}, u32[]{:S(2)}, u32[]{:S(2)}) collective-permute-start(bf16[1216,512]{1,0:T(8,128)(2,1)} %get-tuple-element.197), channel_id=1, source_target_pairs={{0,1},{1,0},{2,3},{3,2},{4,5},{5,4},{6,7},{7,6},{8,9},{9,8},{10,11... | collective-permute-start | bytes 3735560 | tf_op jit(solution)/shard_map/cond/branch_1_fun/ppermute | solution.py:1117
  324.2 15.6 %collective-permute-start.12 = (f32[2,16,1280]{2,1,0:T(8,128)}, f32[2,16,1280]{2,1,0:T(8,128)}, u32[]{:S(2)}, u32[]{:S(2)}) collective-permute-start(f32[2,16,1280]{2,1,0:T(8,128)} %fusion.38), channel_id=1, source_target_pairs={{0,8},{8,0},{1,9},{9,1},{2,10},{10,2},{3,11},{11,3},{4,12},{12,4},... | collective-permute-start | bytes 491528 | tf_op jit(solution)/shard_map/cond/branch_1_fun/ppermute | solution.py:1112
  358.3 4.9 copy-start.12
  358.3 4.9 copy-start.13
  358.3 25.5 %collective-permute-start.14 = (bf16[192,1024]{1,0:T(8,128)(2,1)}, bf16[192,1024]{1,0:T(8,128)(2,1)}, u32[]{:S(2)}, u32[]{:S(2)}) collective-permute-start(bf16[192,1024]{1,0:T(8,128)(2,1)} %get-tuple-element.337), channel_id=1, source_target_pairs={{0,1},{1,0},{2,3},{3,2},{4,5},{5,4},{6,7},{7,6},{8,9},{9,8},{10,11... | collective-permute-start | bytes 1179656 | tf_op jit(solution)/shard_map/cond/branch_1_fun/ppermute | solution.py:1117
  361.6 3.3 copy-start.1
  361.6 22.2 %collective-permute-start.13 = (bf16[608,512]{1,0:T(8,128)(2,1)}, bf16[608,512]{1,0:T(8,128)(2,1)}, u32[]{:S(2)}, u32[]{:S(2)}) collective-permute-start(bf16[608,512]{1,0:T(8,128)(2,1)} %get-tuple-element.333), channel_id=1, source_target_pairs={{0,2},{1,3},{2,0},{3,1},{4,6},{5,7},{6,4},{7,5},{8,10},{9,11},{10,... | collective-permute-start | bytes 1867784 | tf_op jit(solution)/shard_map/cond/branch_1_fun/ppermute | solution.py:1117
  366.4 22.9 %collective-permute-start.26 = (bf16[256,1024]{1,0:T(8,128)(2,1)}, bf16[256,1024]{1,0:T(8,128)(2,1)}, u32[]{:S(2)}, u32[]{:S(2)}) collective-permute-start(bf16[256,1024]{1,0:T(8,128)(2,1)} %broadcast_select_fusion), channel_id=1, source_target_pairs={{0,16},{16,0},{1,17},{17,1},{2,18},{18,2},{3,19},{19,3},{4,20},{20... | collective-permute-start | bytes 1572872 | tf_op jit(solution)/shard_map/cond/branch_1_fun/ppermute | solution.py:1112
  367.4 27.0 %collective-permute-start.25 = (bf16[256,1024]{1,0:T(8,128)(2,1)}, bf16[256,1024]{1,0:T(8,128)(2,1)S(1)}, u32[]{:S(2)}, u32[]{:S(2)}) collective-permute-start(bf16[256,1024]{1,0:T(8,128)(2,1)} %broadcast_select_fusion.1), channel_id=1, source_target_pairs={{0,16},{16,0},{1,17},{17,1},{2,18},{18,2},{3,19},{19,3},{4,20},{20... | collective-permute-start | bytes 1572872 | tf_op jit(solution)/shard_map/cond/branch_1_fun/ppermute | solution.py:1112
  367.9 15.9 %collective-permute-start.15 = (f32[2,8,1152]{2,1,0:T(8,128)S(1)}, f32[2,8,1152]{2,1,0:T(8,128)S(1)}, u32[]{:S(2)}, u32[]{:S(2)}) collective-permute-start(f32[2,8,1152]{2,1,0:T(8,128)S(1)} %fusion.31), channel_id=1, source_target_pairs={{0,2},{1,3},{2,0},{3,1},{4,6},{5,7},{6,4},{7,5},{8,10},{9,11},{10,... | collective-permute-start | bytes 221192 | tf_op jit(solution)/shard_map/cond/branch_1_fun/ppermute | solution.py:1117
  385.0 28.0 %collective-permute-start.16 = (bf16[304,512]{1,0:T(8,128)(2,1)S(1)}, bf16[304,512]{1,0:T(8,128)(2,1)S(1)}, u32[]{:S(2)}, u32[]{:S(2)}) collective-permute-start(bf16[304,512]{1,0:T(8,128)(2,1)S(1)} %get-tuple-element.341), channel_id=1, source_target_pairs={{0,4},{1,5},{2,6},{3,7},{4,0},{5,1},{6,2},{7,3},{8,12},{9,13},{10,... | collective-permute-start | bytes 933896 | tf_op jit(solution)/shard_map/cond/branch_1_fun/ppermute | solution.py:1117
  389.0 24.0 %collective-permute-start.17 = (bf16[96,1024]{1,0:T(8,128)(2,1)S(1)}, bf16[96,1024]{1,0:T(8,128)(2,1)S(1)}, u32[]{:S(2)}, u32[]{:S(2)}) collective-permute-start(bf16[96,1024]{1,0:T(8,128)(2,1)S(1)} %get-tuple-element.347), channel_id=1, source_target_pairs={{0,4},{1,5},{2,6},{3,7},{4,0},{5,1},{6,2},{7,3},{8,12},{9,13},{10,... | collective-permute-start | bytes 589832 | tf_op jit(solution)/shard_map/cond/branch_1_fun/ppermute | solution.py:1117
  391.6 21.4 %collective-permute-start.18 = (f32[2,8,1152]{2,1,0:T(8,128)S(1)}, f32[2,8,1152]{2,1,0:T(8,128)S(1)}, u32[]{:S(2)}, u32[]{:S(2)}) collective-permute-start(f32[2,8,1152]{2,1,0:T(8,128)S(1)} %add.213), channel_id=1, source_target_pairs={{0,4},{1,5},{2,6},{3,7},{4,0},{5,1},{6,2},{7,3},{8,12},{9,13},{10,... | collective-permute-start | bytes 221192 | tf_op jit(solution)/shard_map/cond/branch_1_fun/ppermute | solution.py:1117
  413.0 6.6 %collective-permute-start.20 = (f32[2,8,1152]{2,1,0:T(8,128)S(1)}, f32[2,8,1152]{2,1,0:T(8,128)S(1)}, u32[]{:S(2)}, u32[]{:S(2)}) collective-permute-start(f32[2,8,1152]{2,1,0:T(8,128)S(1)} %add.222), channel_id=1, source_target_pairs={{0,1},{1,0},{2,3},{3,2},{4,5},{5,4},{6,7},{7,6},{8,9},{9,8},{10,11... | collective-permute-start | bytes 221192 | tf_op jit(solution)/shard_map/cond/branch_1_fun/ppermute | solution.py:1117
  413.9 5.6 %collective-permute-start.19 = (bf16[304,256]{1,0:T(8,128)(2,1)S(1)}, bf16[304,256]{1,0:T(8,128)(2,1)S(1)}, u32[]{:S(2)}, u32[]{:S(2)}) collective-permute-start(bf16[304,256]{1,0:T(8,128)(2,1)S(1)} %get-tuple-element.350), channel_id=1, source_target_pairs={{0,8},{8,0},{1,9},{9,1},{2,10},{10,2},{3,11},{11,3},{4,12},{12,4},... | collective-permute-start | bytes 466952 | tf_op jit(solution)/shard_map/cond/branch_1_fun/ppermute | solution.py:1112
  415.5 24.7 %collective-permute-start.23 = (bf16[96,1024]{1,0:T(8,128)(2,1)S(1)}, bf16[96,1024]{1,0:T(8,128)(2,1)S(1)}, u32[]{:S(2)}, u32[]{:S(2)}) collective-permute-start(bf16[96,1024]{1,0:T(8,128)(2,1)S(1)} %add_convert_fusion.9), channel_id=1, source_target_pairs={{0,4},{1,5},{2,6},{3,7},{4,0},{5,1},{6,2},{7,3},{8,12},{9,13},{10,... | collective-permute-start | bytes 589832 | tf_op jit(solution)/shard_map/cond/branch_1_fun/ppermute | solution.py:1117
  419.7 20.2 %collective-permute-start.21 = (bf16[304,512]{1,0:T(8,128)(2,1)S(1)}, bf16[304,512]{1,0:T(8,128)(2,1)S(1)}, u32[]{:S(2)}, u32[]{:S(2)}) collective-permute-start(bf16[304,512]{1,0:T(8,128)(2,1)S(1)} %maximum_select_fusion.6), channel_id=1, source_target_pairs={{0,4},{1,5},{2,6},{3,7},{4,0},{5,1},{6,2},{7,3},{8,12},{9,13},{10,... | collective-permute-start | bytes 933896 | tf_op jit(solution)/shard_map/cond/branch_1_fun/ppermute | solution.py:1117
  440.1 16.0 %collective-permute-start.22 = (bf16[608,512]{1,0:T(8,128)(2,1)S(1)}, bf16[608,512]{1,0:T(8,128)(2,1)S(1)}, u32[]{:S(2)}, u32[]{:S(2)}) collective-permute-start(bf16[608,512]{1,0:T(8,128)(2,1)S(1)} %maximum_select_fusion.4), channel_id=1, source_target_pairs={{0,2},{1,3},{2,0},{3,1},{4,6},{5,7},{6,4},{7,5},{8,10},{9,11},{10,... | collective-permute-start | bytes 1867784 | tf_op jit(solution)/shard_map/cond/branch_1_fun/ppermute | solution.py:1117
  440.3 11.1 %collective-permute-start.24 = (bf16[192,1024]{1,0:T(8,128)(2,1)S(1)}, bf16[192,1024]{1,0:T(8,128)(2,1)S(1)}, u32[]{:S(2)}, u32[]{:S(2)}) collective-permute-start(bf16[192,1024]{1,0:T(8,128)(2,1)S(1)} %maximum_select_fusion.5), channel_id=1, source_target_pairs={{0,1},{1,0},{2,3},{3,2},{4,5},{5,4},{6,7},{7,6},{8,9},{9,8},{10,11... | collective-permute-start | bytes 1179656 | tf_op jit(solution)/shard_map/cond/branch_1_fun/ppermute | solution.py:1117
  457.8 6.4 %copy-start.25 = (bf16[256,1024]{1,0:T(8,128)(2,1)S(1)}, bf16[256,1024]{1,0:T(8,128)(2,1)}, u32[]{:S(2)}) copy-start(bf16[256,1024]{1,0:T(8,128)(2,1)} %all-reduce.11.cloned.1.call-done.refs_10_) | copy-start | bytes 1572868
  457.9 19.0 %collective-permute-start.46 = (bf16[384,1024]{1,0:T(8,128)(2,1)}, bf16[384,1024]{1,0:T(8,128)(2,1)}, u32[]{:S(2)}, u32[]{:S(2)}) collective-permute-start(bf16[384,1024]{1,0:T(8,128)(2,1)} %get-tuple-element.302), channel_id=1, source_target_pairs={{0,2},{1,3},{2,0},{3,1},{4,6},{5,7},{6,4},{7,5},{8,10},{9,11},{10,... | collective-permute-start | bytes 2359304 | tf_op jit(solution)/shard_map/ppermute | solution.py:1117
  458.2 28.8 %collective-permute-start.44 = (bf16[1216,512]{1,0:T(8,128)(2,1)}, bf16[1216,512]{1,0:T(8,128)(2,1)}, u32[]{:S(2)}, u32[]{:S(2)}) collective-permute-start(bf16[1216,512]{1,0:T(8,128)(2,1)} %get-tuple-element.301.refs_3_), channel_id=1, source_target_pairs={{0,1},{1,0},{2,3},{3,2},{4,5},{5,4},{6,7},{7,6},{8,9},{9,8},{10,11... | collective-permute-start | bytes 3735560 | tf_op jit(solution)/shard_map/ppermute | solution.py:1117
  460.8 28.4 %collective-permute-start.49 = (bf16[2432,256]{1,0:T(8,128)(2,1)S(1)}, bf16[2432,256]{1,0:T(8,128)(2,1)}, u32[]{:S(2)}, u32[]{:S(2)}) collective-permute-start(bf16[2432,256]{1,0:T(8,128)(2,1)S(1)} %constant_dynamic-slice_fusion.14), channel_id=1, source_target_pairs={{0,8},{8,0},{1,9},{9,1},{2,10},{10,2},{3,11},{11,3},{4,12},{12,4},... | collective-permute-start | bytes 3735560 | tf_op jit(solution)/shard_map/ppermute | solution.py:1112
  461.4 33.8 %collective-permute-start.48 = (bf16[2432,512]{1,0:T(8,128)(2,1)}, bf16[2432,512]{1,0:T(8,128)(2,1)}, u32[]{:S(2)}, u32[]{:S(2)}) collective-permute-start(bf16[2432,512]{1,0:T(8,128)(2,1)} %all-reduce.13.cloned.1.call-done.refs_6_), channel_id=1, source_target_pairs={{0,16},{1,17},{2,18},{3,19},{4,20},{5,21},{6,22},{7,23},{8,24},{9,... | collective-permute-start | bytes 7471112 | tf_op jit(solution)/shard_map/ppermute | solution.py:1350
  464.2 16.6 %collective-permute-start.51 = (bf16[256,1024]{1,0:T(8,128)(2,1)S(1)}, bf16[256,1024]{1,0:T(8,128)(2,1)}, u32[]{:S(2)}, u32[]{:S(2)}) collective-permute-start(bf16[256,1024]{1,0:T(8,128)(2,1)S(1)} %copy-done.25), channel_id=1, source_target_pairs={{0,16},{1,17},{2,18},{3,19},{4,20},{5,21},{6,22},{7,23},{8,24},{9,... | collective-permute-start | bytes 1572872 | tf_op jit(solution)/shard_map/ppermute | solution.py:1350
  480.8 14.4 %collective-permute-start.47 = (bf16[768,1024]{1,0:T(8,128)(2,1)S(1)}, bf16[768,1024]{1,0:T(8,128)(2,1)}, u32[]{:S(2)}, u32[]{:S(2)}) collective-permute-start(bf16[768,1024]{1,0:T(8,128)(2,1)S(1)} %maximum_select_fusion.8.refs_5_), channel_id=1, source_target_pairs={{0,16},{16,0},{1,17},{17,1},{2,18},{18,2},{3,19},{19,3},{4,20},{20... | collective-permute-start | bytes 4718600 | tf_op jit(solution)/shard_map/ppermute | solution.py:1112
  480.8 14.4 %collective-permute-start.43 = (bf16[1216,512]{1,0:T(8,128)(2,1)}, bf16[1216,512]{1,0:T(8,128)(2,1)}, u32[]{:S(2)}, u32[]{:S(2)}) collective-permute-start(bf16[1216,512]{1,0:T(8,128)(2,1)} %get-tuple-element.301.refs_3_), channel_id=1, source_target_pairs={{16,0},{17,1},{18,2},{19,3},{20,4},{21,5},{22,6},{23,7},{24,8},{25... | collective-permute-start | bytes 3735560 | tf_op jit(solution)/shard_map/ppermute | solution.py:1350
  487.0 8.3 %collective-permute-start.45 = (bf16[1216,512]{1,0:T(8,128)(2,1)}, bf16[1216,512]{1,0:T(8,128)(2,1)}, u32[]{:S(2)}, u32[]{:S(2)}) collective-permute-start(bf16[1216,512]{1,0:T(8,128)(2,1)} %collective-permute-done.44.refs_4_), channel_id=1, source_target_pairs={{16,0},{17,1},{18,2},{19,3},{20,4},{21,5},{22,6},{23,7},{24,8},{25... | collective-permute-start | bytes 3735560 | tf_op jit(solution)/shard_map/ppermute | solution.py:1350
  489.2 6.1 %collective-permute-start.50 = (bf16[2432,256]{1,0:T(8,128)(2,1)}, bf16[2432,256]{1,0:T(8,128)(2,1)}, u32[]{:S(2)}, u32[]{:S(2)}) collective-permute-start(bf16[2432,256]{1,0:T(8,128)(2,1)} %collective-permute-done.49.refs_8_), channel_id=1, source_target_pairs={{0,16},{1,17},{2,18},{3,19},{4,20},{5,21},{6,22},{7,23},{8,24},{9,... | collective-permute-start | bytes 3735560 | tf_op jit(solution)/shard_map/ppermute | solution.py:1350
  (17 other events, 22.6 us)
Sparse Core Ops, SparseCore 0:
  174.8 73.1 all-reduce.10
  252.6 120.2 all-reduce.12

commit v4 on v3

--- a/solution.py
+++ b/solution.py
@@ -20,7 +20,7 @@
 CP = DH + CH + 128
 LANE = 128
 TILE = 256
-RC = 32
+RC = 64
 HEAD_ROWS = 8
 EPS = 1e-05
 VMEM_BYTES = 63 * 1024 * 1024
@@ -171,13 +171,13 @@
 
 def scaled_inputs(conv_s, dt_s, spread_s, xdt_s, xlo_s, count):
     def body(index):
-        rows = tile_at(index, RC * 4)
+        rows = tile_at(index, RC * 2)
         scale = nn(pack3(dt_s[rows]), spread_s[...])
         v = conv_s[rows, :DH] * scale
         xdt_s[rows] = v.astype(bf16)
         xlo_s[rows] = (v - v.astype(bf16).astype(f32)).astype(bf16)
 
-    loop(count // (RC * 4), body)
+    loop(count // (RC * 2), body)
 
 
 def tail_weight(cs_s, bound, span):
@@ -679,7 +679,7 @@
             loop(DH // TILE, state_tile)
 
     def head_rows(index):
-        chunk = RC * 4
+        chunk = RC * 2
         rows = tile_at(index, chunk)
         steps = dt_s[rows]
         scale = nn(pack3(steps), spread_s[...])
@@ -690,7 +690,7 @@
         grad_cs_s[rows] = sums[chunk:] - steps * per_step
         dpre_s[rows, :DH] = gg_s[rows] * skip + grad * scale
 
-    loop(count // (RC * 4), head_rows)
+    loop(count // (RC * 2), head_rows)
     tail = jnp.broadcast_to(dpre_s[count : count + 1, :DH], (8, DH))
     tail_heads = head_sums(tail, gather_s)[0:1]
     last = iota((span, LANE), 0) == span - 1

time: 518 us -> 517 us (level)
  waiting for transfers between devices: 197 us -> 204 us
  Pallas kernels: 153 us -> 147 us
    pallas_call x6, Pallas kernels: 153 us -> 147 us  [call(): pl.pallas_call(kernel, in_specs=specs, out_specs=out_specs, out_shape=[ja...]
    ppermute x15, waiting for transfers between devices: 91.6 us -> 97.6 us  [flip(): lax.ppermute(block, 'replica', [(at, at ^ mask) for at in range(size)])]
  transfers between devices with their start and end apart: 54 -> 54, of which waited for: 23 -> 22; matrix products, arithmetic and copies ran while one was open for 16% -> 16% of each run, Pallas kernels for 23% -> 22%
where the time goes in v4:
time: 517 us; the launch traced here: 510 us
  waiting for transfers between devices  204 us (39%)
  Pallas kernels  147 us (28%)
  starting transfers between devices  46.9 us (9%)
  other arithmetic  39.2 us (8%)
  local copies, waits for them, and re-layouts  36.8 us (7%)
  matrix products  19.3 us (4%)
  between operations  15.4 us (3%)
    pallas_call x6, Pallas kernels, call(): pl.pallas_call(kernel, in_specs=specs, out_specs=out_specs, out_shape=[ja...  147 us
    ppermute x15, waiting for transfers between devices, flip(): lax.ppermute(block, 'replica', [(at, at ^ mask) for at in range(size)])  97.6 us
    ppermute x32, waiting for transfers between devices, swap(): return lax.ppermute(block, axis, [(0, 1), (1, 0)])  97.3 us
    ppermute x32, starting transfers between devices, swap(): return lax.ppermute(block, axis, [(0, 1), (1, 0)])  21.8 us
    dot_general x8, matrix products, tn(): lax.dot_general(left, right, (((0,), (0,)), ((), ())), preferred_element_...  16.4 us
    ppermute x15, starting transfers between devices, flip(): lax.ppermute(block, 'replica', [(at, at ^ mask) for at in range(size)])  12.9 us
    ppermute x5, starting transfers between devices, to_owner(): return lax.ppermute(block, 'section', [(1 - layer, layer)])  12.1 us
    select_n x10, other arithmetic, in_order(): jnp.where(which == 0, jnp.concatenate([mine, other], axis=dim), jnp.conca...  11.4 us
  transfers between devices with their start and end apart: 54, of which 22 were waited for; matrix products, arithmetic and copies ran while one was open for 16% of the time, Pallas kernels for 22%

profile of v4, /device:TPU:0, one launch (start us, length us, event | category | flops | bytes accessed | tf_op | source)
XLA Modules:
  0.0 509.8 jit_solution(15931396922615714491)
XLA Ops:
  9.0 2.7 dynamic-slice_bitcast_fusion
  14.2 3.0 collective-permute-start.34
  17.8 1.9 dynamic-slice_bitcast_fusion.3.refs_12_
  19.7 2.6 broadcast_select_fusion.3
  23.9 1.9 collective-permute-start.28
  26.1 29.7 %collective-permute-done.28 = bf16[2,8,1152]{2,1,0:T(8,128)(2,1)S(1)} collective-permute-done((bf16[2,8,1152]{2,1,0:T(8,128)(2,1)S(1)}, bf16[2,8,1152]{2,1,0:T(8,128)(2,1)S(1)}, u32[]{:S(2)}, u32[]{:S(2)}) %collective-permute-start.28) | collective-permute-done | bytes 36896 | tf_op jit(solution)/shard_map/ppermute | solution.py:1112
  57.0 1.7 collective-permute-start.37
  59.4 2.4 collective-permute-done.32
  62.9 26.8 %conditional.3 = (bf16[512,1024]{1,0:T(8,128)(2,1)}, f32[520,2432]{1,0:T(8,128)}, f32[512,1024]{1,0:T(8,128)}, f32[128,1024]{1,0:T(8,128)}, f32[512,1024]{1,0:T(8,128)}, /*index=5*/f32[8,512]{1,0:T(8,128)S(1)}) conditional(s32[]{:T(128)} %bitcast.12, () %tuple.48, (s32[3]{0:T(128)S(1)}, f32[8,1280]{1,0:T(8,128)S(1)}, f32[8,128]{1,0:T(8,128)S(1)}, ...), branch_computations={%region_0.1_spmd, %region_1.2_spmd} | conditional | flops 35000000512 | bytes 24784204 | solution.py:1296
  63.9 25.6 %forward_0.1 = (bf16[512,1024]{1,0:T(8,128)(2,1)}, f32[520,2432]{1,0:T(8,128)}, f32[512,1024]{1,0:T(8,128)}, f32[128,1024]{1,0:T(8,128)}, f32[512,1024]{1,0:T(8,...) custom-call(s32[3]{0:T(128)S(1)} %get-tuple-element.123.refs_0_, f32[8,1280]{1,0:T(8,128)S(1)} %get-tuple-element.124.refs_1_, ...), custom_call_target="tpu_custom_call" | custom-call | flops 35000000512 | bytes 20000000 | tf_op jit(solution)/shard_map/cond/branch_1_fun/forward_0/pallas_call | solution.py:830
  90.1 1.7 collective-permute-start.36
  91.9 1.8 collective-permute-done.35.stat_far
  93.7 6.3 %project_0.1.refs_10_ = f32[512,1024]{1,0:T(8,128)} custom-call(s32[3]{0:T(128)S(1)} %pad_add_fusion.scal.refs_0_, f32[8,1280]{1,0:T(8,128)S(1)} %pad_maximum_fusion.3.par, bf16[1024,1024]{1,0:T(8,128)(2,1)} %bitcast.147, bf16[1024,1024]{1,0:T(8,128)(2,1)} %collective-permute-done.33.wo_b.refs_8_, f32[8,512]{1,0:T(8,128)S(1)} %get-tuple-element.279.stat_own, ...), custom_call_target="tpu_custom_call" | custom-call | flops 6000000000 | bytes 20000000 | tf_op jit(solution)/shard_map/project_0/pallas_call | solution.py:830
  100.0 4.4 collective-permute-done.36.refs_13_
  104.4 1.8 convert_element_type.170
  106.1 1.6 collective-permute-start.39
  107.9 22.6 %collective-permute-done.39 = f16[512,1024]{1,0:T(8,128)(2,1)S(1)} collective-permute-done((f16[512,1024]{1,0:T(8,128)(2,1)S(1)}, f16[512,1024]{1,0:T(8,128)(2,1)S(1)}, u32[]{:S(2)}, u32[]{:S(2)}) %collective-permute-start.39) | collective-permute-done | bytes 1048608 | tf_op jit(solution)/shard_map/ppermute | solution.py:1112
  130.5 1.5 convert_element_type.171.refs_11_
  132.0 27.8 %forward_1.1 = (bf16[512,1024]{1,0:T(8,128)(2,1)}, f32[520,2432]{1,0:T(8,128)}, f32[512,1024]{1,0:T(8,128)}, f32[128,1024]{1,0:T(8,128)}, f32[512,1024]{1,0:T(8,...) custom-call(s32[3]{0:T(128)S(1)} %pad_add_fusion.scal.refs_0_, f32[8,1280]{1,0:T(8,128)S(1)} %pad_maximum_fusion.4.refs_1_, ...), custom_call_target="tpu_custom_call" | custom-call | flops 35000000512 | bytes 20000000 | tf_op jit(solution)/shard_map/forward_1/pallas_call | solution.py:830
  161.1 2.0 maximum_select_fusion.9
  164.0 1.9 collective-permute-done.42
  166.0 1.5 collective-permute-done.41
  167.5 2.1 fusion.39
  172.2 64.3 %conditional.4 = (bf16[512,1024]{1,0:T(8,128)(2,1)}, bf16[512,1024]{1,0:T(8,128)(2,1)}, bf16[2432,512]{1,0:T(8,128)(2,1)}, f32[16,1280]{1,0:T(8,128)}) conditional(s32[]{:T(128)} %bitcast.12, () %tuple.51, (s32[3]{0:T(128)S(1)}, f32[8,1280]{1,0:T(8,128)S(1)}, f32[8,128]{1,0:T(8,128)S(1)}, bf16[4384,512]{1,0:T(8,128)(2,1)}, ...), branch_computations={%region_2.3_spmd, %region_3.4_spmd} | conditional | flops 57554722816 | bytes 58928640 | solution.py:1296
  172.5 37.9 %backward_1.1 = (bf16[512,1024]{1,0:T(8,128)(2,1)}, bf16[512,2432]{1,0:T(8,128)(2,1)}, bf16[512,1024]{1,0:T(8,128)(2,1)}, bf16[512,1024]{1,0:T(8,128)(2,1)}, bf1...) custom-call(s32[3]{0:T(128)S(1)} %get-tuple-element.140.refs_0_, f32[8,1280]{1,0:T(8,128)S(1)} %get-tuple-element.141.refs_1_, ...), custom_call_target="tpu_custom_call" | custom-call | flops 54999998464 | bytes 20000000 | tf_op jit(solution)/shard_map/cond/branch_1_fun/backward_1/pallas_call | solution.py:830
  212.8 3.2 fusion.1
  217.9 2.9 fusion
  220.8 15.7 %collective-permute-done = bf16[512,1024]{1,0:T(8,128)(2,1)} collective-permute-done((bf16[512,1024]{1,0:T(8,128)(2,1)}, bf16[512,1024]{1,0:T(8,128)(2,1)}, u32[]{:S(2)}, u32[]{:S(2)}) %collective-permute-start) | collective-permute-done | bytes 1048608 | tf_op jit(solution)/shard_map/cond/branch_1_fun/ppermute | solution.py:1112
  236.5 8.9 %all-reduce.11.cloned.1.call-done.refs_10_ = bf16[256,1024]{1,0:T(8,128)(2,1)} async-done(((bf16[256,1024]{1,0:T(8,128)(2,1)}), bf16[256,1024]{1,0:T(8,128)(2,1)}) %all-reduce.11.cloned.1.call-update) | async-done | bytes 524304 | tf_op jit(solution)/shard_map/psum | solution.py:1324
  245.4 211.0 %conditional.5 = (f32[1,512]{1,0:T(1,128)}, f32[4,1152]{1,0:T(4,128)}, f32[1,1152]{1,0:T(1,128)}, f32[3,16]{1,0:T(4,128)}, f32[1,1024]{1,0:T(1,128)}, /*index=5*...) conditional(s32[]{:T(128)} %bitcast.12, () %tuple.46, ...), branch_computations={%region_4.5_spmd, %region_5.9_spmd} | conditional | flops 59740913664 | bytes 217801312 | solution.py:1296
  245.9 40.3 %backward_0.1 = (bf16[512,1024]{1,0:T(8,128)(2,1)}, bf16[512,2432]{1,0:T(8,128)(2,1)}, bf16[512,1024]{1,0:T(8,128)(2,1)}, bf16[512,1024]{1,0:T(8,128)(2,1)}, bf1...) custom-call(s32[3]{0:T(128)S(1)} %get-tuple-element.165.refs_0_, f32[8,1280]{1,0:T(8,128)S(1)} %get-tuple-element.166.refs_1_, ...), custom_call_target="tpu_custom_call" | custom-call | flops 54999998464 | bytes 20000000 | tf_op jit(solution)/shard_map/cond/branch_1_fun/backward_0/pallas_call | solution.py:830
  291.4 2.3 fusion.28
  293.6 1.5 fusion.20
  296.3 2.1 add_convert_fusion
  298.4 2.9 fusion.18
  301.3 1.5 fusion.10
  305.4 1.5 collective-permute-start.9
  306.8 2.9 fusion.11
  313.5 1.6 collective-permute-start.7
  315.8 1.5 slice_reduce_fusion
  319.0 1.5 collective-permute-start.12
  322.7 11.7 %collective-permute-done.12 = f32[2,16,1280]{2,1,0:T(8,128)} collective-permute-done((f32[2,16,1280]{2,1,0:T(8,128)}, f32[2,16,1280]{2,1,0:T(8,128)}, u32[]{:S(2)}, u32[]{:S(2)}) %collective-permute-start.12) | collective-permute-done | bytes 163872 | tf_op jit(solution)/shard_map/cond/branch_1_fun/ppermute | solution.py:1112
  337.7 15.1 %collective-permute-done.7 = bf16[1216,512]{1,0:T(8,128)(2,1)} collective-permute-done((bf16[1216,512]{1,0:T(8,128)(2,1)}, bf16[1216,512]{1,0:T(8,128)(2,1)}, u32[]{:S(2)}, u32[]{:S(2)}) %collective-permute-start.7) | collective-permute-done | bytes 1245216 | tf_op jit(solution)/shard_map/cond/branch_1_fun/ppermute | solution.py:1117
  352.9 2.2 add_convert_fusion.4
  355.6 2.7 add_convert_fusion.1
  358.3 1.6 collective-permute-start.13
  365.3 17.2 %collective-permute-done.15 = f32[2,8,1152]{2,1,0:T(8,128)S(1)} collective-permute-done((f32[2,8,1152]{2,1,0:T(8,128)S(1)}, f32[2,8,1152]{2,1,0:T(8,128)S(1)}, u32[]{:S(2)}, u32[]{:S(2)}) %collective-permute-start.15) | collective-permute-done | bytes 73760 | tf_op jit(solution)/shard_map/cond/branch_1_fun/ppermute | solution.py:1117
  383.8 1.4 collective-permute-start.16
  386.3 1.6 collective-permute-start.17
  388.0 2.4 maximum_select_fusion.2
  392.9 18.3 %collective-permute-done.18 = f32[2,8,1152]{2,1,0:T(8,128)S(1)} collective-permute-done((f32[2,8,1152]{2,1,0:T(8,128)S(1)}, f32[2,8,1152]{2,1,0:T(8,128)S(1)}, u32[]{:S(2)}, u32[]{:S(2)}) %collective-permute-start.18) | collective-permute-done | bytes 73760 | tf_op jit(solution)/shard_map/cond/branch_1_fun/ppermute | solution.py:1117
  412.2 1.5 collective-permute-start.19
  413.9 4.1 collective-permute-done.19
  420.7 17.8 %collective-permute-done.21 = bf16[304,512]{1,0:T(8,128)(2,1)S(1)} collective-permute-done((bf16[304,512]{1,0:T(8,128)(2,1)S(1)}, bf16[304,512]{1,0:T(8,128)(2,1)S(1)}, u32[]{:S(2)}, u32[]{:S(2)}) %collective-permute-start.21) | collective-permute-done | bytes 311328 | tf_op jit(solution)/shard_map/cond/branch_1_fun/ppermute | solution.py:1117
  440.3 9.7 %collective-permute-done.24 = bf16[192,1024]{1,0:T(8,128)(2,1)S(1)} collective-permute-done((bf16[192,1024]{1,0:T(8,128)(2,1)S(1)}, bf16[192,1024]{1,0:T(8,128)(2,1)S(1)}, u32[]{:S(2)}, u32[]{:S(2)}) %collective-permute-start.24) | collective-permute-done | bytes 393248 | tf_op jit(solution)/shard_map/cond/branch_1_fun/ppermute | solution.py:1117
  451.2 3.6 collective-permute-done.22
  454.8 1.5 maximum_select_fusion
  459.5 2.8 collective-permute-start.48
  462.3 2.1 collective-permute-start.51
  464.4 11.1 %collective-permute-done.46 = bf16[384,1024]{1,0:T(8,128)(2,1)} collective-permute-done((bf16[384,1024]{1,0:T(8,128)(2,1)}, bf16[384,1024]{1,0:T(8,128)(2,1)}, u32[]{:S(2)}, u32[]{:S(2)}) %collective-permute-start.46) | collective-permute-done | bytes 786464 | tf_op jit(solution)/shard_map/ppermute | solution.py:1117
  475.5 2.7 maximum_select_fusion.8.refs_5_
  480.7 4.9 collective-permute-done.44.refs_4_
  487.3 4.7 collective-permute-start.50
  493.9 8.8 %assemble.1 = (f32[4384,512]{1,0:T(8,128)}, f32[1024,1024]{1,0:T(8,128)}) custom-call(s32[3]{0:T(128)} %pad_add_fusion.2.scal, bf16[1216,512]{1,0:T(8,128)(2,1)} %collective-permute-done.43.refs_0_, bf16[1216,512]{1,0:T(8,128)(2,1)} %collective-permute-done.45.refs_1_, bf16[768,1024]{1,0:T(8,128)(2,1)} %collective-permute-done.47.refs_2_, ...), custom_call_target="tpu_custom_call" | custom-call | flops 6000000000 | bytes 20000000 | tf_op jit(solution)/shard_map/assemble/pallas_call | solution.py:830
  (230 shorter events, 66.8 us)
Async XLA Ops:
  7.2 238.2 %all-reduce.11.cloned.1.call-start = ((), (), s32[]{:S(2)}) async-start(), calls=%async_computation | async-start | bytes 1048576 | tf_op jit(solution)/shard_map/psum | solution.py:1324
  11.6 5.6 %copy-start.21 = (s32[2,1]{0,1:T(1,128)S(1)}, s32[2,1]{0,1:T(1,128)}, u32[]{:S(2)}) copy-start(s32[2,1]{0,1:T(1,128)} %param.17) | copy-start | bytes 28
  11.7 8.0 %collective-permute-start.30 = (bf16[1168,512]{1,0:T(8,128)(2,1)S(1)}, bf16[1168,512]{1,0:T(8,128)(2,1)S(1)}, u32[]{:S(2)}, u32[]{:S(2)}) collective-permute-start(bf16[1168,512]{1,0:T(8,128)(2,1)S(1)} %pad_maximum_fusion.1), channel_id=1, source_target_pairs={{0,16},{16,0},{1,17},{17,1},{2,18},{18,2},{3,19},{19,3},{4,20},{20... | collective-permute-start | bytes 3588104 | tf_op jit(solution)/shard_map/ppermute | solution.py:1112
  12.6 11.3 %collective-permute-start.27 = (bf16[8,1152]{1,0:T(8,128)(2,1)S(1)}, bf16[8,1152]{1,0:T(8,128)(2,1)S(1)}, u32[]{:S(2)}, u32[]{:S(2)}) collective-permute-start(bf16[8,1152]{1,0:T(8,128)(2,1)S(1)} %concatenate.152), channel_id=1, source_target_pairs={{0,16},{16,0},{1,17},{17,1},{2,18},{18,2},{3,19},{19,3},{4,20},{20... | collective-permute-start | bytes 55304 | tf_op jit(solution)/shard_map/ppermute | solution.py:1112
  13.1 48.7 %collective-permute-start.29 = (bf16[4384,512]{1,0:T(8,128)(2,1)}, bf16[4384,512]{1,0:T(8,128)(2,1)}, u32[]{:S(2)}, u32[]{:S(2)}) collective-permute-start(bf16[4384,512]{1,0:T(8,128)(2,1)} %bitcast.120), channel_id=1, source_target_pairs={{0,16},{16,0},{1,17},{17,1},{2,18},{18,2},{3,19},{19,3},{4,20},{20... | collective-permute-start | bytes 13467656 | tf_op jit(solution)/shard_map/ppermute | solution.py:1112
  14.2 44.6 %collective-permute-start.34 = (bf16[256,1024]{1,0:T(8,128)(2,1)S(1)}, bf16[256,1024]{1,0:T(8,128)(2,1)}, u32[]{:S(2)}, u32[]{:S(2)}) collective-permute-start(bf16[256,1024]{1,0:T(8,128)(2,1)S(1)} %dynamic-slice_bitcast_fusion.2), channel_id=1, source_target_pairs={{0,8},{8,0},{1,9},{9,1},{2,10},{10,2},{3,11},{11,3},{4,12},{12,4},... | collective-permute-start | bytes 1572872 | tf_op jit(solution)/shard_map/ppermute | solution.py:1112
  17.2 42.2 %collective-permute-start.33 = (bf16[1024,1024]{1,0:T(8,128)(2,1)}, bf16[1024,1024]{1,0:T(8,128)(2,1)}, u32[]{:S(2)}, u32[]{:S(2)}) collective-permute-start(bf16[1024,1024]{1,0:T(8,128)(2,1)} %bitcast.145), channel_id=1, source_target_pairs={{0,16},{16,0},{1,17},{17,1},{2,18},{18,2},{3,19},{19,3},{4,20},{20... | collective-permute-start | bytes 6291464 | tf_op jit(solution)/shard_map/ppermute | solution.py:1112
  22.3 33.5 %collective-permute-start.31 = (bf16[1168,512]{1,0:T(8,128)(2,1)}, bf16[1168,512]{1,0:T(8,128)(2,1)}, u32[]{:S(2)}, u32[]{:S(2)}) collective-permute-start(bf16[1168,512]{1,0:T(8,128)(2,1)} %get-tuple-element.361), channel_id=1, source_target_pairs={{0,8},{8,0},{1,9},{9,1},{2,10},{10,2},{3,11},{11,3},{4,12},{12,4},... | collective-permute-start | bytes 3588104 | tf_op jit(solution)/shard_map/ppermute | solution.py:1112
  23.9 31.9 %collective-permute-start.28 = (bf16[2,8,1152]{2,1,0:T(8,128)(2,1)S(1)}, bf16[2,8,1152]{2,1,0:T(8,128)(2,1)S(1)}, u32[]{:S(2)}, u32[]{:S(2)}) collective-permute-start(bf16[2,8,1152]{2,1,0:T(8,128)(2,1)S(1)} %get-tuple-element.328), channel_id=1, source_target_pairs={{0,8},{8,0},{1,9},{9,1},{2,10},{10,2},{3,11},{11,3},{4,12},{12,4},... | collective-permute-start | bytes 110600 | tf_op jit(solution)/shard_map/ppermute | solution.py:1112
  57.0 34.9 %collective-permute-start.37 = (bf16[1168,512]{1,0:T(8,128)(2,1)}, bf16[1168,512]{1,0:T(8,128)(2,1)}, u32[]{:S(2)}, u32[]{:S(2)}) collective-permute-start(bf16[1168,512]{1,0:T(8,128)(2,1)} %broadcast_select_fusion.2), channel_id=1, source_target_pairs={{0,8},{8,0},{1,9},{9,1},{2,10},{10,2},{3,11},{11,3},{4,12},{12,4},... | collective-permute-start | bytes 3588104 | tf_op jit(solution)/shard_map/ppermute | solution.py:1112
  58.7 3.1 collective-permute-start.32
  89.8 3.9 collective-permute-start.35
  90.1 14.2 %collective-permute-start.36 = (bf16[256,1024]{1,0:T(8,128)(2,1)}, bf16[256,1024]{1,0:T(8,128)(2,1)}, u32[]{:S(2)}, u32[]{:S(2)}) collective-permute-start(bf16[256,1024]{1,0:T(8,128)(2,1)} %dynamic-slice_bitcast_fusion.3.refs_12_), channel_id=1, source_target_pairs={{0,8},{8,0},{1,9},{9,1},{2,10},{10,2},{3,11},{11,3},{4,12},{12,4},... | collective-permute-start | bytes 1572872 | tf_op jit(solution)/shard_map/ppermute | solution.py:1112
  91.9 40.2 %collective-permute-start.38 = (bf16[1168,512]{1,0:T(8,128)(2,1)}, bf16[1168,512]{1,0:T(8,128)(2,1)}, u32[]{:S(2)}, u32[]{:S(2)}) collective-permute-start(bf16[1168,512]{1,0:T(8,128)(2,1)} %collective-permute-done.37.refs_5_), channel_id=1, source_target_pairs={{0,16},{16,0},{1,17},{17,1},{2,18},{18,2},{3,19},{19,3},{4,20},{20... | collective-permute-start | bytes 3588104 | tf_op jit(solution)/shard_map/ppermute | solution.py:1112
  106.1 24.4 %collective-permute-start.39 = (f16[512,1024]{1,0:T(8,128)(2,1)S(1)}, f16[512,1024]{1,0:T(8,128)(2,1)S(1)}, u32[]{:S(2)}, u32[]{:S(2)}) collective-permute-start(f16[512,1024]{1,0:T(8,128)(2,1)S(1)} %convert_element_type.170), channel_id=1, source_target_pairs={{0,8},{8,0},{1,9},{9,1},{2,10},{10,2},{3,11},{11,3},{4,12},{12,4},... | collective-permute-start | bytes 3145736 | tf_op jit(solution)/shard_map/ppermute | solution.py:1112
  159.8 3.8 copy-start.8
  159.8 3.8 collective-permute-start.40
  163.1 2.9 collective-permute-start.42
  163.9 5.7 %copy-start.4 = (bf16[512,1024]{1,0:T(8,128)(2,1)}, bf16[512,1024]{1,0:T(8,128)(2,1)S(1)}, u32[]{:S(2)}) copy-start(bf16[512,1024]{1,0:T(8,128)(2,1)S(1)} %multiply_convert_fusion) | copy-start | bytes 3145732
  163.9 3.6 collective-permute-start.41
  172.2 285.4 %all-reduce.13.cloned.1.call-start = ((), (), s32[]{:S(2)}) async-start(), calls=%async_computation.1 | async-start | bytes 4980736 | tf_op jit(solution)/shard_map/psum | solution.py:1337
  210.4 7.5 %collective-permute-start.1 = (bf16[512,2432]{1,0:T(8,128)(2,1)}, bf16[512,2432]{1,0:T(8,128)(2,1)S(1)}, u32[]{:S(2)}, u32[]{:S(2)}) collective-permute-start(bf16[512,2432]{1,0:T(8,128)(2,1)} %get-tuple-element.158), channel_id=1, source_target_pairs={{0,16},{16,0},{1,17},{17,1},{2,18},{18,2},{3,19},{19,3},{4,20},{20... | collective-permute-start | bytes 7471112 | tf_op jit(solution)/shard_map/cond/branch_1_fun/ppermute | solution.py:1112
  210.6 6.2 %collective-permute-start.2 = (bf16[512,1024]{1,0:T(8,128)(2,1)}, bf16[512,1024]{1,0:T(8,128)(2,1)}, u32[]{:S(2)}, u32[]{:S(2)}) collective-permute-start(bf16[512,1024]{1,0:T(8,128)(2,1)} %get-tuple-element.159), channel_id=1, source_target_pairs={{0,16},{16,0},{1,17},{17,1},{2,18},{18,2},{3,19},{19,3},{4,20},{20... | collective-permute-start | bytes 3145736 | tf_op jit(solution)/shard_map/cond/branch_1_fun/ppermute | solution.py:1112
  211.0 25.5 %collective-permute-start = (bf16[512,1024]{1,0:T(8,128)(2,1)}, bf16[512,1024]{1,0:T(8,128)(2,1)}, u32[]{:S(2)}, u32[]{:S(2)}) collective-permute-start(bf16[512,1024]{1,0:T(8,128)(2,1)} %get-tuple-element.399), channel_id=1, source_target_pairs={{0,8},{8,0},{1,9},{9,1},{2,10},{10,2},{3,11},{11,3},{4,12},{12,4},... | collective-permute-start | bytes 3145736 | tf_op jit(solution)/shard_map/cond/branch_1_fun/ppermute | solution.py:1112
  286.2 15.1 %collective-permute-start.3 = (bf16[512,2432]{1,0:T(8,128)(2,1)}, bf16[512,2432]{1,0:T(8,128)(2,1)S(1)}, u32[]{:S(2)}, u32[]{:S(2)}) collective-permute-start(bf16[512,2432]{1,0:T(8,128)(2,1)} %get-tuple-element.187), channel_id=1, source_target_pairs={{0,16},{16,0},{1,17},{17,1},{2,18},{18,2},{3,19},{19,3},{4,20},{20... | collective-permute-start | bytes 7471112 | tf_op jit(solution)/shard_map/cond/branch_1_fun/ppermute | solution.py:1112
  286.3 8.9 %collective-permute-start.4 = (bf16[512,1024]{1,0:T(8,128)(2,1)}, bf16[512,1024]{1,0:T(8,128)(2,1)}, u32[]{:S(2)}, u32[]{:S(2)}) collective-permute-start(bf16[512,1024]{1,0:T(8,128)(2,1)} %get-tuple-element.188), channel_id=1, source_target_pairs={{0,16},{16,0},{1,17},{17,1},{2,18},{18,2},{3,19},{19,3},{4,20},{20... | collective-permute-start | bytes 3145736 | tf_op jit(solution)/shard_map/cond/branch_1_fun/ppermute | solution.py:1112
  286.8 9.5 %collective-permute-start.5 = (bf16[512,1024]{1,0:T(8,128)(2,1)}, bf16[512,1024]{1,0:T(8,128)(2,1)}, u32[]{:S(2)}, u32[]{:S(2)}) collective-permute-start(bf16[512,1024]{1,0:T(8,128)(2,1)} %get-tuple-element.190), channel_id=1, source_target_pairs={{0,16},{16,0},{1,17},{17,1},{2,18},{18,2},{3,19},{19,3},{4,20},{20... | collective-permute-start | bytes 3145736 | tf_op jit(solution)/shard_map/cond/branch_1_fun/ppermute | solution.py:1112
  286.9 9.4 %collective-permute-start.6 = (bf16[512,1024]{1,0:T(8,128)(2,1)}, bf16[512,1024]{1,0:T(8,128)(2,1)}, u32[]{:S(2)}, u32[]{:S(2)}) collective-permute-start(bf16[512,1024]{1,0:T(8,128)(2,1)} %get-tuple-element.223), channel_id=1, source_target_pairs={{0,16},{16,0},{1,17},{17,1},{2,18},{18,2},{3,19},{19,3},{4,20},{20... | collective-permute-start | bytes 3145736 | tf_op jit(solution)/shard_map/cond/branch_1_fun/ppermute | solution.py:1112
  302.9 4.0 copy-start.5
  302.9 4.0 copy-start.22
  304.1 11.0 %collective-permute-start.11 = (f32[2,16,1280]{2,1,0:T(8,128)S(1)}, f32[2,16,1280]{2,1,0:T(8,128)S(1)}, u32[]{:S(2)}, u32[]{:S(2)}) collective-permute-start(f32[2,16,1280]{2,1,0:T(8,128)S(1)} %pad_maximum_fusion), channel_id=1, source_target_pairs={{0,16},{16,0},{1,17},{17,1},{2,18},{18,2},{3,19},{19,3},{4,20},{20... | collective-permute-start | bytes 491528 | tf_op jit(solution)/shard_map/cond/branch_1_fun/ppermute | solution.py:1112
  305.4 32.3 %collective-permute-start.9 = (bf16[256,1024]{1,0:T(8,128)(2,1)}, bf16[256,1024]{1,0:T(8,128)(2,1)S(1)}, u32[]{:S(2)}, u32[]{:S(2)}) collective-permute-start(bf16[256,1024]{1,0:T(8,128)(2,1)} %constant_dynamic-slice_fusion.7), channel_id=1, source_target_pairs={{0,8},{8,0},{1,9},{9,1},{2,10},{10,2},{3,11},{11,3},{4,12},{12,4},... | collective-permute-start | bytes 1572872 | tf_op jit(solution)/shard_map/cond/branch_1_fun/ppermute | solution.py:1112
  311.0 41.8 %copy-start.2 = (bf16[384,1024]{1,0:T(8,128)(2,1)S(1)}, bf16[384,1024]{1,0:T(8,128)(2,1)}, u32[]{:S(2)}) copy-start(bf16[384,1024]{1,0:T(8,128)(2,1)} %get-tuple-element.207) | copy-start | bytes 2359300 | tf_op jit(solution)/shard_map/cond
  311.9 25.8 %collective-permute-start.10 = (bf16[256,1024]{1,0:T(8,128)(2,1)}, bf16[256,1024]{1,0:T(8,128)(2,1)}, u32[]{:S(2)}, u32[]{:S(2)}) collective-permute-start(bf16[256,1024]{1,0:T(8,128)(2,1)} %dynamic-slice_convert_fusion), channel_id=1, source_target_pairs={{0,8},{8,0},{1,9},{9,1},{2,10},{10,2},{3,11},{11,3},{4,12},{12,4},... | collective-permute-start | bytes 1572872 | tf_op jit(solution)/shard_map/cond/branch_1_fun/ppermute | solution.py:1112
  312.5 25.2 %collective-permute-start.8 = (bf16[384,1024]{1,0:T(8,128)(2,1)}, bf16[384,1024]{1,0:T(8,128)(2,1)}, u32[]{:S(2)}, u32[]{:S(2)}) collective-permute-start(bf16[384,1024]{1,0:T(8,128)(2,1)} %get-tuple-element.198), channel_id=1, source_target_pairs={{0,2},{1,3},{2,0},{3,1},{4,6},{5,7},{6,4},{7,5},{8,10},{9,11},{10,... | collective-permute-start | bytes 2359304 | tf_op jit(solution)/shard_map/cond/branch_1_fun/ppermute | solution.py:1117
  313.5 39.3 %collective-permute-start.7 = (bf16[1216,512]{1,0:T(8,128)(2,1)}, bf16[1216,512]{1,0:T(8,128)(2,1)}, u32[]{:S(2)}, u32[]{:S(2)}) collective-permute-start(bf16[1216,512]{1,0:T(8,128)(2,1)} %get-tuple-element.197), channel_id=1, source_target_pairs={{0,1},{1,0},{2,3},{3,2},{4,5},{5,4},{6,7},{7,6},{8,9},{9,8},{10,11... | collective-permute-start | bytes 3735560 | tf_op jit(solution)/shard_map/cond/branch_1_fun/ppermute | solution.py:1117
  319.0 15.4 %collective-permute-start.12 = (f32[2,16,1280]{2,1,0:T(8,128)}, f32[2,16,1280]{2,1,0:T(8,128)}, u32[]{:S(2)}, u32[]{:S(2)}) collective-permute-start(f32[2,16,1280]{2,1,0:T(8,128)} %fusion.38), channel_id=1, source_target_pairs={{0,8},{8,0},{1,9},{9,1},{2,10},{10,2},{3,11},{11,3},{4,12},{12,4},... | collective-permute-start | bytes 491528 | tf_op jit(solution)/shard_map/cond/branch_1_fun/ppermute | solution.py:1112
  355.0 4.8 copy-start.12
  355.0 4.8 copy-start.13
  355.0 27.5 %collective-permute-start.14 = (bf16[192,1024]{1,0:T(8,128)(2,1)}, bf16[192,1024]{1,0:T(8,128)(2,1)}, u32[]{:S(2)}, u32[]{:S(2)}) collective-permute-start(bf16[192,1024]{1,0:T(8,128)(2,1)} %get-tuple-element.337), channel_id=1, source_target_pairs={{0,1},{1,0},{2,3},{3,2},{4,5},{5,4},{6,7},{7,6},{8,9},{9,8},{10,11... | collective-permute-start | bytes 1179656 | tf_op jit(solution)/shard_map/cond/branch_1_fun/ppermute | solution.py:1117
  358.3 3.3 copy-start.1
  358.3 24.2 %collective-permute-start.13 = (bf16[608,512]{1,0:T(8,128)(2,1)}, bf16[608,512]{1,0:T(8,128)(2,1)}, u32[]{:S(2)}, u32[]{:S(2)}) collective-permute-start(bf16[608,512]{1,0:T(8,128)(2,1)} %get-tuple-element.333), channel_id=1, source_target_pairs={{0,2},{1,3},{2,0},{3,1},{4,6},{5,7},{6,4},{7,5},{8,10},{9,11},{10,... | collective-permute-start | bytes 1867784 | tf_op jit(solution)/shard_map/cond/branch_1_fun/ppermute | solution.py:1117
  363.2 24.8 %collective-permute-start.26 = (bf16[256,1024]{1,0:T(8,128)(2,1)}, bf16[256,1024]{1,0:T(8,128)(2,1)}, u32[]{:S(2)}, u32[]{:S(2)}) collective-permute-start(bf16[256,1024]{1,0:T(8,128)(2,1)} %broadcast_select_fusion), channel_id=1, source_target_pairs={{0,16},{16,0},{1,17},{17,1},{2,18},{18,2},{3,19},{19,3},{4,20},{20... | collective-permute-start | bytes 1572872 | tf_op jit(solution)/shard_map/cond/branch_1_fun/ppermute | solution.py:1112
  364.2 27.6 %collective-permute-start.25 = (bf16[256,1024]{1,0:T(8,128)(2,1)}, bf16[256,1024]{1,0:T(8,128)(2,1)S(1)}, u32[]{:S(2)}, u32[]{:S(2)}) collective-permute-start(bf16[256,1024]{1,0:T(8,128)(2,1)} %broadcast_select_fusion.1), channel_id=1, source_target_pairs={{0,16},{16,0},{1,17},{17,1},{2,18},{18,2},{3,19},{19,3},{4,20},{20... | collective-permute-start | bytes 1572872 | tf_op jit(solution)/shard_map/cond/branch_1_fun/ppermute | solution.py:1112
  364.7 17.9 %collective-permute-start.15 = (f32[2,8,1152]{2,1,0:T(8,128)S(1)}, f32[2,8,1152]{2,1,0:T(8,128)S(1)}, u32[]{:S(2)}, u32[]{:S(2)}) collective-permute-start(f32[2,8,1152]{2,1,0:T(8,128)S(1)} %fusion.31), channel_id=1, source_target_pairs={{0,2},{1,3},{2,0},{3,1},{4,6},{5,7},{6,4},{7,5},{8,10},{9,11},{10,... | collective-permute-start | bytes 221192 | tf_op jit(solution)/shard_map/cond/branch_1_fun/ppermute | solution.py:1117
  383.8 27.5 %collective-permute-start.16 = (bf16[304,512]{1,0:T(8,128)(2,1)S(1)}, bf16[304,512]{1,0:T(8,128)(2,1)S(1)}, u32[]{:S(2)}, u32[]{:S(2)}) collective-permute-start(bf16[304,512]{1,0:T(8,128)(2,1)S(1)} %get-tuple-element.341), channel_id=1, source_target_pairs={{0,4},{1,5},{2,6},{3,7},{4,0},{5,1},{6,2},{7,3},{8,12},{9,13},{10,... | collective-permute-start | bytes 933896 | tf_op jit(solution)/shard_map/cond/branch_1_fun/ppermute | solution.py:1117
  386.3 24.9 %collective-permute-start.17 = (bf16[96,1024]{1,0:T(8,128)(2,1)S(1)}, bf16[96,1024]{1,0:T(8,128)(2,1)S(1)}, u32[]{:S(2)}, u32[]{:S(2)}) collective-permute-start(bf16[96,1024]{1,0:T(8,128)(2,1)S(1)} %get-tuple-element.347), channel_id=1, source_target_pairs={{0,4},{1,5},{2,6},{3,7},{4,0},{5,1},{6,2},{7,3},{8,12},{9,13},{10,... | collective-permute-start | bytes 589832 | tf_op jit(solution)/shard_map/cond/branch_1_fun/ppermute | solution.py:1117
  390.4 20.9 %collective-permute-start.18 = (f32[2,8,1152]{2,1,0:T(8,128)S(1)}, f32[2,8,1152]{2,1,0:T(8,128)S(1)}, u32[]{:S(2)}, u32[]{:S(2)}) collective-permute-start(f32[2,8,1152]{2,1,0:T(8,128)S(1)} %add.213), channel_id=1, source_target_pairs={{0,4},{1,5},{2,6},{3,7},{4,0},{5,1},{6,2},{7,3},{8,12},{9,13},{10,... | collective-permute-start | bytes 221192 | tf_op jit(solution)/shard_map/cond/branch_1_fun/ppermute | solution.py:1117
  411.2 6.9 %collective-permute-start.20 = (f32[2,8,1152]{2,1,0:T(8,128)S(1)}, f32[2,8,1152]{2,1,0:T(8,128)S(1)}, u32[]{:S(2)}, u32[]{:S(2)}) collective-permute-start(f32[2,8,1152]{2,1,0:T(8,128)S(1)} %add.222), channel_id=1, source_target_pairs={{0,1},{1,0},{2,3},{3,2},{4,5},{5,4},{6,7},{7,6},{8,9},{9,8},{10,11... | collective-permute-start | bytes 221192 | tf_op jit(solution)/shard_map/cond/branch_1_fun/ppermute | solution.py:1117
  412.2 5.7 %collective-permute-start.19 = (bf16[304,256]{1,0:T(8,128)(2,1)S(1)}, bf16[304,256]{1,0:T(8,128)(2,1)S(1)}, u32[]{:S(2)}, u32[]{:S(2)}) collective-permute-start(bf16[304,256]{1,0:T(8,128)(2,1)S(1)} %get-tuple-element.350), channel_id=1, source_target_pairs={{0,8},{8,0},{1,9},{9,1},{2,10},{10,2},{3,11},{11,3},{4,12},{12,4},... | collective-permute-start | bytes 466952 | tf_op jit(solution)/shard_map/cond/branch_1_fun/ppermute | solution.py:1112
  413.8 25.0 %collective-permute-start.23 = (bf16[96,1024]{1,0:T(8,128)(2,1)S(1)}, bf16[96,1024]{1,0:T(8,128)(2,1)S(1)}, u32[]{:S(2)}, u32[]{:S(2)}) collective-permute-start(bf16[96,1024]{1,0:T(8,128)(2,1)S(1)} %add_convert_fusion.9), channel_id=1, source_target_pairs={{0,4},{1,5},{2,6},{3,7},{4,0},{5,1},{6,2},{7,3},{8,12},{9,13},{10,... | collective-permute-start | bytes 589832 | tf_op jit(solution)/shard_map/cond/branch_1_fun/ppermute | solution.py:1117
  418.2 20.3 %collective-permute-start.21 = (bf16[304,512]{1,0:T(8,128)(2,1)S(1)}, bf16[304,512]{1,0:T(8,128)(2,1)S(1)}, u32[]{:S(2)}, u32[]{:S(2)}) collective-permute-start(bf16[304,512]{1,0:T(8,128)(2,1)S(1)} %maximum_select_fusion.6), channel_id=1, source_target_pairs={{0,4},{1,5},{2,6},{3,7},{4,0},{5,1},{6,2},{7,3},{8,12},{9,13},{10,... | collective-permute-start | bytes 933896 | tf_op jit(solution)/shard_map/cond/branch_1_fun/ppermute | solution.py:1117
  438.7 16.0 %collective-permute-start.22 = (bf16[608,512]{1,0:T(8,128)(2,1)S(1)}, bf16[608,512]{1,0:T(8,128)(2,1)S(1)}, u32[]{:S(2)}, u32[]{:S(2)}) collective-permute-start(bf16[608,512]{1,0:T(8,128)(2,1)S(1)} %maximum_select_fusion.4), channel_id=1, source_target_pairs={{0,2},{1,3},{2,0},{3,1},{4,6},{5,7},{6,4},{7,5},{8,10},{9,11},{10,... | collective-permute-start | bytes 1867784 | tf_op jit(solution)/shard_map/cond/branch_1_fun/ppermute | solution.py:1117
  438.9 11.1 %collective-permute-start.24 = (bf16[192,1024]{1,0:T(8,128)(2,1)S(1)}, bf16[192,1024]{1,0:T(8,128)(2,1)S(1)}, u32[]{:S(2)}, u32[]{:S(2)}) collective-permute-start(bf16[192,1024]{1,0:T(8,128)(2,1)S(1)} %maximum_select_fusion.5), channel_id=1, source_target_pairs={{0,1},{1,0},{2,3},{3,2},{4,5},{5,4},{6,7},{7,6},{8,9},{9,8},{10,11... | collective-permute-start | bytes 1179656 | tf_op jit(solution)/shard_map/cond/branch_1_fun/ppermute | solution.py:1117
  456.5 5.8 %copy-start.25 = (bf16[256,1024]{1,0:T(8,128)(2,1)S(1)}, bf16[256,1024]{1,0:T(8,128)(2,1)}, u32[]{:S(2)}) copy-start(bf16[256,1024]{1,0:T(8,128)(2,1)} %all-reduce.11.cloned.1.call-done.refs_10_) | copy-start | bytes 1572868
  456.5 19.0 %collective-permute-start.46 = (bf16[384,1024]{1,0:T(8,128)(2,1)}, bf16[384,1024]{1,0:T(8,128)(2,1)}, u32[]{:S(2)}, u32[]{:S(2)}) collective-permute-start(bf16[384,1024]{1,0:T(8,128)(2,1)} %get-tuple-element.302), channel_id=1, source_target_pairs={{0,2},{1,3},{2,0},{3,1},{4,6},{5,7},{6,4},{7,5},{8,10},{9,11},{10,... | collective-permute-start | bytes 2359304 | tf_op jit(solution)/shard_map/ppermute | solution.py:1117
  456.8 28.8 %collective-permute-start.44 = (bf16[1216,512]{1,0:T(8,128)(2,1)}, bf16[1216,512]{1,0:T(8,128)(2,1)}, u32[]{:S(2)}, u32[]{:S(2)}) collective-permute-start(bf16[1216,512]{1,0:T(8,128)(2,1)} %get-tuple-element.301.refs_3_), channel_id=1, source_target_pairs={{0,1},{1,0},{2,3},{3,2},{4,5},{5,4},{6,7},{7,6},{8,9},{9,8},{10,11... | collective-permute-start | bytes 3735560 | tf_op jit(solution)/shard_map/ppermute | solution.py:1117
  458.9 28.4 %collective-permute-start.49 = (bf16[2432,256]{1,0:T(8,128)(2,1)S(1)}, bf16[2432,256]{1,0:T(8,128)(2,1)}, u32[]{:S(2)}, u32[]{:S(2)}) collective-permute-start(bf16[2432,256]{1,0:T(8,128)(2,1)S(1)} %constant_dynamic-slice_fusion.14), channel_id=1, source_target_pairs={{0,8},{8,0},{1,9},{9,1},{2,10},{10,2},{3,11},{11,3},{4,12},{12,4},... | collective-permute-start | bytes 3735560 | tf_op jit(solution)/shard_map/ppermute | solution.py:1112
  459.5 34.4 %collective-permute-start.48 = (bf16[2432,512]{1,0:T(8,128)(2,1)}, bf16[2432,512]{1,0:T(8,128)(2,1)}, u32[]{:S(2)}, u32[]{:S(2)}) collective-permute-start(bf16[2432,512]{1,0:T(8,128)(2,1)} %all-reduce.13.cloned.1.call-done.refs_6_), channel_id=1, source_target_pairs={{0,16},{1,17},{2,18},{3,19},{4,20},{5,21},{6,22},{7,23},{8,24},{9,... | collective-permute-start | bytes 7471112 | tf_op jit(solution)/shard_map/ppermute | solution.py:1350
  462.3 17.2 %collective-permute-start.51 = (bf16[256,1024]{1,0:T(8,128)(2,1)S(1)}, bf16[256,1024]{1,0:T(8,128)(2,1)}, u32[]{:S(2)}, u32[]{:S(2)}) collective-permute-start(bf16[256,1024]{1,0:T(8,128)(2,1)S(1)} %copy-done.25), channel_id=1, source_target_pairs={{0,16},{1,17},{2,18},{3,19},{4,20},{5,21},{6,22},{7,23},{8,24},{9,... | collective-permute-start | bytes 1572872 | tf_op jit(solution)/shard_map/ppermute | solution.py:1350
  479.5 14.4 %collective-permute-start.47 = (bf16[768,1024]{1,0:T(8,128)(2,1)S(1)}, bf16[768,1024]{1,0:T(8,128)(2,1)}, u32[]{:S(2)}, u32[]{:S(2)}) collective-permute-start(bf16[768,1024]{1,0:T(8,128)(2,1)S(1)} %maximum_select_fusion.8.refs_5_), channel_id=1, source_target_pairs={{0,16},{16,0},{1,17},{17,1},{2,18},{18,2},{3,19},{19,3},{4,20},{20... | collective-permute-start | bytes 4718600 | tf_op jit(solution)/shard_map/ppermute | solution.py:1112
  479.5 14.4 %collective-permute-start.43 = (bf16[1216,512]{1,0:T(8,128)(2,1)}, bf16[1216,512]{1,0:T(8,128)(2,1)}, u32[]{:S(2)}, u32[]{:S(2)}) collective-permute-start(bf16[1216,512]{1,0:T(8,128)(2,1)} %get-tuple-element.301.refs_3_), channel_id=1, source_target_pairs={{16,0},{17,1},{18,2},{19,3},{20,4},{21,5},{22,6},{23,7},{24,8},{25... | collective-permute-start | bytes 3735560 | tf_op jit(solution)/shard_map/ppermute | solution.py:1350
  485.6 8.3 %collective-permute-start.45 = (bf16[1216,512]{1,0:T(8,128)(2,1)}, bf16[1216,512]{1,0:T(8,128)(2,1)}, u32[]{:S(2)}, u32[]{:S(2)}) collective-permute-start(bf16[1216,512]{1,0:T(8,128)(2,1)} %collective-permute-done.44.refs_4_), channel_id=1, source_target_pairs={{16,0},{17,1},{18,2},{19,3},{20,4},{21,5},{22,6},{23,7},{24,8},{25... | collective-permute-start | bytes 3735560 | tf_op jit(solution)/shard_map/ppermute | solution.py:1350
  487.3 6.6 %collective-permute-start.50 = (bf16[2432,256]{1,0:T(8,128)(2,1)}, bf16[2432,256]{1,0:T(8,128)(2,1)}, u32[]{:S(2)}, u32[]{:S(2)}) collective-permute-start(bf16[2432,256]{1,0:T(8,128)(2,1)} %collective-permute-done.49.refs_8_), channel_id=1, source_target_pairs={{0,16},{1,17},{2,18},{3,19},{4,20},{5,21},{6,22},{7,23},{8,24},{9,... | collective-permute-start | bytes 3735560 | tf_op jit(solution)/shard_map/ppermute | solution.py:1350
  (17 other events, 22.6 us)
Sparse Core Ops, SparseCore 0:
  172.3 73.0 all-reduce.10
  250.0 122.9 all-reduce.12
